TPU v7x, 256 devices: a whole 4x4x8 slice. The times are simulated.
256 devices in a mesh: band: 16 (over x_hi, z), slab: 16 (over x_lo, y, core).
Axes of the slice: x: 4 (x_hi: 2, x_lo: 2; x = x_hi * 2 + x_lo), y: 4, z: 8, core: 2. Of those that a mesh axis runs over, the one named last changes fastest.
Arguments:
- orbitals: float32 [256, 128, 4096], P('band', 'slab'), may hold values from -0.6 to 0.6
- occupations: float32 [256], P('band'), may hold values from 0.1 to 2
- projectors: float32 [128, 13, 512], P('slab'), may hold values from -0.25 to 0.25
- shapes: float32 [128, 9, 512], P('slab'), may hold values from -6 to 6
- coupling: float32 [9, 13, 13], replicated, may hold values from -0.3 to 0.3
- sphere_offsets: int32 [128, 512], P('slab'), may hold values from 0 to 73727, as said below
- sphere_sizes: int32 [128], P('slab'), may hold values from 64 to 512
Outputs:
- density: float32 [128, 4096], P('slab', 'band')
- density_matrices: float32 [128, 13, 13], P('slab')
Inputs may be any that keep to these rules, and one draw needn't show every extreme that they name: `sphere_offsets`: the plane part o // 4096 of an offset lies within 5 planes of the atom's centre plane, which lies in the slab's own planes 5 to 12; in-plane parts are arbitrary.
All inputs are finite; a program needn't handle non-finite values.
Results may differ from a plain program's by a relative error of at most 0.000062.
Values sent between devices are 32-bit elements; how exact they have to be, the bound alone decides.
No kernel may reach another device: no remote copies, remote signals or barrier semaphores. Data moves between devices by JAX's collectives and lax.ppermute only.
A program may use at most 128 MiB of HBM per device.

v0:
```python
import jax
import jax.numpy as jnp
from jax import lax
from jax.sharding import PartitionSpec as P

HALO = 5


def extended_2(cells, sides, width):
    for axis, dim in sides:
        count = lax.axis_size(axis)
        head = lax.slice_in_dim(cells, 0, width, axis=dim)
        tail = lax.slice_in_dim(cells, cells.shape[dim] - width, cells.shape[dim], axis=dim)
        cells = jnp.concatenate(
            [
                lax.ppermute(tail, axis, [(i, (i + 1) % count) for i in range(count)]),
                cells,
                lax.ppermute(head, axis, [((i + 1) % count, i) for i in range(count)]),
            ],
            axis=dim,
        )
    return cells


def from_behind(block, axis, distance):
    devices = range(lax.axis_size(axis))
    route = [((i - distance) % len(devices), i) for i in devices]
    return lax.ppermute(block, axis, route)


def add_rims(extended, planes, from_below, from_above):
    core = extended[HALO : HALO + planes]
    core = core.at[:HALO].add(from_below)
    core = core.at[planes - HALO :].add(from_above)
    return core


def local(orbitals, occupations, projectors, shapes, coupling, sphere_offsets, sphere_sizes):
    highest = lax.Precision.HIGHEST
    bands, planes, plane_pts = orbitals.shape
    groups = lax.axis_size("band")
    width = plane_pts // groups
    column_start = lax.axis_index("band") * width
    sphere_len = sphere_offsets.shape[1]
    live = (jnp.arange(sphere_len, dtype=jnp.int32)[None, :] < sphere_sizes[:, None]).astype(
        jnp.float32
    )
    masked = projectors * live[:, None, :]
    padded = extended_2(orbitals, (("slab", 1),), HALO)
    flat = padded.reshape(bands, -1)
    on_sphere = flat[:, sphere_offsets]
    proj = jnp.einsum("bag,aig->bai", on_sphere, masked, precision=highest)
    weighted = proj * occupations[:, None, None]
    partial_matrix = jnp.einsum("bai,baj->aij", weighted, proj, precision=highest)
    density_matrices = lax.psum(partial_matrix, "band")
    pseudo_local = jnp.einsum("b,bzp->zp", occupations, orbitals * orbitals, precision=highest)
    summed = lax.psum(pseudo_local, "band")
    pseudo_part = lax.dynamic_slice_in_dim(summed, column_start, width, 1)
    charges = jnp.einsum("lij,aij->al", coupling, density_matrices, precision=highest)
    comp = jnp.einsum("al,alg->ag", charges, shapes, precision=highest) * live
    extent = planes + 2 * HALO
    comp_flat = (
        jnp.zeros((extent * plane_pts,), jnp.float32)
        .at[sphere_offsets.reshape(-1)]
        .add(comp.reshape(-1))
    )
    comp_ext = comp_flat.reshape(extent, plane_pts)
    from_below = from_behind(comp_ext[HALO + planes :], "slab", 1)
    from_above = from_behind(comp_ext[:HALO], "slab", -1)
    core = add_rims(comp_ext, planes, from_below, from_above)
    comp_part = lax.dynamic_slice_in_dim(core, column_start, width, 1)
    density = pseudo_part + comp_part
    return (density, density_matrices)


def solution(mesh):
    placed = (
        P("band", "slab", None),
        P("band"),
        P("slab", None, None),
        P("slab", None, None),
        P(),
        P("slab", None),
        P("slab"),
    )
    return jax.shard_map(
        local,
        mesh=mesh,
        in_specs=placed,
        out_specs=(P("slab", "band"), P("slab", None, None)),
        check_vma=False,
    )
```

profile of v0, /device:TPU:32, one launch (start us, length us, event | category | flops | bytes accessed | tf_op | source)
XLA Modules:
  0.0 347.2 jit_solution(8475129955008542908)
XLA Ops:
  7.2 0.0 copy-start
  7.2 0.0 all-reduce.2.cloned.1.call-start
  7.2 2.6 fusion.17
  9.8 0.8 copy.30
  10.6 0.0 copy-start.1
  10.6 0.1 collective-permute-start
  10.7 0.8 copy.31
  11.4 0.0 copy-start.5
  11.4 0.0 copy-start.7
  11.5 0.0 copy-start.2
  11.5 3.9 %collective-permute-start.1 = (f32[16,5,4096]{2,0,1:T(8,128)S(1)}, f32[16,5,4096]{2,0,1:T(8,128)S(1)}, u32[]{:S(2)}, u32[]{:S(2)}) collective-permute-start(f32[16,5,4096]{2,0,1:T(8,128)S(1)} %copy.31), channel_id=1, source_target_pairs={{1,0},{2,1},{3,2},{4,3},{5,4},{6,5},{7,6},{8,7},{9,8},{10,9},{11,1... | collective-permute-start | bytes 3932168 | tf_op jit(solution)/shard_map/ppermute | solution.py:18
  15.4 0.0 copy-done.1
  15.4 0.2 mul.25
  15.6 0.0 copy-done.5
  15.7 0.0 copy-done.7
  15.7 0.1 fusion.15
  15.8 0.0 copy-done.2
  15.8 14.0 %collective-permute-done = f32[16,5,4096]{2,0,1:T(8,128)S(1)} collective-permute-done((f32[16,5,4096]{2,0,1:T(8,128)S(1)}, f32[16,5,4096]{2,0,1:T(8,128)S(1)}, u32[]{:S(2)}, u32[]{:S(2)}) %collective-permute-start) | collective-permute-done | bytes 1310752 | tf_op jit(solution)/shard_map/ppermute | solution.py:16
  29.8 0.8 copy.16
  30.6 0.0 collective-permute-done.1
  30.6 0.8 copy.17
  31.4 3.7 %pad_maximum_fusion = f32[16,18,4096]{2,1,0:T(8,128)} fusion(f32[16,5,4096]{2,1,0:T(8,128)S(1)} %copy.17, f32[16,8,4096]{2,1,0:T(8,128)S(1)} %copy-done.1, f32[16,5,4096]{2,1,0:T(8,128)S(1)} %copy.16), kind=kLoop, calls=%fused_computation.2 | loop fusion | flops 2359296 | bytes 9437184 | tf_op jit(solution)/shard_map/concatenate | solution.py:14
  35.1 19.7 %copy.18 = f32[16,18,4096]{0,2,1:T(8,128)} copy(f32[16,18,4096]{2,1,0:T(8,128)} %pad_maximum_fusion) | data formatting | bytes 9437184 | tf_op jit(solution)/shard_map/concatenate | solution.py:14
  54.8 0.0 copy-start.6
  54.8 25.9 %gather_fusion = f32[4096,16]{1,0:T(8,128)} fusion(f32[16,73728]{0,1:T(8,128)} %bitcast.33, s32[4096]{0:T(1024)S(1)} %broadcast_clamp_fusion), kind=kCustom, calls=%fused_computation | custom fusion | bytes 540672 | tf_op jit(solution)/shard_map/gather | solution.py:51
  80.8 0.0 copy-start.4
  80.8 2.2 copy.19
  82.9 0.6 convolution_bitcast_fusion
  83.5 0.0 copy-done.6
  83.5 0.2 fusion.10
  83.8 74.4 %psum.15 = f32[8,13,13]{2,1,0:T(8,128)S(1)} all-reduce(f32[8,13,13]{2,1,0:T(8,128)S(1)} %fusion.10), channel_id=1, replica_groups=mesh['band'=16,'slab'=16] {'band'}, use_global_device_ids=true, to_apply=%region_1.0 | all-reduce | flops 1352 | bytes 10816 | tf_op jit(solution)/shard_map/psum | solution.py:55
  158.1 0.0 copy-done.4
  158.2 0.0 copy-start.3
  158.2 0.2 fusion.8
  158.4 0.0 copy-done
  158.4 0.4 fusion.3
  158.8 0.1 fusion.14
  158.9 22.0 %scatter_custom_fusion = f32[73728]{0:T(1024)S(1)} fusion(s32[4096]{0:T(1024)S(1)} %bitcast.40, f32[4096]{0:T(1024)S(1)} %bitcast.41, f32[]{:T(128)} %constant.71.clone.1), kind=kCustom, calls=%fused_computation.10 | custom fusion | flops 4096 | bytes 294916 | tf_op jit(solution)/shard_map/scatter-add | solution.py:65
  180.9 0.1 collective-permute-start.2
  181.0 4.1 %collective-permute-start.3 = (f32[5,4096]{1,0:T(8,128)S(1)}, f32[5,4096]{1,0:T(8,128)S(1)}, u32[]{:S(2)}, u32[]{:S(2)}) collective-permute-start(f32[5,4096]{1,0:T(8,128)S(1)} %slice.101), channel_id=1, source_target_pairs={{1,0},{2,1},{3,2},{4,3},{5,4},{6,5},{7,6},{8,7},{9,8},{10,9},{11,1... | collective-permute-start | bytes 245768 | tf_op jit(solution)/shard_map/ppermute | solution.py:28
  185.1 2.4 fusion
  187.5 0.7 copy.45
  188.2 0.0 copy-done.3
  188.2 0.0 all-reduce.2.cloned.1.call-update
  188.4 0.0 collective-permute-done.2
  188.4 0.5 scatter-add.18
  188.9 0.0 collective-permute-done.3
  188.9 0.5 scatter-add.19
  189.4 149.7 %all-reduce.2.cloned.1.call-done = f32[8,4096]{1,0:T(8,128)} async-done(((f32[8,4096]{1,0:T(8,128)}), f32[8,4096]{1,0:T(8,128)}) %all-reduce.2.cloned.1.call-update) | async-done | bytes 131088 | tf_op jit(solution)/shard_map/psum | solution.py:57
  339.1 1.3 dynamic-slice_add_fusion
  (16 shorter events, 0.2 us)
Async XLA Ops:
  7.2 151.2 %copy-start = (f32[8,9,512]{2,0,1:T(8,128)S(1)}, f32[8,9,512]{2,0,1:T(8,128)}, u32[]{:S(2)}) copy-start(f32[8,9,512]{2,0,1:T(8,128)} %param.14) | copy-start | bytes 442372
  7.2 331.9 %all-reduce.2.cloned.1.call-start = ((), (), s32[]{:S(2)}) async-start(), calls=%async_computation | async-start | bytes 262144 | tf_op jit(solution)/shard_map/psum | solution.py:57
  10.6 4.8 %copy-start.1 = (f32[16,8,4096]{2,1,0:T(8,128)S(1)}, f32[16,8,4096]{2,1,0:T(8,128)}, u32[]{:S(2)}) copy-start(f32[16,8,4096]{2,1,0:T(8,128)} %param.11) | copy-start | bytes 6291460
  10.6 19.2 %collective-permute-start = (f32[16,5,4096]{2,0,1:T(8,128)S(1)}, f32[16,5,4096]{2,0,1:T(8,128)S(1)}, u32[]{:S(2)}, u32[]{:S(2)}) collective-permute-start(f32[16,5,4096]{2,0,1:T(8,128)S(1)} %copy.30), channel_id=1, source_target_pairs={{0,1},{1,2},{2,3},{3,4},{4,5},{5,6},{6,7},{7,8},{8,9},{9,10},{10,1... | collective-permute-start | bytes 3932168 | tf_op jit(solution)/shard_map/ppermute | solution.py:16
  11.4 4.2 %copy-start.5 = (s32[8,512]{1,0:T(8,128)S(1)}, s32[8,512]{1,0:T(8,128)}, u32[]{:S(2)}) copy-start(s32[8,512]{1,0:T(8,128)} %param.16) | copy-start | bytes 49156
  11.4 4.2 %copy-start.7 = (s32[8]{0:T(128)S(1)}, s32[8]{0:T(128)}, u32[]{:S(2)}) copy-start(s32[8]{0:T(128)} %param.17) | copy-start | bytes 100
  11.5 4.3 %copy-start.2 = (f32[8,13,512]{2,0,1:T(8,128)S(1)}, f32[8,13,512]{2,0,1:T(8,128)}, u32[]{:S(2)}) copy-start(f32[8,13,512]{2,0,1:T(8,128)} %param.13) | copy-start | bytes 638980
  11.5 19.1 %collective-permute-start.1 = (f32[16,5,4096]{2,0,1:T(8,128)S(1)}, f32[16,5,4096]{2,0,1:T(8,128)S(1)}, u32[]{:S(2)}, u32[]{:S(2)}) collective-permute-start(f32[16,5,4096]{2,0,1:T(8,128)S(1)} %copy.31), channel_id=1, source_target_pairs={{1,0},{2,1},{3,2},{4,3},{5,4},{6,5},{7,6},{8,7},{9,8},{10,9},{11,1... | collective-permute-start | bytes 3932168 | tf_op jit(solution)/shard_map/ppermute | solution.py:18
  54.8 28.7 %copy-start.6 = (f32[16]{0:T(128)S(1)}, f32[16]{0:T(128)}, u32[]{:S(2)}) copy-start(f32[16]{0:T(128)} %param.12) | copy-start | bytes 196
  80.8 77.4 %copy-start.4 = (f32[9,13,13]{2,1,0:T(8,128)S(1)}, f32[9,13,13]{2,1,0:T(8,128)}, u32[]{:S(2)}) copy-start(f32[9,13,13]{2,1,0:T(8,128)} %param.15) | copy-start | bytes 18256
  158.2 30.1 %copy-start.3 = (f32[8,13,13]{2,0,1:T(8,128)}, f32[8,13,13]{2,0,1:T(8,128)S(1)}, u32[]{:S(2)}) copy-start(f32[8,13,13]{2,0,1:T(8,128)S(1)} %copy.22) | copy-start | bytes 16228
  180.9 7.5 %collective-permute-start.2 = (f32[5,4096]{1,0:T(8,128)S(1)}, f32[5,4096]{1,0:T(8,128)S(1)}, u32[]{:S(2)}, u32[]{:S(2)}) collective-permute-start(f32[5,4096]{1,0:T(8,128)S(1)} %slice.98), channel_id=1, source_target_pairs={{15,0},{0,1},{1,2},{2,3},{3,4},{4,5},{5,6},{6,7},{7,8},{8,9},{9,10... | collective-permute-start | bytes 245768 | tf_op jit(solution)/shard_map/ppermute | solution.py:28
  181.0 7.9 %collective-permute-start.3 = (f32[5,4096]{1,0:T(8,128)S(1)}, f32[5,4096]{1,0:T(8,128)S(1)}, u32[]{:S(2)}, u32[]{:S(2)}) collective-permute-start(f32[5,4096]{1,0:T(8,128)S(1)} %slice.101), channel_id=1, source_target_pairs={{1,0},{2,1},{3,2},{4,3},{5,4},{6,5},{7,6},{8,7},{9,8},{10,9},{11,1... | collective-permute-start | bytes 245768 | tf_op jit(solution)/shard_map/ppermute | solution.py:28
Sparse Core Ops, SparseCore 0:
  188.4 150.6 all-reduce.1
where the time goes:
time: 349 us; the launch traced here: 347 us
  waiting for transfers between devices  164 us (47%)
  blocking collectives  74.4 us (21%)
  local copies, waits for them, and re-layouts  55.5 us (16%)
  other arithmetic  27.4 us (8%)
  between operations  14.4 us (4%)
  starting transfers between devices  8.21 us (2%)
  matrix products  3.8 us (1%)
    psum x1, waiting for transfers between devices, local(): summed = lax.psum(pseudo_local, 'band')  150 us
    psum x1, blocking collectives, local(): density_matrices = lax.psum(partial_matrix, 'band')  74.4 us
    gather x2, local copies, waits for them, and re-layouts, local(): on_sphere = flat[:, sphere_offsets]  28.1 us
    scatter-add x1, other arithmetic, local(): comp_flat = jnp.zeros((extent * plane_pts,), jnp.float32).at[sphere_offse...  22 us
    concatenate x1, local copies, waits for them, and re-layouts, extended_2(): jnp.concatenate([lax.ppermute(tail, axis, [(i, (i + 1) % count) for i in...  19.7 us
    ppermute x1, waiting for transfers between devices, extended_2(): lax.ppermute(tail, axis, [(i, (i + 1) % count) for i in range(count)])  14 us
  transfers between devices with their start and end apart: 5, of which 2 were waited for; matrix products, arithmetic and copies ran while one was open for 2% of the time, Pallas kernels for 0%

commit v1 on v0

v1 whole, which is shorter than its diff:
```python
import functools

import jax
import jax.numpy as jnp
from jax import lax
from jax.experimental import pallas as pl
from jax.experimental.pallas import tpu as pltpu
from jax.sharding import PartitionSpec as P

HALO = 5
PLANE = 4096
CZ = 8
ATOM_DEV = 8
SPHERE = 512
NI = 13
NL = 9
BANDS = 16
LANES = 128
STEP = 16
HIGHEST = lax.Precision.HIGHEST
F32 = jnp.float32
BF16 = jnp.bfloat16

VM = pl.BlockSpec(memory_space=pltpu.VMEM)
SM = pl.BlockSpec(memory_space=pltpu.SMEM)


def params():
    return pltpu.CompilerParams(vmem_limit_bytes=48 * 2**20)


def gather_rows(offsets, sizes, table, rows):
    for a in range(ATOM_DEV):
        steps = (sizes[a] + (STEP - 1)) // STEP

        def body(step, carry, a=a):
            first = pl.multiple_of(a * SPHERE + step * STEP, STEP)
            for u in range(STEP):
                point = offsets[first + u] & (PLANE - 1)
                rows[pl.ds(first + u, 1), :] = table[pl.ds(point, 1), :]
            return carry

        lax.fori_loop(0, steps, body, 0)


def project(pay, rows, shift):
    lane_plane = lax.broadcasted_iota(jnp.int32, (16, LANES), 1) % CZ
    sub = lax.broadcasted_iota(jnp.int32, (16, SPHERE), 0)
    parts = []
    for a in range(ATOM_DEV):
        block = pay[a]
        plane = (block[13:14, :].astype(jnp.int32) >> 12) + shift
        proj = jnp.where(sub < NI, block, 0.0)
        high = proj.astype(BF16).astype(F32)
        low = proj - high
        pieces = []
        for piece in (high, low):
            for z in range(CZ):
                pieces.append(jnp.where(plane == z, piece, 0.0))
        left = jnp.concatenate(pieces, axis=0).astype(BF16)
        gathered = rows[a * SPHERE : (a + 1) * SPHERE, :]
        g_high = gathered.astype(BF16)
        g_low = (gathered - g_high.astype(F32)).astype(BF16)
        first = jnp.dot(left, g_high, preferred_element_type=F32)
        second = jnp.dot(left[:LANES], g_low, preferred_element_type=F32)
        total = first[:LANES] + first[LANES:] + second
        acc = jnp.zeros((16, LANES), F32)
        for z in range(CZ):
            acc = acc + jnp.where(lane_plane == z, total[z * 16 : (z + 1) * 16, :], 0.0)
        parts.append(acc)
    summed = jnp.concatenate(parts, axis=0)
    band = lax.broadcasted_iota(jnp.int32, (BANDS, LANES), 0)
    lane_band = lax.broadcasted_iota(jnp.int32, (BANDS, LANES), 1) // CZ
    pick = (band == lane_band).astype(F32)
    return lax.dot_general(
        pick, summed, (((1,), (1,)), ((), ())), precision=HIGHEST, preferred_element_type=F32
    )


def own_kernel(offsets, sizes, occ, x, pay, pseudo, table, q, rows):
    for c in range(PLANE // LANES):
        cols = slice(c * LANES, (c + 1) * LANES)
        acc = jnp.zeros((CZ, LANES), F32)
        for n in range(BANDS):
            v = x[n * CZ : (n + 1) * CZ, cols]
            acc = acc + occ[n] * (v * v)
        pseudo[c // 2, (c % 2) * CZ : (c % 2 + 1) * CZ, :] = acc
        table[cols, :] = x[:, cols].T
    rows[...] = jnp.zeros_like(rows)
    gather_rows(offsets, sizes, table, rows)
    q[...] = project(pay, rows, -HALO)


def side_kernel(off_lo, size_lo, off_hi, size_hi, table, pay_lo, pay_hi, q_lo, q_hi, rows):
    rows[...] = jnp.zeros_like(rows)
    gather_rows(off_lo, size_lo, table, rows)
    q_lo[...] = project(pay_lo, rows, -HALO - CZ)
    gather_rows(off_hi, size_hi, table, rows)
    q_hi[...] = project(pay_hi, rows, CZ - HALO)


def matrix_kernel(q0, q1, q2, occ, pseudo, out):
    proj = q0[...] + q1[...] + q2[...]
    weighted = proj * occ[...]
    full = lax.dot_general(
        weighted, proj, (((0,), (0,)), ((), ())), precision=HIGHEST, preferred_element_type=F32
    )
    lane_atom = lax.broadcasted_iota(jnp.int32, (16, LANES), 1) // 16
    acc = jnp.zeros((16, LANES), F32)
    for a in range(ATOM_DEV):
        acc = acc + jnp.where(lane_atom == a, full[a * 16 : (a + 1) * 16, :], 0.0)
    for b in range(16):
        out[b, 0:16, :] = pseudo[b]
        out[b, 16:32, :] = acc


def charge_kernel(start, recv, coupling, shapes, offsets, core, down, up, matrices):
    total = recv[0]
    for b in range(1, 16):
        total = total + recv[b]
    matrix = total[16:32]
    matrices[...] = matrix
    per_lane = jnp.concatenate(
        [jnp.sum(coupling[l] * matrix, axis=0, keepdims=True) for l in range(NL)], axis=0
    )
    atom = lax.broadcasted_iota(jnp.int32, (ATOM_DEV, LANES), 0)
    lane_atom = lax.broadcasted_iota(jnp.int32, (ATOM_DEV, LANES), 1) // 16
    pick = (atom == lane_atom).astype(F32)
    charges = lax.dot_general(
        pick, per_lane, (((1,), (1,)), ((), ())), precision=HIGHEST, preferred_element_type=F32
    )
    comp = jnp.zeros((ATOM_DEV, SPHERE), F32)
    for l in range(NL):
        comp = comp + charges[:, l : l + 1] * shapes[l]
    c1 = comp.astype(BF16).astype(F32)
    c2 = (comp - c1).astype(BF16).astype(F32)
    c3 = comp - c1 - c2
    plane = offsets[...] >> 12
    column = (offsets[...] & (PLANE - 1)) - start[0]
    row = lax.broadcasted_iota(jnp.int32, (24, SPHERE), 0)
    target = jnp.where(row < 8, row + HALO, jnp.where(row < 16, row - 11, row - 3))
    col = lax.broadcasted_iota(jnp.int32, (256, SPHERE), 0)
    acc = jnp.zeros((80, 256), F32)
    for a in range(ATOM_DEV):
        here = target == plane[a : a + 1, :]
        left = jnp.concatenate(
            [jnp.where(here, c[a : a + 1, :], 0.0) for c in (c1, c2, c3)]
            + [jnp.zeros((8, SPHERE), F32)],
            axis=0,
        ).astype(BF16)
        right = jnp.where(col == column[a : a + 1, :], 1.0, 0.0).astype(BF16)
        acc = acc + lax.dot_general(
            left, right, (((1,), (1,)), ((), ())), preferred_element_type=F32
        )
    placed = acc[0:24] + acc[24:48] + acc[48:72]
    core[...] = placed[0:8] + jnp.concatenate([total[0:8], total[8:16]], axis=1)
    down[...] = placed[8:16]
    up[...] = placed[16:24]


def shape(*dims):
    return jax.ShapeDtypeStruct(dims, F32)


def local(orbitals, occupations, projectors, shapes, coupling, sphere_offsets, sphere_sizes):
    slabs = lax.axis_size("slab")
    to_next = [(i, (i + 1) % slabs) for i in range(slabs)]
    to_prev = [((i + 1) % slabs, i) for i in range(slabs)]
    live = jnp.arange(SPHERE, dtype=jnp.int32)[None, :] < sphere_sizes[:, None]
    masked = jnp.where(live[:, None, :], projectors, 0.0)
    pay = jnp.concatenate(
        [
            masked,
            sphere_offsets.astype(F32)[:, None, :],
            jnp.broadcast_to(sphere_sizes.astype(F32)[:, None, None], (ATOM_DEV, 1, SPHERE)),
            jnp.zeros((ATOM_DEV, 1, SPHERE), F32),
        ],
        axis=1,
    )
    pay_lo = lax.ppermute(pay, "slab", to_next)
    pay_hi = lax.ppermute(pay, "slab", to_prev)

    pseudo, table, q_own = pl.pallas_call(
        own_kernel,
        out_shape=(shape(16, 16, LANES), shape(PLANE, LANES), shape(BANDS, LANES)),
        in_specs=[SM, SM, SM, VM, VM],
        out_specs=(VM, VM, VM),
        scratch_shapes=[pltpu.VMEM((ATOM_DEV * SPHERE, LANES), F32)],
        compiler_params=params(),
        cost_estimate=pl.CostEstimate(flops=2 * 10**9, bytes_accessed=8 * 2**20, transcendentals=0),
        name="own_points",
    )(
        sphere_offsets.reshape(-1),
        sphere_sizes,
        occupations,
        orbitals.reshape(BANDS * CZ, PLANE),
        pay,
    )

    def lists(block):
        return block[:, 13, :].astype(jnp.int32).reshape(-1), block[:, 14, 0].astype(jnp.int32)

    off_lo, size_lo = lists(pay_lo)
    off_hi, size_hi = lists(pay_hi)
    q_lo, q_hi = pl.pallas_call(
        side_kernel,
        out_shape=(shape(BANDS, LANES), shape(BANDS, LANES)),
        in_specs=[SM, SM, SM, SM, VM, VM, VM],
        out_specs=(VM, VM),
        scratch_shapes=[pltpu.VMEM((ATOM_DEV * SPHERE, LANES), F32)],
        compiler_params=params(),
        name="side_points",
    )(off_lo, size_lo, off_hi, size_hi, table, pay_lo, pay_hi)
    back_hi = lax.ppermute(q_lo, "slab", to_prev)
    back_lo = lax.ppermute(q_hi, "slab", to_next)

    packed = pl.pallas_call(
        matrix_kernel,
        out_shape=shape(16, 32, LANES),
        in_specs=[VM] * 5,
        out_specs=VM,
        compiler_params=params(),
        name="partial_matrices",
    )(q_own, back_hi, back_lo, jnp.broadcast_to(occupations[:, None], (BANDS, LANES)), pseudo)
    recv = lax.all_to_all(packed, "band", 0, 0)

    coupling_lanes = jnp.tile(jnp.pad(coupling, ((0, 0), (0, 3), (0, 3))), (1, 1, ATOM_DEV))
    shapes_live = jnp.where(live[:, None, :], shapes, 0.0).transpose(1, 0, 2)
    width = PLANE // lax.axis_size("band")
    start = (lax.axis_index("band") * width).astype(jnp.int32).reshape(1)
    core, down, up, matrices = pl.pallas_call(
        charge_kernel,
        out_shape=(shape(CZ, 256), shape(CZ, 256), shape(CZ, 256), shape(16, LANES)),
        in_specs=[SM, VM, VM, VM, VM],
        out_specs=(VM, VM, VM, VM),
        compiler_params=params(),
        name="charges",
    )(start, recv, coupling_lanes, shapes_live, sphere_offsets)
    from_above = lax.ppermute(down, "slab", to_prev)
    from_below = lax.ppermute(up, "slab", to_next)
    density = core + from_above + from_below
    density_matrices = matrices.reshape(16, ATOM_DEV, 16)[:NI, :, :NI].transpose(1, 0, 2)
    return (density, density_matrices)


def solution(mesh):
    placed = (
        P("band", "slab", None),
        P("band"),
        P("slab", None, None),
        P("slab", None, None),
        P(),
        P("slab", None),
        P("slab"),
    )
    return jax.shard_map(
        local,
        mesh=mesh,
        in_specs=placed,
        out_specs=(P("slab", "band"), P("slab", None, None)),
        check_vma=False,
    )
```

time: 349 us -> 68 us (0.19)
  waiting for transfers between devices: 164 us -> 19.6 us
  blocking collectives: 74.4 us -> 0 us
  local copies, waits for them, and re-layouts: 55.5 us -> 4.82 us
  other arithmetic: 27.4 us -> 4.45 us
  Pallas kernels: 0 us -> 19.1 us
  between operations: 14.4 us -> 0.77 us
  starting transfers between devices: 8.21 us -> 19.2 us
  matrix products: 3.8 us -> 0 us
    psum x1 -> x0, waiting for transfers between devices: 150 us -> none  [local(): summed = lax.psum(pseudo_local, 'band')]
    psum x1 -> x0, blocking collectives: 74.4 us -> none  [local(): density_matrices = lax.psum(partial_matrix, 'band')]
    gather x2 -> x0, local copies, waits for them, and re-layouts: 28.1 us -> none  [local(): on_sphere = flat[:, sphere_offsets]]
    scatter-add x1 -> x0, other arithmetic: 22 us -> none  [local(): comp_flat = jnp.zeros((extent * plane_pts,), jnp.float32).at[sphere_offse...]
    concatenate x1, local copies, waits for them, and re-layouts: 19.7 us -> 0.07 us  [local(): jnp.concatenate([masked, sphere_offsets.astype(F32)[:, None, :], jnp.broa...]
    pallas_call x0 -> x4, Pallas kernels: none -> 19.1 us  [the longest x1 10.3 us: local(): pl.pallas_call(side_kernel, out_shape=(shape(BANDS, LANES), shape(BANDS,...]
    all_to_all x0 -> x1, starting transfers between devices: none -> 10.8 us  [local(): recv = lax.all_to_all(packed, 'band', 0, 0)]
    all_to_all x0 -> x1, waiting for transfers between devices: none -> 10.2 us  [local(): recv = lax.all_to_all(packed, 'band', 0, 0)]
  transfers between devices with their start and end apart: 5 -> 7, of which waited for: 2 -> 5; matrix products, arithmetic and copies ran while one was open for 2% -> 3% of each run, Pallas kernels for 0% -> 10%
where the time goes in v1:
time: 68 us; the launch traced here: 67.8 us
  waiting for transfers between devices  19.6 us (29%)
  starting transfers between devices  19.2 us (28%)
  Pallas kernels  19.1 us (28%)
  local copies, waits for them, and re-layouts  4.82 us (7%)
  other arithmetic  4.45 us (7%)
  between operations  0.77 us (1%)
    all_to_all x1, starting transfers between devices, local(): recv = lax.all_to_all(packed, 'band', 0, 0)  10.8 us
    pallas_call x1, Pallas kernels, local(): pl.pallas_call(side_kernel, out_shape=(shape(BANDS, LANES), shape(BANDS,...  10.3 us
    all_to_all x1, waiting for transfers between devices, local(): recv = lax.all_to_all(packed, 'band', 0, 0)  10.2 us
    pallas_call x1, Pallas kernels, local(): pl.pallas_call(own_kernel, out_shape=(shape(16, 16, LANES), shape(PLANE,...  6.79 us
    ppermute x1, starting transfers between devices, local(): back_hi = lax.ppermute(q_lo, 'slab', to_prev)  4.36 us
    ppermute x1, waiting for transfers between devices, local(): from_below = lax.ppermute(up, 'slab', to_next)  3.9 us
    ppermute x1, waiting for transfers between devices, local(): back_lo = lax.ppermute(q_hi, 'slab', to_next)  3.82 us
    unnamed x13, local copies, waits for them, and re-layouts  3.64 us
  transfers between devices with their start and end apart: 7, of which 5 were waited for; matrix products, arithmetic and copies ran while one was open for 3% of the time, Pallas kernels for 10%

profile of v1, /device:TPU:32, one launch (start us, length us, event | category | flops | bytes accessed | tf_op | source)
XLA Modules:
  0.0 67.8 jit_solution(17207566169467317159)
XLA Ops:
  0.6 0.7 %iota_compare_fusion = pred[8,512]{1,0:T(8,128)(4,1)S(1)} fusion(s32[8]{0:T(128)} %sizes.1), kind=kLoop, calls=%fused_computation.6 | loop fusion | flops 4096 | bytes 4128 | tf_op jit(solution)/shard_map/lt | solution.py:169
  1.4 0.7 convert_element_type.33
  2.0 0.7 %convert_element_type.32 = f32[8,512]{1,0:T(8,128)S(1)} convert(s32[8,512]{1,0:T(8,128)} %offsets.1) | non-fusion elementwise | flops 4096 | bytes 32768 | tf_op jit(solution)/shard_map/convert_element_type | solution.py:174
  2.8 1.1 %copy_select_fusion = f32[8,13,512]{2,1,0:T(8,128)S(1)} fusion(f32[8,13,512]{2,0,1:T(8,128)} %param.9, pred[8,512]{1,0:T(8,128)(4,1)S(1)} %iota_compare_fusion), kind=kLoop, calls=%fused_computation.1 | loop fusion | flops 53248 | bytes 430080 | tf_op jit(solution)/shard_map/jit(_where)/select_n | solution.py:170
  3.8 0.1 pad.8.clone
  3.9 0.1 broadcast_in_dim.49
  4.0 0.1 maximum_maximum_fusion.pay
  4.1 3.5 %collective-permute-start.1 = (f32[8,16,512]{2,1,0:T(8,128)S(1)}, f32[8,16,512]{2,1,0:T(8,128)S(1)}, u32[]{:S(2)}, u32[]{:S(2)}) collective-permute-start(f32[8,16,512]{2,1,0:T(8,128)S(1)} %maximum_maximum_fusion.pay), channel_id=1, source_target_pairs={{1,0},{2,1},{3,2},{4,3},{5,4},{6,5},{7,6},{8,7},{9,8},{10,9},{11,1... | collective-permute-start | bytes 786440 | tf_op jit(solution)/shard_map/ppermute | solution.py:181
  7.5 0.0 collective-permute-start
  7.5 0.7 %copy.11 = s32[1,4,8,128]{3,1,2,0:T(4,128)S(1)} copy(s32[1,4,8,128]{3,2,1,0:T(8,128)} %bitcast.13) | data formatting | bytes 32768
  8.3 0.0 copy-start.1
  8.3 0.7 copy-done.1
  8.9 0.0 copy-start.2
  8.9 0.7 copy-done.2
  9.6 0.0 copy-start.3
  9.6 1.6 %copy-done.3 = f32[16,8,4096]{2,1,0:T(8,128)S(1)} copy-done((f32[16,8,4096]{2,1,0:T(8,128)S(1)}, f32[16,8,4096]{2,1,0:T(8,128)}, u32[]{:S(2)}) %copy-start.3) | copy-done | bytes 2097176
  11.2 6.8 %own_points.1 = (f32[16,16,128]{2,1,0:T(8,128)S(1)}, f32[4096,128]{1,0:T(8,128)S(1)}, f32[16,128]{1,0:T(8,128)S(1)}) custom-call(s32[4096]{0:T(1024)S(1)} %bitcast.16, s32[8]{0:T(128)S(1)} %copy-done.1, f32[16]{0:T(128)S(1)} %copy-done.2, f32[128,4096]{1,0:T(8,128)S(1)} %bitcast.17, f32[8,16,512]{2,1,0:T(8,128)S(1)} %maximum_maximum_fusion.pay), custom_call_target="tpu_custom_call" | custom-call | flops 2000000000 | bytes 8388608 | tf_op jit(solution)/shard_map/own_points/pallas_call | solution.py:183
  18.0 0.0 copy-start.5
  18.0 0.0 collective-permute-done.1.pay_hi
  18.0 0.3 fusion.size_hi
  18.3 0.0 collective-permute-done.pay_lo
  18.3 0.2 fusion.1.size_lo
  18.5 0.0 copy-start.4
  18.6 0.0 copy-start
  18.6 10.3 %side_points.1 = (f32[16,128]{1,0:T(8,128)S(1)}, f32[16,128]{1,0:T(8,128)S(1)}) custom-call(s32[4096]{0:T(1024)S(1)} %bitcast.15, s32[8]{0:T(128)S(1)} %fusion.1.size_lo, s32[4096]{0:T(1024)S(1)} %bitcast.14, s32[8]{0:T(128)S(1)} %fusion.size_hi, f32[4096,128]{1,0:T(8,128)S(1)} %get-tuple-element.12.table, f32[8,16,512]{2,1,0:T(8,128)S(1)} %collective-permute-done.pay_lo, ...), custom_call_target="tpu_custom_call" | custom-call | tf_op jit(solution)/shard_map/side_points/pallas_call | solution.py:205
  28.9 4.4 %collective-permute-start.2 = (f32[16,128]{1,0:T(8,128)S(1)}, f32[16,128]{1,0:T(8,128)S(1)}, u32[]{:S(2)}, u32[]{:S(2)}) collective-permute-start(f32[16,128]{1,0:T(8,128)S(1)} %get-tuple-element.13), channel_id=1, source_target_pairs={{1,0},{2,1},{3,2},{4,3},{5,4},{6,5},{7,6},{8,7},{9,8},{10,9},{11,1... | collective-permute-start | bytes 24584 | tf_op jit(solution)/shard_map/ppermute | solution.py:214
  33.3 0.0 collective-permute-start.3
  33.3 1.4 %collective-permute-done.2.q1 = f32[16,128]{1,0:T(8,128)S(1)} collective-permute-done((f32[16,128]{1,0:T(8,128)S(1)}, f32[16,128]{1,0:T(8,128)S(1)}, u32[]{:S(2)}, u32[]{:S(2)}) %collective-permute-start.2) | collective-permute-done | bytes 8224 | tf_op jit(solution)/shard_map/ppermute | solution.py:214
  34.6 3.8 %collective-permute-done.3.q2 = f32[16,128]{1,0:T(8,128)S(1)} collective-permute-done((f32[16,128]{1,0:T(8,128)S(1)}, f32[16,128]{1,0:T(8,128)S(1)}, u32[]{:S(2)}, u32[]{:S(2)}) %collective-permute-start.3) | collective-permute-done | bytes 8224 | tf_op jit(solution)/shard_map/ppermute | solution.py:215
  38.4 0.1 broadcast_in_dim.51.occ
  38.5 1.0 %partial_matrices.1 = f32[16,32,128]{2,1,0:T(8,128)} custom-call(f32[16,128]{1,0:T(8,128)S(1)} %get-tuple-element.11.q0, f32[16,128]{1,0:T(8,128)S(1)} %collective-permute-done.2.q1, f32[16,128]{1,0:T(8,128)S(1)} %collective-permute-done.3.q2, f32[16,128]{1,0:T(8,128)S(1)} %broadcast_in_dim.51.occ, f32[16,16,128]{2,1,0:T(8,128)S(1)} %get-tuple-element.15.pseudo), custom_call_target="tpu_custom_call" | custom-call | tf_op jit(solution)/shard_map/partial_matrices/pallas_call | solution.py:217
  39.5 10.8 %all-to-all-start = ((f32[16,32,128]{2,1,0:T(8,128)}), f32[16,32,128]{2,1,0:T(8,128)S(1)}, u32[]{:S(2)}, u32[]{:S(2)}) async-start(f32[16,32,128]{2,1,0:T(8,128)} %partial_matrices.1), calls=%async_computation | async-start | bytes 524288 | tf_op jit(solution)/shard_map/all_to_all | solution.py:225
  50.3 0.0 copy-done.5
  50.3 0.2 tile.10.coupling
  50.5 0.0 copy-done.4
  50.6 10.2 %all-to-all-done.recv = f32[16,32,128]{2,1,0:T(8,128)S(1)} async-done(((f32[16,32,128]{2,1,0:T(8,128)}), f32[16,32,128]{2,1,0:T(8,128)S(1)}, u32[]{:S(2)}, u32[]{:S(2)}) %all-to-all-start) | async-done | bytes 262176 | tf_op jit(solution)/shard_map/all_to_all | solution.py:225
  60.8 0.0 copy-done
  60.8 1.0 %charges.1 = (f32[8,256]{1,0:T(8,128)S(1)}, f32[8,256]{1,0:T(8,128)S(1)}, f32[8,256]{1,0:T(8,128)S(1)}, f32[16,128]{1,0:T(8,128)S(1)}) custom-call(s32[1]{0:T(128)} %bitcast.start, f32[16,32,128]{2,1,0:T(8,128)S(1)} %all-to-all-done.recv, f32[9,16,128]{2,1,0:T(8,128)S(1)} %tile.10.coupling, f32[9,8,512]{2,1,0:T(8,128)S(1)} %select_bitcast_fusion.shapes, ...), custom_call_target="tpu_custom_call" | custom-call | tf_op jit(solution)/shard_map/charges/pallas_call | solution.py:231
  61.8 0.1 reshape.52
  61.9 0.1 collective-permute-start.4
  61.9 0.5 collective-permute-start.5
  62.4 0.6 slice_bitcast_fusion
  63.1 0.2 collective-permute-done.4
  63.3 3.9 %collective-permute-done.5 = f32[8,256]{1,0:T(8,128)S(1)} collective-permute-done((f32[8,256]{1,0:T(8,128)S(1)}, f32[8,256]{1,0:T(8,128)S(1)}, u32[]{:S(2)}, u32[]{:S(2)}) %collective-permute-start.5) | collective-permute-done | bytes 8224 | tf_op jit(solution)/shard_map/ppermute | solution.py:240
  67.2 0.6 add_add_fusion
  (6 shorter events, 0.1 us)
Async XLA Ops:
  4.1 13.9 %collective-permute-start.1 = (f32[8,16,512]{2,1,0:T(8,128)S(1)}, f32[8,16,512]{2,1,0:T(8,128)S(1)}, u32[]{:S(2)}, u32[]{:S(2)}) collective-permute-start(f32[8,16,512]{2,1,0:T(8,128)S(1)} %maximum_maximum_fusion.pay), channel_id=1, source_target_pairs={{1,0},{2,1},{3,2},{4,3},{5,4},{6,5},{7,6},{8,7},{9,8},{10,9},{11,1... | collective-permute-start | bytes 786440 | tf_op jit(solution)/shard_map/ppermute | solution.py:181
  7.5 10.7 %collective-permute-start = (f32[8,16,512]{2,1,0:T(8,128)S(1)}, f32[8,16,512]{2,1,0:T(8,128)S(1)}, u32[]{:S(2)}, u32[]{:S(2)}) collective-permute-start(f32[8,16,512]{2,1,0:T(8,128)S(1)} %maximum_maximum_fusion.pay), channel_id=1, source_target_pairs={{0,1},{1,2},{2,3},{3,4},{4,5},{5,6},{6,7},{7,8},{8,9},{9,10},{10,1... | collective-permute-start | bytes 786440 | tf_op jit(solution)/shard_map/ppermute | solution.py:180
  8.3 0.7 copy-start.1
  8.9 0.7 copy-start.2
  9.6 1.6 %copy-start.3 = (f32[16,8,4096]{2,1,0:T(8,128)S(1)}, f32[16,8,4096]{2,1,0:T(8,128)}, u32[]{:S(2)}) copy-start(f32[16,8,4096]{2,1,0:T(8,128)} %param.7) | copy-start | bytes 6291460
  18.0 32.3 %copy-start.5 = (f32[9,13,13]{2,1,0:T(8,128)S(1)}, f32[9,13,13]{2,1,0:T(8,128)}, u32[]{:S(2)}) copy-start(f32[9,13,13]{2,1,0:T(8,128)} %param.11) | copy-start | bytes 18256
  18.5 32.0 %copy-start.4 = (f32[8,9,512]{2,0,1:T(8,128)S(1)}, f32[8,9,512]{2,0,1:T(8,128)}, u32[]{:S(2)}) copy-start(f32[8,9,512]{2,0,1:T(8,128)} %param.10) | copy-start | bytes 442372
  18.6 42.3 %copy-start = (s32[8,512]{1,0:T(8,128)S(1)}, s32[8,512]{1,0:T(8,128)}, u32[]{:S(2)}) copy-start(s32[8,512]{1,0:T(8,128)} %offsets.1) | copy-start | bytes 49156
  28.9 5.7 %collective-permute-start.2 = (f32[16,128]{1,0:T(8,128)S(1)}, f32[16,128]{1,0:T(8,128)S(1)}, u32[]{:S(2)}, u32[]{:S(2)}) collective-permute-start(f32[16,128]{1,0:T(8,128)S(1)} %get-tuple-element.13), channel_id=1, source_target_pairs={{1,0},{2,1},{3,2},{4,3},{5,4},{6,5},{7,6},{8,7},{9,8},{10,9},{11,1... | collective-permute-start | bytes 24584 | tf_op jit(solution)/shard_map/ppermute | solution.py:214
  33.3 5.2 %collective-permute-start.3 = (f32[16,128]{1,0:T(8,128)S(1)}, f32[16,128]{1,0:T(8,128)S(1)}, u32[]{:S(2)}, u32[]{:S(2)}) collective-permute-start(f32[16,128]{1,0:T(8,128)S(1)} %get-tuple-element.14), channel_id=1, source_target_pairs={{0,1},{1,2},{2,3},{3,4},{4,5},{5,6},{6,7},{7,8},{8,9},{9,10},{10,1... | collective-permute-start | bytes 24584 | tf_op jit(solution)/shard_map/ppermute | solution.py:215
  39.5 21.3 %all-to-all-start = ((f32[16,32,128]{2,1,0:T(8,128)}), f32[16,32,128]{2,1,0:T(8,128)S(1)}, u32[]{:S(2)}, u32[]{:S(2)}) async-start(f32[16,32,128]{2,1,0:T(8,128)} %partial_matrices.1), calls=%async_computation | async-start | bytes 524288 | tf_op jit(solution)/shard_map/all_to_all | solution.py:225
  61.9 1.5 %collective-permute-start.4 = (f32[8,256]{1,0:T(8,128)S(1)}, f32[8,256]{1,0:T(8,128)S(1)}, u32[]{:S(2)}, u32[]{:S(2)}) collective-permute-start(f32[8,256]{1,0:T(8,128)S(1)} %get-tuple-element.17), channel_id=1, source_target_pairs={{1,0},{2,1},{3,2},{4,3},{5,4},{6,5},{7,6},{8,7},{9,8},{10,9},{11,1... | collective-permute-start | bytes 24584 | tf_op jit(solution)/shard_map/ppermute | solution.py:239
  61.9 5.3 %collective-permute-start.5 = (f32[8,256]{1,0:T(8,128)S(1)}, f32[8,256]{1,0:T(8,128)S(1)}, u32[]{:S(2)}, u32[]{:S(2)}) collective-permute-start(f32[8,256]{1,0:T(8,128)S(1)} %get-tuple-element.18), channel_id=1, source_target_pairs={{0,1},{1,2},{2,3},{3,4},{4,5},{5,6},{6,7},{7,8},{8,9},{9,10},{10,1... | collective-permute-start | bytes 24584 | tf_op jit(solution)/shard_map/ppermute | solution.py:240

commit v2 on v1

v2 whole, which is shorter than its diff:
```python
import jax
import jax.numpy as jnp
import numpy as np
from jax import lax
from jax.experimental import pallas as pl
from jax.experimental.pallas import tpu as pltpu
from jax.sharding import PartitionSpec as P

HALO = 5
PLANE = 4096
CZ = 8
ATOM_DEV = 8
SPHERE = 512
NI = 13
NL = 9
BANDS = 16
LANES = 128
STEP = 32
HIGHEST = lax.Precision.HIGHEST
F32 = jnp.float32
BF16 = jnp.bfloat16

VM = pl.BlockSpec(memory_space=pltpu.VMEM)
SM = pl.BlockSpec(memory_space=pltpu.SMEM)


def params():
    return pltpu.CompilerParams(vmem_limit_bytes=48 * 2**20)


def gather_rows(points, row, first, last, table, rows, base):
    def body(step, carry):
        k = pl.multiple_of(step * STEP, STEP)
        for u in range(STEP):
            rows[pl.ds(base + k + u, 1), :] = table[pl.ds(points[row, k + u], 1), :]
        return carry

    lax.fori_loop(first, last, body, 0)


def project(pay, rows, shift, planes, begin, end):
    width = end - begin
    span = len(planes) * 16
    lane_plane = lax.broadcasted_iota(jnp.int32, (16, LANES), 1) % CZ
    sub = lax.broadcasted_iota(jnp.int32, (16, width), 0)
    parts = []
    for a in range(ATOM_DEV):
        block = pay[a * 16 : (a + 1) * 16, begin:end]
        plane = block[15:16, :].astype(jnp.int32) + shift
        proj = jnp.where(sub < NI, block, 0.0)
        high = proj.astype(BF16).astype(F32)
        low = proj - high
        pieces = []
        for piece in (high, low):
            for z in planes:
                pieces.append(jnp.where(plane == z, piece, 0.0))
        left = jnp.concatenate(pieces, axis=0).astype(BF16)
        gathered = rows[a * SPHERE + begin : a * SPHERE + end, :]
        g_high = gathered.astype(BF16)
        g_low = (gathered - g_high.astype(F32)).astype(BF16)
        first = jnp.dot(left, g_high, preferred_element_type=F32)
        second = jnp.dot(left[:span], g_low, preferred_element_type=F32)
        total = first[:span] + first[span:] + second
        acc = jnp.zeros((16, LANES), F32)
        for k, z in enumerate(planes):
            acc = acc + jnp.where(lane_plane == z, total[k * 16 : (k + 1) * 16, :], 0.0)
        parts.append(acc)
    summed = jnp.concatenate(parts, axis=0)
    band = lax.broadcasted_iota(jnp.int32, (BANDS, LANES), 0)
    lane_band = lax.broadcasted_iota(jnp.int32, (BANDS, LANES), 1) // CZ
    pick = (band == lane_band).astype(F32)
    return lax.dot_general(
        pick, summed, (((1,), (1,)), ((), ())), precision=HIGHEST, preferred_element_type=F32
    )


def sort_kernel(sizes, offsets, projectors, pay, lists):
    sub = lax.broadcasted_iota(jnp.int32, (ATOM_DEV, SPHERE), 0)
    lane = lax.broadcasted_iota(jnp.int32, (ATOM_DEV, SPHERE), 1)
    size = jnp.zeros((ATOM_DEV, SPHERE), jnp.int32)
    for a in range(ATOM_DEV):
        size = jnp.where(sub == a, sizes[a], size)
    live = lane < size
    off = offsets[...]
    plane = off >> 12
    point = off & (PLANE - 1)
    below = live & (plane < HALO)
    above = live & (plane >= HALO + CZ)
    own = live & (plane >= HALO) & (plane < HALO + CZ)
    flags = jnp.concatenate(
        [jnp.where(m, 1.0, 0.0) for m in (below, own, above)] + [jnp.zeros((8, SPHERE), F32)],
        axis=0,
    ).astype(BF16)
    before = lax.broadcasted_iota(jnp.int32, (SPHERE, SPHERE), 0)
    after = lax.broadcasted_iota(jnp.int32, (SPHERE, SPHERE), 1)
    until = jnp.where(before <= after, 1.0, 0.0).astype(BF16)
    rank = jnp.dot(flags, until, preferred_element_type=F32).astype(jnp.int32)
    n_below = jnp.max(rank[0:8], axis=1, keepdims=True)
    n_own = jnp.max(rank[8:16], axis=1, keepdims=True)
    n_above = jnp.max(rank[16:24], axis=1, keepdims=True)
    place = jnp.where(
        below,
        rank[0:8] - 1,
        jnp.where(own, n_below + rank[8:16] - 1, jnp.where(above, SPHERE - rank[16:24], -1)),
    )
    table = jnp.concatenate(
        [
            projectors[...],
            (point >> 6).astype(F32)[None],
            (point & 63).astype(F32)[None],
            plane.astype(F32)[None],
        ],
        axis=0,
    )
    table = jnp.transpose(table, (1, 0, 2))
    points = []
    for a in range(ATOM_DEV):
        high = table[a].astype(BF16)
        low = (table[a] - high.astype(F32)).astype(BF16)
        move = jnp.where(before == place[a : a + 1, :], 1.0, 0.0).astype(BF16)
        moved = lax.dot_general(
            jnp.concatenate([high, low], axis=0),
            move,
            (((1,), (1,)), ((), ())),
            preferred_element_type=F32,
        )
        moved = moved[0:16] + moved[16:32]
        pay[a * 16 : (a + 1) * 16, :] = moved
        points.append(moved[13:14] * 64.0 + moved[14:15])
    points = jnp.concatenate(points, axis=0)
    pay[128:136, :] = points
    pay[136:144, :] = jnp.where(lane < SPHERE // 2, n_below, n_above).astype(F32)
    lists[0:8, :] = points.astype(jnp.int32)
    lists[8:16, :] = jnp.where(lane < SPHERE // 2, n_below, n_below + n_own)


def own_kernel(lists, occ, x, pay, pseudo, table, q, rows):
    rows[...] = jnp.zeros_like(rows)
    for c in range(PLANE // LANES):
        cols = slice(c * LANES, (c + 1) * LANES)
        acc = jnp.zeros((CZ, LANES), F32)
        for n in range(BANDS):
            v = x[n * CZ : (n + 1) * CZ, cols]
            acc = acc + occ[n] * (v * v)
        pseudo[c // 2, (c % 2) * CZ : (c % 2 + 1) * CZ, :] = acc
        table[cols, :] = x[:, cols].T
    for a in range(ATOM_DEV):
        first = lists[8 + a, 0] // STEP
        last = (lists[8 + a, SPHERE - 1] + (STEP - 1)) // STEP
        gather_rows(lists, a, first, last, table, rows, a * SPHERE)
    q[...] = project(pay, rows, -HALO, range(CZ), 0, SPHERE)


def side_kernel(table, pay_lo, pay_hi, q_lo, q_hi, rows, ints, lists, sem):
    ints[0:16, :] = pay_lo[128:144, :].astype(jnp.int32)
    ints[16:32, :] = pay_hi[128:144, :].astype(jnp.int32)
    copy = pltpu.make_async_copy(ints, lists, sem)
    copy.start()
    rows[...] = jnp.zeros_like(rows)
    copy.wait()
    half = SPHERE // 2
    most = lists[8, SPHERE - 1]
    for a in range(ATOM_DEV):
        most = jnp.maximum(most, jnp.maximum(lists[8 + a, SPHERE - 1], lists[24 + a, 0]))

    def from_below():
        for a in range(ATOM_DEV):
            first = (SPHERE - lists[8 + a, SPHERE - 1]) // STEP
            gather_rows(lists, a, first, SPHERE // STEP, table, rows, a * SPHERE)

    def from_above():
        for a in range(ATOM_DEV):
            last = (lists[24 + a, 0] + (STEP - 1)) // STEP
            gather_rows(lists, 16 + a, 0, last, table, rows, a * SPHERE)

    @pl.when(most <= half)
    def _():
        from_below()
        from_above()
        q_lo[...] = project(pay_lo, rows, -HALO - CZ, range(HALO), half, SPHERE)
        q_hi[...] = project(pay_hi, rows, CZ - HALO, range(CZ - HALO, CZ), 0, half)

    @pl.when(most > half)
    def _():
        from_below()
        q_lo[...] = project(pay_lo, rows, -HALO - CZ, range(HALO), 0, SPHERE)
        from_above()
        q_hi[...] = project(pay_hi, rows, CZ - HALO, range(CZ - HALO, CZ), 0, SPHERE)


def matrix_kernel(q0, q1, q2, occ, pseudo, out):
    proj = q0[...] + q1[...] + q2[...]
    weighted = proj * occ[...]
    full = lax.dot_general(
        weighted, proj, (((0,), (0,)), ((), ())), precision=HIGHEST, preferred_element_type=F32
    )
    lane_atom = lax.broadcasted_iota(jnp.int32, (16, LANES), 1) // 16
    acc = jnp.zeros((16, LANES), F32)
    for a in range(ATOM_DEV):
        acc = acc + jnp.where(lane_atom == a, full[a * 16 : (a + 1) * 16, :], 0.0)
    i = lax.broadcasted_iota(jnp.int32, (8, LANES), 0)
    j = lax.broadcasted_iota(jnp.int32, (8, LANES), 1) % 16
    corner = pltpu.roll(pltpu.roll(acc[8:16], 1, 0), LANES - 8, 1)
    packed = jnp.where(j < i, corner, acc[0:8])
    for b in range(16):
        out[b, 0:16, :] = pseudo[b]
        out[b, 16:24, :] = packed


def charge_kernel(start, recv, coupling, shapes, offsets, core, down, up, matrices):
    total = recv[0]
    for b in range(1, 16):
        total = total + recv[b]
    matrix = total[16:24]
    matrices[...] = matrix
    per_lane = jnp.concatenate(
        [jnp.sum(coupling[l] * matrix, axis=0, keepdims=True) for l in range(NL)], axis=0
    )
    atom = lax.broadcasted_iota(jnp.int32, (ATOM_DEV, LANES), 0)
    lane_atom = lax.broadcasted_iota(jnp.int32, (ATOM_DEV, LANES), 1) // 16
    pick = (atom == lane_atom).astype(F32)
    charges = lax.dot_general(
        pick, per_lane, (((1,), (1,)), ((), ())), precision=HIGHEST, preferred_element_type=F32
    )
    comp = jnp.zeros((ATOM_DEV, SPHERE), F32)
    for l in range(NL):
        comp = comp + charges[:, l : l + 1] * shapes[l]
    c1 = comp.astype(BF16).astype(F32)
    c2 = (comp - c1).astype(BF16).astype(F32)
    c3 = comp - c1 - c2
    plane = offsets[...] >> 12
    column = (offsets[...] & (PLANE - 1)) - start[0]
    row = lax.broadcasted_iota(jnp.int32, (24, SPHERE), 0)
    target = jnp.where(row < 8, row + HALO, jnp.where(row < 16, row - 11, row - 3))
    col = lax.broadcasted_iota(jnp.int32, (256, SPHERE), 0)
    acc = jnp.zeros((80, 256), F32)
    for a in range(ATOM_DEV):
        here = target == plane[a : a + 1, :]
        left = jnp.concatenate(
            [jnp.where(here, c[a : a + 1, :], 0.0) for c in (c1, c2, c3)]
            + [jnp.zeros((8, SPHERE), F32)],
            axis=0,
        ).astype(BF16)
        right = jnp.where(col == column[a : a + 1, :], 1.0, 0.0).astype(BF16)
        acc = acc + lax.dot_general(
            left, right, (((1,), (1,)), ((), ())), preferred_element_type=F32
        )
    placed = acc[0:24] + acc[24:48] + acc[48:72]
    core[...] = placed[0:8] + jnp.concatenate([total[0:8], total[8:16]], axis=1)
    down[...] = placed[8:16]
    up[...] = placed[16:24]


def shape(*dims):
    return jax.ShapeDtypeStruct(dims, F32)


def packed_places():
    places = {}
    for i in range(NI):
        for j in range(NI):
            r, c = min(i, j), max(i, j)
            places[i, j] = (r, c) if r < 8 else (c - 7, r - 8)
    return places


def local(orbitals, occupations, projectors, shapes, coupling, sphere_offsets, sphere_sizes):
    slabs = lax.axis_size("slab")
    to_next = [(i, (i + 1) % slabs) for i in range(slabs)]
    to_prev = [((i + 1) % slabs, i) for i in range(slabs)]
    pay, lists = pl.pallas_call(
        sort_kernel,
        out_shape=(shape(144, SPHERE), jax.ShapeDtypeStruct((16, SPHERE), jnp.int32)),
        in_specs=[SM, VM, VM],
        out_specs=(VM, VM),
        compiler_params=params(),
        name="sort_points",
    )(sphere_sizes, sphere_offsets, projectors.transpose(1, 0, 2))
    pay_lo = lax.ppermute(pay, "slab", to_next)
    pay_hi = lax.ppermute(pay, "slab", to_prev)

    pseudo, table, q_own = pl.pallas_call(
        own_kernel,
        out_shape=(shape(16, 16, LANES), shape(PLANE, LANES), shape(BANDS, LANES)),
        in_specs=[SM, SM, VM, VM],
        out_specs=(VM, VM, VM),
        scratch_shapes=[pltpu.VMEM((ATOM_DEV * SPHERE, LANES), F32)],
        compiler_params=params(),
        cost_estimate=pl.CostEstimate(flops=2 * 10**9, bytes_accessed=8 * 2**20, transcendentals=0),
        name="own_points",
    )(lists, occupations, orbitals.reshape(BANDS * CZ, PLANE), pay)

    q_lo, q_hi = pl.pallas_call(
        side_kernel,
        out_shape=(shape(BANDS, LANES), shape(BANDS, LANES)),
        in_specs=[VM, VM, VM],
        out_specs=(VM, VM),
        scratch_shapes=[
            pltpu.VMEM((ATOM_DEV * SPHERE, LANES), F32),
            pltpu.VMEM((32, SPHERE), jnp.int32),
            pltpu.SMEM((32, SPHERE), jnp.int32),
            pltpu.SemaphoreType.DMA,
        ],
        compiler_params=params(),
        name="side_points",
    )(table, pay_lo, pay_hi)
    back_hi = lax.ppermute(q_lo, "slab", to_prev)
    back_lo = lax.ppermute(q_hi, "slab", to_next)

    packed = pl.pallas_call(
        matrix_kernel,
        out_shape=shape(16, 24, LANES),
        in_specs=[VM] * 5,
        out_specs=VM,
        compiler_params=params(),
        name="partial_matrices",
    )(q_own, back_hi, back_lo, jnp.broadcast_to(occupations[:, None], (BANDS, LANES)), pseudo)
    recv = lax.all_to_all(packed, "band", 0, 0)

    places = packed_places()
    unpack = np.zeros((8, 16, NI, NI), np.float32)
    for (i, j), (p, q) in places.items():
        unpack[p, q, i, j] = 1.0
    coupling_packed = jnp.einsum("lij,pqij->lpq", coupling, unpack, precision=HIGHEST)
    coupling_lanes = jnp.tile(coupling_packed, (1, 1, ATOM_DEV))
    live = jnp.arange(SPHERE, dtype=jnp.int32)[None, :] < sphere_sizes[:, None]
    shapes_live = jnp.where(live[:, None, :], shapes, 0.0).transpose(1, 0, 2)
    width = PLANE // lax.axis_size("band")
    start = (lax.axis_index("band") * width).astype(jnp.int32).reshape(1)
    core, down, up, matrices = pl.pallas_call(
        charge_kernel,
        out_shape=(shape(CZ, 256), shape(CZ, 256), shape(CZ, 256), shape(8, LANES)),
        in_specs=[SM, VM, VM, VM, VM],
        out_specs=(VM, VM, VM, VM),
        compiler_params=params(),
        name="charges",
    )(start, recv, coupling_lanes, shapes_live, sphere_offsets)
    from_above = lax.ppermute(down, "slab", to_prev)
    from_below = lax.ppermute(up, "slab", to_next)
    density = core + from_above + from_below
    density_matrices = jnp.einsum(
        "paq,pqij->aij", matrices.reshape(8, ATOM_DEV, 16), unpack, precision=HIGHEST
    )
    return (density, density_matrices)


def solution(mesh):
    placed = (
        P("band", "slab", None),
        P("band"),
        P("slab", None, None),
        P("slab", None, None),
        P(),
        P("slab", None),
        P("slab"),
    )
    return jax.shard_map(
        local,
        mesh=mesh,
        in_specs=placed,
        out_specs=(P("slab", "band"), P("slab", None, None)),
        check_vma=False,
    )
```

time: 68 us -> 59.9 us (0.88)
  other arithmetic: 4.45 us -> 0.69 us
  starting transfers between devices: 19.2 us -> 16.3 us
  waiting for transfers between devices: 19.6 us -> 17 us
  matrix products: 0 us -> 2.5 us
  Pallas kernels: 19.1 us -> 17.2 us
    pallas_call x1, Pallas kernels: 10.3 us -> 5.95 us  [local(): pl.pallas_call(side_kernel, out_shape=(shape(BANDS, LANES), shape(BANDS,...]
    ppermute x1, starting transfers between devices: 4.36 us -> 1.04 us  [local(): back_hi = lax.ppermute(q_lo, 'slab', to_prev)]
    dot_general x0 -> x2, matrix products: none -> 2.5 us  [the longest x1 1.7 us: local(): jnp.einsum('paq,pqij->aij', matrices.reshape(8, ATOM_DEV, 16), unpack, pr...]
    pallas_call x1 -> x2, Pallas kernels: 0.99 us -> 3.22 us  [the longest x1 2.21 us: local(): pl.pallas_call(sort_kernel, out_shape=(shape(144, SPHERE), jax.ShapeDtype...]
    convert_element_type x6 -> x0, other arithmetic: 1.93 us -> none  [the longest x1 0.72 us: local(): sphere_offsets.astype(F32)[:, None, :]]
    ppermute x1, waiting for transfers between devices: 1.36 us -> 0.23 us  [local(): back_hi = lax.ppermute(q_lo, 'slab', to_prev)]
    select_n x1 -> x0, other arithmetic: 1.08 us -> none  [local(): masked = jnp.where(live[:, None, :], projectors, 0.0)]
    unnamed x13 -> x24, local copies, waits for them, and re-layouts: 3.64 us -> 4.58 us
  transfers between devices with their start and end apart: 7 -> 7, of which waited for: 5 -> 4; matrix products, arithmetic and copies ran while one was open for 3% -> 5% of each run, Pallas kernels for 10% -> 12%
where the time goes in v2:
time: 59.9 us; the launch traced here: 59.5 us
  Pallas kernels  17.2 us (29%)
  waiting for transfers between devices  17 us (28%)
  starting transfers between devices  16.3 us (27%)
  local copies, waits for them, and re-layouts  5 us (8%)
  matrix products  2.5 us (4%)
  between operations  0.79 us (1%)
  other arithmetic  0.69 us (1%)
    all_to_all x1, starting transfers between devices, local(): recv = lax.all_to_all(packed, 'band', 0, 0)  10.8 us
    all_to_all x1, waiting for transfers between devices, local(): recv = lax.all_to_all(packed, 'band', 0, 0)  9.94 us
    pallas_call x1, Pallas kernels, local(): pl.pallas_call(own_kernel, out_shape=(shape(16, 16, LANES), shape(PLANE,...  7.11 us
    pallas_call x1, Pallas kernels, local(): pl.pallas_call(side_kernel, out_shape=(shape(BANDS, LANES), shape(BANDS,...  5.95 us
    unnamed x24, local copies, waits for them, and re-layouts  4.58 us
    ppermute x1, starting transfers between devices, local(): pay_hi = lax.ppermute(pay, 'slab', to_prev)  3.84 us
    ppermute x1, waiting for transfers between devices, local(): back_lo = lax.ppermute(q_hi, 'slab', to_next)  3.82 us
    ppermute x1, waiting for transfers between devices, local(): from_below = lax.ppermute(up, 'slab', to_next)  2.99 us
  transfers between devices with their start and end apart: 7, of which 4 were waited for; matrix products, arithmetic and copies ran while one was open for 5% of the time, Pallas kernels for 12%

profile of v2, /device:TPU:32, one launch (start us, length us, event | category | flops | bytes accessed | tf_op | source)
XLA Modules:
  0.0 59.5 jit_solution(3742315585430760110)
XLA Ops:
  0.6 0.0 copy-start
  0.6 0.9 %copy-done = f32[8,13,512]{2,0,1:T(8,128)S(1)} copy-done((f32[8,13,512]{2,0,1:T(8,128)S(1)}, f32[8,13,512]{2,0,1:T(8,128)}, u32[]{:S(2)}) %copy-start) | copy-done | bytes 213016
  1.6 0.0 copy-start.1
  1.6 0.7 %copy-done.1 = s32[8,512]{1,0:T(8,128)S(1)} copy-done((s32[8,512]{1,0:T(8,128)S(1)}, s32[8,512]{1,0:T(8,128)}, u32[]{:S(2)}) %copy-start.1) | copy-done | bytes 16408
  2.3 0.0 copy-start.3
  2.3 0.7 %copy-done.3 = s32[8]{0:T(128)S(1)} copy-done((s32[8]{0:T(128)S(1)}, s32[8]{0:T(128)}, u32[]{:S(2)}) %copy-start.3) | copy-done | bytes 56
  2.9 2.2 %sort_points.1 = (f32[144,512]{1,0:T(8,128)S(1)}, s32[16,512]{1,0:T(8,128)S(1)}) custom-call(s32[8]{0:T(128)S(1)} %copy-done.3, s32[8,512]{1,0:T(8,128)S(1)} %copy-done.1, f32[13,8,512]{2,1,0:T(8,128)S(1)} %bitcast.21), custom_call_target="tpu_custom_call" | custom-call | tf_op jit(solution)/shard_map/sort_points/pallas_call | solution.py:271
  5.2 0.1 collective-permute-start
  5.2 3.8 %collective-permute-start.1 = (f32[144,512]{1,0:T(8,128)S(1)}, f32[144,512]{1,0:T(8,128)S(1)}, u32[]{:S(2)}, u32[]{:S(2)}) collective-permute-start(f32[144,512]{1,0:T(8,128)S(1)} %get-tuple-element.14.pay), channel_id=1, source_target_pairs={{1,0},{2,1},{3,2},{4,3},{5,4},{6,5},{7,6},{8,7},{9,8},{10,9},{11,1... | collective-permute-start | bytes 884744 | tf_op jit(solution)/shard_map/ppermute | solution.py:280
  9.1 0.0 copy-start.5
  9.1 0.7 %copy-done.5 = f32[16]{0:T(128)S(1)} copy-done((f32[16]{0:T(128)S(1)}, f32[16]{0:T(128)}, u32[]{:S(2)}) %copy-start.5) | copy-done | bytes 88
  9.7 0.0 copy-start.7
  9.7 1.6 %copy-done.7 = f32[16,8,4096]{2,1,0:T(8,128)S(1)} copy-done((f32[16,8,4096]{2,1,0:T(8,128)S(1)}, f32[16,8,4096]{2,1,0:T(8,128)}, u32[]{:S(2)}) %copy-start.7) | copy-done | bytes 2097176
  11.3 7.1 %own_points.1 = (f32[16,16,128]{2,1,0:T(8,128)S(1)}, f32[4096,128]{1,0:T(8,128)S(1)}, f32[16,128]{1,0:T(8,128)S(1)}) custom-call(s32[16,512]{1,0:T(8,128)S(1)} %get-tuple-element.13.lists, f32[16]{0:T(128)S(1)} %copy-done.5, f32[128,4096]{1,0:T(8,128)S(1)} %bitcast.22, f32[144,512]{1,0:T(8,128)S(1)} %get-tuple-element.14.pay), custom_call_target="tpu_custom_call" | custom-call | flops 2000000000 | bytes 8388608 | tf_op jit(solution)/shard_map/own_points/pallas_call | solution.py:282
  18.4 0.0 copy-start.9
  18.4 0.0 copy-start.10
  18.4 0.0 collective-permute-done.pay_lo
  18.5 0.0 collective-permute-done.1.pay_hi
  18.5 0.0 copy-start.6
  18.5 0.0 copy-start.4
  18.5 0.0 copy-start.11
  18.5 6.0 %side_points.1 = (f32[16,128]{1,0:T(8,128)S(1)}, f32[16,128]{1,0:T(8,128)S(1)}) custom-call(f32[4096,128]{1,0:T(8,128)S(1)} %get-tuple-element.16.table, f32[144,512]{1,0:T(8,128)S(1)} %collective-permute-done.pay_lo, f32[144,512]{1,0:T(8,128)S(1)} %collective-permute-done.1.pay_hi), custom_call_target="tpu_custom_call" | custom-call | tf_op jit(solution)/shard_map/side_points/pallas_call | solution.py:293
  24.5 0.0 copy-start.2
  24.5 0.0 copy-start.8
  24.5 1.0 %collective-permute-start.2 = (f32[16,128]{1,0:T(8,128)S(1)}, f32[16,128]{1,0:T(8,128)S(1)}, u32[]{:S(2)}, u32[]{:S(2)}) collective-permute-start(f32[16,128]{1,0:T(8,128)S(1)} %get-tuple-element.17), channel_id=1, source_target_pairs={{1,0},{2,1},{3,2},{4,3},{5,4},{6,5},{7,6},{8,7},{9,8},{10,9},{11,1... | collective-permute-start | bytes 24584 | tf_op jit(solution)/shard_map/ppermute | solution.py:307
  25.6 0.0 collective-permute-start.3
  25.6 0.0 copy-done.9
  25.6 0.0 copy-done.10
  25.6 0.8 %convolution_bitcast_fusion = f32[9,8,16]{0,2,1:T(8,128)S(1)} fusion(f32[8,16,13,13]{3,1,2,0:T(8,128)S(1)} %copy-done.9, f32[9,13,13]{2,1,0:T(8,128)S(1)} %copy-done.10), kind=kOutput, calls=%fused_computation | convolution fusion | flops 2336256 | bytes 97220 | tf_op jit(solution)/shard_map/lij,pqij->lpq/dot_general | solution.py:324
  26.4 0.1 copy.12
  26.5 0.1 tile.10.coupling
  26.7 0.2 collective-permute-done.2.q1
  26.9 3.8 %collective-permute-done.3.q2 = f32[16,128]{1,0:T(8,128)S(1)} collective-permute-done((f32[16,128]{1,0:T(8,128)S(1)}, f32[16,128]{1,0:T(8,128)S(1)}, u32[]{:S(2)}, u32[]{:S(2)}) %collective-permute-start.3) | collective-permute-done | bytes 8224 | tf_op jit(solution)/shard_map/ppermute | solution.py:308
  30.7 0.0 copy-done.6
  30.8 0.1 broadcast_in_dim.10.occ
  30.8 1.0 %partial_matrices.1 = f32[16,24,128]{2,1,0:T(8,128)} custom-call(f32[16,128]{1,0:T(8,128)S(1)} %get-tuple-element.15.q0, f32[16,128]{1,0:T(8,128)S(1)} %collective-permute-done.2.q1, f32[16,128]{1,0:T(8,128)S(1)} %collective-permute-done.3.q2, f32[16,128]{1,0:T(8,128)S(1)} %broadcast_in_dim.10.occ, f32[16,16,128]{2,1,0:T(8,128)S(1)} %get-tuple-element.19.pseudo), custom_call_target="tpu_custom_call" | custom-call | tf_op jit(solution)/shard_map/partial_matrices/pallas_call | solution.py:310
  31.8 10.8 %all-to-all-start = ((f32[16,24,128]{2,1,0:T(8,128)}), f32[16,24,128]{2,1,0:T(8,128)S(1)}, u32[]{:S(2)}, u32[]{:S(2)}) async-start(f32[16,24,128]{2,1,0:T(8,128)} %partial_matrices.1), calls=%async_computation | async-start | bytes 393216 | tf_op jit(solution)/shard_map/all_to_all | solution.py:318
  42.6 0.0 copy-done.4
  42.6 0.1 iota_compare_fusion
  42.7 0.0 copy-done.11
  42.7 9.9 %all-to-all-done.recv = f32[16,24,128]{2,1,0:T(8,128)S(1)} async-done(((f32[16,24,128]{2,1,0:T(8,128)}), f32[16,24,128]{2,1,0:T(8,128)S(1)}, u32[]{:S(2)}, u32[]{:S(2)}) %all-to-all-start) | async-done | bytes 196640 | tf_op jit(solution)/shard_map/all_to_all | solution.py:318
  52.6 0.0 copy-done.2
  52.6 0.9 %charges.1 = (f32[8,256]{1,0:T(8,128)S(1)}, f32[8,256]{1,0:T(8,128)S(1)}, f32[8,256]{1,0:T(8,128)S(1)}, f32[8,128]{1,0:T(8,128)S(1)}) custom-call(s32[1]{0:T(128)} %bitcast.start, f32[16,24,128]{2,1,0:T(8,128)S(1)} %all-to-all-done.recv, f32[9,8,128]{2,1,0:T(8,128)S(1)} %tile.10.coupling, f32[9,8,512]{2,1,0:T(8,128)S(1)} %select_bitcast_fusion.shapes, ...), custom_call_target="tpu_custom_call" | custom-call | tf_op jit(solution)/shard_map/charges/pallas_call | solution.py:330
  53.6 0.1 collective-permute-start.4
  53.7 0.5 collective-permute-start.5
  54.2 0.1 reshape.40
  54.2 0.0 copy-done.8
  54.2 1.7 %convolution_bitcast_fusion.1 = f32[8,13,13]{2,0,1:T(8,128)} fusion(f32[8,8,16,1]{2,1,0,3:T(8,128)S(1)} %reshape.40, f32[8,16,13,13]{3,1,0,2:T(8,128)S(1)} %copy-done.8), kind=kOutput, calls=%fused_computation.1 | convolution fusion | flops 2076672 | bytes 96032 | tf_op jit(solution)/shard_map/paq,pqij->aij/dot_general | solution.py:341
  55.9 0.0 collective-permute-done.4
  55.9 3.0 %collective-permute-done.5 = f32[8,256]{1,0:T(8,128)S(1)} collective-permute-done((f32[8,256]{1,0:T(8,128)S(1)}, f32[8,256]{1,0:T(8,128)S(1)}, u32[]{:S(2)}, u32[]{:S(2)}) %collective-permute-start.5) | collective-permute-done | bytes 8224 | tf_op jit(solution)/shard_map/ppermute | solution.py:339
  58.9 0.6 %add_add_fusion = f32[8,256]{1,0:T(8,128)} fusion(f32[8,256]{1,0:T(8,128)S(1)} %collective-permute-done.5, f32[8,256]{1,0:T(8,128)S(1)} %get-tuple-element.20, f32[8,256]{1,0:T(8,128)S(1)} %collective-permute-done.4), kind=kLoop, calls=%fused_computation.5 | loop fusion | flops 4096 | bytes 32768 | tf_op jit(solution)/shard_map/add | solution.py:340
  (2 shorter events, 0.0 us)
Async XLA Ops:
  0.6 0.9 %copy-start = (f32[8,13,512]{2,0,1:T(8,128)S(1)}, f32[8,13,512]{2,0,1:T(8,128)}, u32[]{:S(2)}) copy-start(f32[8,13,512]{2,0,1:T(8,128)} %param.11) | copy-start | bytes 638980
  1.6 0.7 %copy-start.1 = (s32[8,512]{1,0:T(8,128)S(1)}, s32[8,512]{1,0:T(8,128)}, u32[]{:S(2)}) copy-start(s32[8,512]{1,0:T(8,128)} %offsets.3) | copy-start | bytes 49156
  2.3 0.7 %copy-start.3 = (s32[8]{0:T(128)S(1)}, s32[8]{0:T(128)}, u32[]{:S(2)}) copy-start(s32[8]{0:T(128)} %sizes.1) | copy-start | bytes 100
  5.2 13.3 %collective-permute-start = (f32[144,512]{1,0:T(8,128)S(1)}, f32[144,512]{1,0:T(8,128)S(1)}, u32[]{:S(2)}, u32[]{:S(2)}) collective-permute-start(f32[144,512]{1,0:T(8,128)S(1)} %get-tuple-element.14.pay), channel_id=1, source_target_pairs={{0,1},{1,2},{2,3},{3,4},{4,5},{5,6},{6,7},{7,8},{8,9},{9,10},{10,1... | collective-permute-start | bytes 884744 | tf_op jit(solution)/shard_map/ppermute | solution.py:279
  5.2 13.2 %collective-permute-start.1 = (f32[144,512]{1,0:T(8,128)S(1)}, f32[144,512]{1,0:T(8,128)S(1)}, u32[]{:S(2)}, u32[]{:S(2)}) collective-permute-start(f32[144,512]{1,0:T(8,128)S(1)} %get-tuple-element.14.pay), channel_id=1, source_target_pairs={{1,0},{2,1},{3,2},{4,3},{5,4},{6,5},{7,6},{8,7},{9,8},{10,9},{11,1... | collective-permute-start | bytes 884744 | tf_op jit(solution)/shard_map/ppermute | solution.py:280
  9.1 0.7 %copy-start.5 = (f32[16]{0:T(128)S(1)}, f32[16]{0:T(128)}, u32[]{:S(2)}) copy-start(f32[16]{0:T(128)} %occ.1) | copy-start | bytes 196
  9.7 1.6 %copy-start.7 = (f32[16,8,4096]{2,1,0:T(8,128)S(1)}, f32[16,8,4096]{2,1,0:T(8,128)}, u32[]{:S(2)}) copy-start(f32[16,8,4096]{2,1,0:T(8,128)} %param.9) | copy-start | bytes 6291460
  18.4 7.1 %copy-start.9 = (f32[8,16,13,13]{3,1,2,0:T(8,128)S(1)}, f32[8,16,13,13]{3,1,2,0:T(8,128)}, u32[]{:S(2)}) copy-start(f32[8,16,13,13]{3,1,2,0:T(8,128)} %constant.11.clone) | copy-start | bytes 259588
  18.4 7.1 %copy-start.10 = (f32[9,13,13]{2,1,0:T(8,128)S(1)}, f32[9,13,13]{2,1,0:T(8,128)}, u32[]{:S(2)}) copy-start(f32[9,13,13]{2,1,0:T(8,128)} %param.13) | copy-start | bytes 18256
  18.5 12.3 %copy-start.6 = (f32[16]{0:T(128)S(1)}, f32[16]{0:T(128)}, u32[]{:S(2)}) copy-start(f32[16]{0:T(128)} %occ.1) | copy-start | bytes 196
  18.5 24.1 %copy-start.4 = (s32[8]{0:T(128)S(1)}, s32[8]{0:T(128)}, u32[]{:S(2)}) copy-start(s32[8]{0:T(128)} %sizes.1) | copy-start | bytes 100
  18.5 24.1 %copy-start.11 = (f32[8,9,512]{2,0,1:T(8,128)S(1)}, f32[8,9,512]{2,0,1:T(8,128)}, u32[]{:S(2)}) copy-start(f32[8,9,512]{2,0,1:T(8,128)} %param.12) | copy-start | bytes 442372
  24.5 28.1 %copy-start.2 = (s32[8,512]{1,0:T(8,128)S(1)}, s32[8,512]{1,0:T(8,128)}, u32[]{:S(2)}) copy-start(s32[8,512]{1,0:T(8,128)} %offsets.3) | copy-start | bytes 49156
  24.5 29.7 %copy-start.8 = (f32[8,16,13,13]{3,1,0,2:T(8,128)S(1)}, f32[8,16,13,13]{3,1,0,2:T(8,128)}, u32[]{:S(2)}) copy-start(f32[8,16,13,13]{3,1,0,2:T(8,128)} %constant.17) | copy-start | bytes 259588
  24.5 2.4 %collective-permute-start.2 = (f32[16,128]{1,0:T(8,128)S(1)}, f32[16,128]{1,0:T(8,128)S(1)}, u32[]{:S(2)}, u32[]{:S(2)}) collective-permute-start(f32[16,128]{1,0:T(8,128)S(1)} %get-tuple-element.17), channel_id=1, source_target_pairs={{1,0},{2,1},{3,2},{4,3},{5,4},{6,5},{7,6},{8,7},{9,8},{10,9},{11,1... | collective-permute-start | bytes 24584 | tf_op jit(solution)/shard_map/ppermute | solution.py:307
  25.6 5.2 %collective-permute-start.3 = (f32[16,128]{1,0:T(8,128)S(1)}, f32[16,128]{1,0:T(8,128)S(1)}, u32[]{:S(2)}, u32[]{:S(2)}) collective-permute-start(f32[16,128]{1,0:T(8,128)S(1)} %get-tuple-element.18), channel_id=1, source_target_pairs={{0,1},{1,2},{2,3},{3,4},{4,5},{5,6},{6,7},{7,8},{8,9},{9,10},{10,1... | collective-permute-start | bytes 24584 | tf_op jit(solution)/shard_map/ppermute | solution.py:308
  31.8 20.8 %all-to-all-start = ((f32[16,24,128]{2,1,0:T(8,128)}), f32[16,24,128]{2,1,0:T(8,128)S(1)}, u32[]{:S(2)}, u32[]{:S(2)}) async-start(f32[16,24,128]{2,1,0:T(8,128)} %partial_matrices.1), calls=%async_computation | async-start | bytes 393216 | tf_op jit(solution)/shard_map/all_to_all | solution.py:318
  53.6 2.4 %collective-permute-start.4 = (f32[8,256]{1,0:T(8,128)S(1)}, f32[8,256]{1,0:T(8,128)S(1)}, u32[]{:S(2)}, u32[]{:S(2)}) collective-permute-start(f32[8,256]{1,0:T(8,128)S(1)} %get-tuple-element.21), channel_id=1, source_target_pairs={{1,0},{2,1},{3,2},{4,3},{5,4},{6,5},{7,6},{8,7},{9,8},{10,9},{11,1... | collective-permute-start | bytes 24584 | tf_op jit(solution)/shard_map/ppermute | solution.py:338
  53.7 5.3 %collective-permute-start.5 = (f32[8,256]{1,0:T(8,128)S(1)}, f32[8,256]{1,0:T(8,128)S(1)}, u32[]{:S(2)}, u32[]{:S(2)}) collective-permute-start(f32[8,256]{1,0:T(8,128)S(1)} %get-tuple-element.22), channel_id=1, source_target_pairs={{0,1},{1,2},{2,3},{3,4},{4,5},{5,6},{6,7},{7,8},{8,9},{9,10},{10,1... | collective-permute-start | bytes 24584 | tf_op jit(solution)/shard_map/ppermute | solution.py:339

commit v3 on v2

--- a/solution.py
+++ b/solution.py
@@ -16,6 +16,9 @@
 BANDS = 16
 LANES = 128
 STEP = 32
+LIST = 16
+TILES = SPHERE // LANES
+SORTED = TILES * ATOM_DEV * 16
 HIGHEST = lax.Precision.HIGHEST
 F32 = jnp.float32
 BF16 = jnp.bfloat16
@@ -24,15 +27,16 @@
 SM = pl.BlockSpec(memory_space=pltpu.SMEM)
 
 
-def params():
-    return pltpu.CompilerParams(vmem_limit_bytes=48 * 2**20)
+def params(limit=48 * 2**20):
+    return pltpu.CompilerParams(vmem_limit_bytes=limit)
 
 
 def gather_rows(points, row, first, last, table, rows, base):
     def body(step, carry):
         k = pl.multiple_of(step * STEP, STEP)
+        at = (step >> 2) * (LIST * LANES) + row * LANES + (step & 3) * STEP
         for u in range(STEP):
-            rows[pl.ds(base + k + u, 1), :] = table[pl.ds(points[row, k + u], 1), :]
+            rows[pl.ds(base + k + u, 1), :] = table[pl.ds(points[at + u], 1), :]
         return carry
 
     lax.fori_loop(first, last, body, 0)
@@ -45,7 +49,13 @@
     sub = lax.broadcasted_iota(jnp.int32, (16, width), 0)
     parts = []
     for a in range(ATOM_DEV):
-        block = pay[a * 16 : (a + 1) * 16, begin:end]
+        block = jnp.concatenate(
+            [
+                pay[(t * ATOM_DEV + a) * 16 : (t * ATOM_DEV + a + 1) * 16, :]
+                for t in range(begin // LANES, end // LANES)
+            ],
+            axis=1,
+        )
         plane = block[15:16, :].astype(jnp.int32) + shift
         proj = jnp.where(sub < NI, block, 0.0)
         high = proj.astype(BF16).astype(F32)
@@ -74,6 +84,12 @@
     )
 
 
+def table_kernel(x, table):
+    for c in range(PLANE // LANES):
+        cols = slice(c * LANES, (c + 1) * LANES)
+        table[cols, :] = x[:, cols].T
+
+
 def sort_kernel(sizes, offsets, projectors, pay, lists):
     sub = lax.broadcasted_iota(jnp.int32, (ATOM_DEV, SPHERE), 0)
     lane = lax.broadcasted_iota(jnp.int32, (ATOM_DEV, SPHERE), 1)
@@ -125,16 +141,26 @@
             preferred_element_type=F32,
         )
         moved = moved[0:16] + moved[16:32]
-        pay[a * 16 : (a + 1) * 16, :] = moved
+        for t in range(TILES):
+            first = (t * ATOM_DEV + a) * 16
+            pay[first : first + 16, :] = moved[:, t * LANES : (t + 1) * LANES]
         points.append(moved[13:14] * 64.0 + moved[14:15])
     points = jnp.concatenate(points, axis=0)
-    pay[128:136, :] = points
-    pay[136:144, :] = jnp.where(lane < SPHERE // 2, n_below, n_above).astype(F32)
-    lists[0:8, :] = points.astype(jnp.int32)
-    lists[8:16, :] = jnp.where(lane < SPHERE // 2, n_below, n_below + n_own)
-
-
-def own_kernel(lists, occ, x, pay, pseudo, table, q, rows):
+    counts = jnp.where(lane < SPHERE // 2, n_below, n_above).astype(F32)
+    ends = jnp.where(lane < SPHERE // 2, n_below, n_below + n_own)
+    for t in range(TILES):
+        cols = slice(t * LANES, (t + 1) * LANES)
+        for k, (sent, kept) in enumerate(((points, points.astype(jnp.int32)), (counts, ends))):
+            first = t * LIST + k * ATOM_DEV
+            pay[SORTED + first : SORTED + first + ATOM_DEV, :] = sent[:, cols]
+            lists[first : first + ATOM_DEV, :] = kept[:, cols]
+
+
+def listed(points, row, k):
+    return points[(k // LANES * LIST + row) * LANES + k % LANES]
+
+
+def own_kernel(lists, occ, x, table, pay, pseudo, q, rows):
     rows[...] = jnp.zeros_like(rows)
     for c in range(PLANE // LANES):
         cols = slice(c * LANES, (c + 1) * LANES)
@@ -143,35 +169,30 @@
             v = x[n * CZ : (n + 1) * CZ, cols]
             acc = acc + occ[n] * (v * v)
         pseudo[c // 2, (c % 2) * CZ : (c % 2 + 1) * CZ, :] = acc
-        table[cols, :] = x[:, cols].T
-    for a in range(ATOM_DEV):
-        first = lists[8 + a, 0] // STEP
-        last = (lists[8 + a, SPHERE - 1] + (STEP - 1)) // STEP
+    for a in range(ATOM_DEV):
+        first = listed(lists, 8 + a, 0) // STEP
+        last = (listed(lists, 8 + a, SPHERE - 1) + (STEP - 1)) // STEP
         gather_rows(lists, a, first, last, table, rows, a * SPHERE)
     q[...] = project(pay, rows, -HALO, range(CZ), 0, SPHERE)
 
 
-def side_kernel(table, pay_lo, pay_hi, q_lo, q_hi, rows, ints, lists, sem):
-    ints[0:16, :] = pay_lo[128:144, :].astype(jnp.int32)
-    ints[16:32, :] = pay_hi[128:144, :].astype(jnp.int32)
-    copy = pltpu.make_async_copy(ints, lists, sem)
-    copy.start()
+def side_kernel(list_lo, list_hi, table, pay_lo, pay_hi, q_lo, q_hi, rows):
     rows[...] = jnp.zeros_like(rows)
-    copy.wait()
     half = SPHERE // 2
-    most = lists[8, SPHERE - 1]
-    for a in range(ATOM_DEV):
-        most = jnp.maximum(most, jnp.maximum(lists[8 + a, SPHERE - 1], lists[24 + a, 0]))
+    most = jnp.int32(0)
+    for a in range(ATOM_DEV):
+        most = jnp.maximum(most, listed(list_lo, 8 + a, SPHERE - 1))
+        most = jnp.maximum(most, listed(list_hi, 8 + a, 0))
 
     def from_below():
         for a in range(ATOM_DEV):
-            first = (SPHERE - lists[8 + a, SPHERE - 1]) // STEP
-            gather_rows(lists, a, first, SPHERE // STEP, table, rows, a * SPHERE)
+            first = (SPHERE - listed(list_lo, 8 + a, SPHERE - 1)) // STEP
+            gather_rows(list_lo, a, first, SPHERE // STEP, table, rows, a * SPHERE)
 
     def from_above():
         for a in range(ATOM_DEV):
-            last = (lists[24 + a, 0] + (STEP - 1)) // STEP
-            gather_rows(lists, 16 + a, 0, last, table, rows, a * SPHERE)
+            last = (listed(list_hi, 8 + a, 0) + (STEP - 1)) // STEP
+            gather_rows(list_hi, a, 0, last, table, rows, a * SPHERE)
 
     @pl.when(most <= half)
     def _():
@@ -268,42 +289,57 @@
     slabs = lax.axis_size("slab")
     to_next = [(i, (i + 1) % slabs) for i in range(slabs)]
     to_prev = [((i + 1) % slabs, i) for i in range(slabs)]
+    grid_values = orbitals.reshape(BANDS * CZ, PLANE)
+    table = pl.pallas_call(
+        table_kernel,
+        out_shape=shape(PLANE, LANES),
+        in_specs=[VM],
+        out_specs=VM,
+        compiler_params=params(),
+        cost_estimate=pl.CostEstimate(flops=0, bytes_accessed=8 * 2**20, transcendentals=0),
+        name="grid_table",
+    )(grid_values)
     pay, lists = pl.pallas_call(
         sort_kernel,
-        out_shape=(shape(144, SPHERE), jax.ShapeDtypeStruct((16, SPHERE), jnp.int32)),
+        out_shape=(
+            shape(SORTED + TILES * LIST, LANES),
+            jax.ShapeDtypeStruct((TILES * LIST, LANES), jnp.int32),
+        ),
         in_specs=[SM, VM, VM],
         out_specs=(VM, VM),
         compiler_params=params(),
+        cost_estimate=pl.CostEstimate(flops=10**9, bytes_accessed=8 * 2**20, transcendentals=0),
         name="sort_points",
     )(sphere_sizes, sphere_offsets, projectors.transpose(1, 0, 2))
     pay_lo = lax.ppermute(pay, "slab", to_next)
     pay_hi = lax.ppermute(pay, "slab", to_prev)
 
-    pseudo, table, q_own = pl.pallas_call(
+    pseudo, q_own = pl.pallas_call(
         own_kernel,
-        out_shape=(shape(16, 16, LANES), shape(PLANE, LANES), shape(BANDS, LANES)),
-        in_specs=[SM, SM, VM, VM],
-        out_specs=(VM, VM, VM),
+        out_shape=(shape(16, 16, LANES), shape(BANDS, LANES)),
+        in_specs=[SM, SM, VM, VM, VM],
+        out_specs=(VM, VM),
         scratch_shapes=[pltpu.VMEM((ATOM_DEV * SPHERE, LANES), F32)],
         compiler_params=params(),
-        cost_estimate=pl.CostEstimate(flops=2 * 10**9, bytes_accessed=8 * 2**20, transcendentals=0),
+        cost_estimate=pl.CostEstimate(flops=2 * 10**9, bytes_accessed=12 * 2**20, transcendentals=0),
         name="own_points",
-    )(lists, occupations, orbitals.reshape(BANDS * CZ, PLANE), pay)
+    )(lists.reshape(-1), occupations, grid_values, table, pay)
 
     q_lo, q_hi = pl.pallas_call(
         side_kernel,
         out_shape=(shape(BANDS, LANES), shape(BANDS, LANES)),
-        in_specs=[VM, VM, VM],
+        in_specs=[SM, SM, VM, VM, VM],
         out_specs=(VM, VM),
-        scratch_shapes=[
-            pltpu.VMEM((ATOM_DEV * SPHERE, LANES), F32),
-            pltpu.VMEM((32, SPHERE), jnp.int32),
-            pltpu.SMEM((32, SPHERE), jnp.int32),
-            pltpu.SemaphoreType.DMA,
-        ],
+        scratch_shapes=[pltpu.VMEM((ATOM_DEV * SPHERE, LANES), F32)],
         compiler_params=params(),
         name="side_points",
-    )(table, pay_lo, pay_hi)
+    )(
+        pay_lo[SORTED:].astype(jnp.int32).reshape(-1),
+        pay_hi[SORTED:].astype(jnp.int32).reshape(-1),
+        table,
+        pay_lo,
+        pay_hi,
+    )
     back_hi = lax.ppermute(q_lo, "slab", to_prev)
     back_lo = lax.ppermute(q_hi, "slab", to_next)
 

time: 59.9 us -> 56.6 us (0.945)
  Pallas kernels: 17.2 us -> 13 us
  waiting for transfers between devices: 17 us -> 20.4 us
  local copies, waits for them, and re-layouts: 5 us -> 2.95 us
    ppermute x1, waiting for transfers between devices: 0.03 us -> 3.41 us  [local(): pay_lo = lax.ppermute(pay, 'slab', to_next)]
    pallas_call x2 -> x3, Pallas kernels: 9.32 us -> 6.93 us  [the longest x1 4.13 us: local(): pl.pallas_call(own_kernel, out_shape=(shape(16, 16, LANES), shape(BANDS,...]
    unnamed x24 -> x22, local copies, waits for them, and re-layouts: 4.58 us -> 2.53 us
    pallas_call x1, Pallas kernels: 5.95 us -> 4.08 us  [local(): pl.pallas_call(side_kernel, out_shape=(shape(BANDS, LANES), shape(BANDS,...]
  transfers between devices with their start and end apart: 7 -> 7, of which waited for: 4 -> 5; matrix products, arithmetic and copies ran while one was open for 5% -> 5% of each run, Pallas kernels for 12% -> 8%
where the time goes in v3:
time: 56.6 us; the launch traced here: 56.5 us
  waiting for transfers between devices  20.4 us (36%)
  starting transfers between devices  16.2 us (29%)
  Pallas kernels  13 us (23%)
  local copies, waits for them, and re-layouts  2.95 us (5%)
  matrix products  2.5 us (4%)
  between operations  0.77 us (1%)
  other arithmetic  0.7 us (1%)
    all_to_all x1, starting transfers between devices, local(): recv = lax.all_to_all(packed, 'band', 0, 0)  10.8 us
    all_to_all x1, waiting for transfers between devices, local(): recv = lax.all_to_all(packed, 'band', 0, 0)  9.94 us
    pallas_call x1, Pallas kernels, local(): pl.pallas_call(own_kernel, out_shape=(shape(16, 16, LANES), shape(BANDS,...  4.13 us
    pallas_call x1, Pallas kernels, local(): pl.pallas_call(side_kernel, out_shape=(shape(BANDS, LANES), shape(BANDS,...  4.08 us
    ppermute x1, waiting for transfers between devices, local(): back_lo = lax.ppermute(q_hi, 'slab', to_next)  3.82 us
    ppermute x1, starting transfers between devices, local(): pay_hi = lax.ppermute(pay, 'slab', to_prev)  3.46 us
    ppermute x1, waiting for transfers between devices, local(): pay_lo = lax.ppermute(pay, 'slab', to_next)  3.41 us
    ppermute x1, waiting for transfers between devices, local(): from_below = lax.ppermute(up, 'slab', to_next)  2.99 us
  transfers between devices with their start and end apart: 7, of which 5 were waited for; matrix products, arithmetic and copies ran while one was open for 5% of the time, Pallas kernels for 8%

profile of v3, /device:TPU:32, one launch (start us, length us, event | category | flops | bytes accessed | tf_op | source)
XLA Modules:
  0.0 56.5 jit_solution(11636795498589606974)
XLA Ops:
  0.6 0.0 copy-start
  0.6 0.0 copy-start.1
  0.7 0.9 %copy-done.1 = s32[8,512]{1,0:T(8,128)S(1)} copy-done((s32[8,512]{1,0:T(8,128)S(1)}, s32[8,512]{1,0:T(8,128)}, u32[]{:S(2)}) %copy-start.1) | copy-done | bytes 16408
  1.5 0.0 copy-start.4
  1.5 0.7 %copy-done.4 = s32[8]{0:T(128)S(1)} copy-done((s32[8]{0:T(128)S(1)}, s32[8]{0:T(128)}, u32[]{:S(2)}) %copy-start.4) | copy-done | bytes 56
  2.2 0.0 copy-start.6
  2.2 0.9 %copy-done.6 = f32[8,13,512]{2,0,1:T(8,128)S(1)} copy-done((f32[8,13,512]{2,0,1:T(8,128)S(1)}, f32[8,13,512]{2,0,1:T(8,128)}, u32[]{:S(2)}) %copy-start.6) | copy-done | bytes 213016
  3.1 2.2 %sort_points.1 = (f32[576,128]{1,0:T(8,128)S(1)}, s32[64,128]{1,0:T(8,128)S(1)}) custom-call(s32[8]{0:T(128)S(1)} %copy-done.4, s32[8,512]{1,0:T(8,128)S(1)} %copy-done.1, f32[13,8,512]{2,1,0:T(8,128)S(1)} %bitcast.28), custom_call_target="tpu_custom_call" | custom-call | flops 1000000000 | bytes 8388608 | tf_op jit(solution)/shard_map/sort_points/pallas_call | solution.py:302
  5.3 3.5 %collective-permute-start.1 = (f32[576,128]{1,0:T(8,128)S(1)}, f32[576,128]{1,0:T(8,128)S(1)}, u32[]{:S(2)}, u32[]{:S(2)}) collective-permute-start(f32[576,128]{1,0:T(8,128)S(1)} %get-tuple-element.13.pay), channel_id=1, source_target_pairs={{1,0},{2,1},{3,2},{4,3},{5,4},{6,5},{7,6},{8,7},{9,8},{10,9},{11,1... | collective-permute-start | bytes 884744 | tf_op jit(solution)/shard_map/ppermute | solution.py:315
  8.8 0.0 collective-permute-start
  8.8 0.0 copy-done
  8.8 0.0 copy-start.3
  8.8 0.6 %grid_table.1.table = f32[4096,128]{1,0:T(8,128)S(1)} custom-call(f32[128,4096]{1,0:T(8,128)S(1)} %bitcast.26), custom_call_target="tpu_custom_call" | custom-call | bytes 8388608 | tf_op jit(solution)/shard_map/grid_table/pallas_call | solution.py:293
  9.4 0.1 copy-done.3
  9.4 4.1 %own_points.1 = (f32[16,16,128]{2,1,0:T(8,128)S(1)}, f32[16,128]{1,0:T(8,128)S(1)}) custom-call(s32[8192]{0:T(1024)S(1)} %bitcast.29, f32[16]{0:T(128)S(1)} %copy-done.3, f32[128,4096]{1,0:T(8,128)S(1)} %bitcast.27, f32[4096,128]{1,0:T(8,128)S(1)} %grid_table.1.table, f32[576,128]{1,0:T(8,128)S(1)} %get-tuple-element.13.pay), custom_call_target="tpu_custom_call" | custom-call | flops 2000000000 | bytes 12582912 | tf_op jit(solution)/shard_map/own_points/pallas_call | solution.py:317
  13.6 0.0 copy-start.8
  13.6 0.0 copy-start.9
  13.6 0.0 collective-permute-done.1.pay_hi
  13.6 3.4 %collective-permute-done.pay_lo = f32[576,128]{1,0:T(8,128)S(1)} collective-permute-done((f32[576,128]{1,0:T(8,128)S(1)}, f32[576,128]{1,0:T(8,128)S(1)}, u32[]{:S(2)}, u32[]{:S(2)}) %collective-permute-start) | collective-permute-done | bytes 294944 | tf_op jit(solution)/shard_map/ppermute | solution.py:314
  17.0 0.0 copy-start.5
  17.0 0.0 copy-start.10
  17.1 4.1 %side_points.1 = (f32[16,128]{1,0:T(8,128)S(1)}, f32[16,128]{1,0:T(8,128)S(1)}) custom-call(s32[8192]{0:T(1024)S(1)} %fusion.1.list_lo, s32[8192]{0:T(1024)S(1)} %fusion.list_hi, f32[4096,128]{1,0:T(8,128)S(1)} %grid_table.1.table, f32[576,128]{1,0:T(8,128)S(1)} %collective-permute-done.pay_lo, f32[576,128]{1,0:T(8,128)S(1)} %collective-permute-done.1.pay_hi), custom_call_target="tpu_custom_call" | custom-call | tf_op jit(solution)/shard_map/side_points/pallas_call | solution.py:328
  21.1 0.0 copy-start.2
  21.1 0.0 copy-start.7
  21.1 1.4 %collective-permute-start.2 = (f32[16,128]{1,0:T(8,128)S(1)}, f32[16,128]{1,0:T(8,128)S(1)}, u32[]{:S(2)}, u32[]{:S(2)}) collective-permute-start(f32[16,128]{1,0:T(8,128)S(1)} %get-tuple-element.15), channel_id=1, source_target_pairs={{1,0},{2,1},{3,2},{4,3},{5,4},{6,5},{7,6},{8,7},{9,8},{10,9},{11,1... | collective-permute-start | bytes 24584 | tf_op jit(solution)/shard_map/ppermute | solution.py:343
  22.6 0.0 collective-permute-start.3
  22.6 0.0 copy-done.8
  22.6 0.0 copy-done.9
  22.6 0.8 %convolution_bitcast_fusion = f32[9,8,16]{0,2,1:T(8,128)S(1)} fusion(f32[8,16,13,13]{3,1,2,0:T(8,128)S(1)} %copy-done.8, f32[9,13,13]{2,1,0:T(8,128)S(1)} %copy-done.9), kind=kOutput, calls=%fused_computation | convolution fusion | flops 2336256 | bytes 97220 | tf_op jit(solution)/shard_map/lij,pqij->lpq/dot_general | solution.py:360
  23.4 0.1 copy.12
  23.5 0.1 tile.10.coupling
  23.7 0.2 collective-permute-done.2.q1
  23.9 3.8 %collective-permute-done.3.q2 = f32[16,128]{1,0:T(8,128)S(1)} collective-permute-done((f32[16,128]{1,0:T(8,128)S(1)}, f32[16,128]{1,0:T(8,128)S(1)}, u32[]{:S(2)}, u32[]{:S(2)}) %collective-permute-start.3) | collective-permute-done | bytes 8224 | tf_op jit(solution)/shard_map/ppermute | solution.py:344
  27.7 0.1 broadcast_in_dim.10.occ
  27.8 1.0 %partial_matrices.1 = f32[16,24,128]{2,1,0:T(8,128)} custom-call(f32[16,128]{1,0:T(8,128)S(1)} %get-tuple-element.14.q0, f32[16,128]{1,0:T(8,128)S(1)} %collective-permute-done.2.q1, f32[16,128]{1,0:T(8,128)S(1)} %collective-permute-done.3.q2, f32[16,128]{1,0:T(8,128)S(1)} %broadcast_in_dim.10.occ, f32[16,16,128]{2,1,0:T(8,128)S(1)} %get-tuple-element.17.pseudo), custom_call_target="tpu_custom_call" | custom-call | tf_op jit(solution)/shard_map/partial_matrices/pallas_call | solution.py:346
  28.8 10.8 %all-to-all-start = ((f32[16,24,128]{2,1,0:T(8,128)}), f32[16,24,128]{2,1,0:T(8,128)S(1)}, u32[]{:S(2)}, u32[]{:S(2)}) async-start(f32[16,24,128]{2,1,0:T(8,128)} %partial_matrices.1), calls=%async_computation | async-start | bytes 393216 | tf_op jit(solution)/shard_map/all_to_all | solution.py:354
  39.6 0.0 copy-done.5
  39.6 0.1 iota_compare_fusion
  39.7 0.0 copy-done.10
  39.7 9.9 %all-to-all-done.recv = f32[16,24,128]{2,1,0:T(8,128)S(1)} async-done(((f32[16,24,128]{2,1,0:T(8,128)}), f32[16,24,128]{2,1,0:T(8,128)S(1)}, u32[]{:S(2)}, u32[]{:S(2)}) %all-to-all-start) | async-done | bytes 196640 | tf_op jit(solution)/shard_map/all_to_all | solution.py:354
  49.6 0.0 copy-done.2
  49.6 0.9 %charges.1 = (f32[8,256]{1,0:T(8,128)S(1)}, f32[8,256]{1,0:T(8,128)S(1)}, f32[8,256]{1,0:T(8,128)S(1)}, f32[8,128]{1,0:T(8,128)S(1)}) custom-call(s32[1]{0:T(128)} %bitcast.start, f32[16,24,128]{2,1,0:T(8,128)S(1)} %all-to-all-done.recv, f32[9,8,128]{2,1,0:T(8,128)S(1)} %tile.10.coupling, f32[9,8,512]{2,1,0:T(8,128)S(1)} %select_bitcast_fusion.shapes, ...), custom_call_target="tpu_custom_call" | custom-call | tf_op jit(solution)/shard_map/charges/pallas_call | solution.py:366
  50.6 0.1 collective-permute-start.4
  50.7 0.5 collective-permute-start.5
  51.2 0.1 reshape.52
  51.2 0.0 copy-done.7
  51.2 1.7 %convolution_bitcast_fusion.1 = f32[8,13,13]{2,0,1:T(8,128)} fusion(f32[8,8,16,1]{2,1,0,3:T(8,128)S(1)} %reshape.52, f32[8,16,13,13]{3,1,0,2:T(8,128)S(1)} %copy-done.7), kind=kOutput, calls=%fused_computation.1 | convolution fusion | flops 2076672 | bytes 96032 | tf_op jit(solution)/shard_map/paq,pqij->aij/dot_general | solution.py:377
  52.9 0.0 collective-permute-done.4
  52.9 3.0 %collective-permute-done.5 = f32[8,256]{1,0:T(8,128)S(1)} collective-permute-done((f32[8,256]{1,0:T(8,128)S(1)}, f32[8,256]{1,0:T(8,128)S(1)}, u32[]{:S(2)}, u32[]{:S(2)}) %collective-permute-start.5) | collective-permute-done | bytes 8224 | tf_op jit(solution)/shard_map/ppermute | solution.py:375
  55.9 0.6 %add_add_fusion = f32[8,256]{1,0:T(8,128)} fusion(f32[8,256]{1,0:T(8,128)S(1)} %collective-permute-done.5, f32[8,256]{1,0:T(8,128)S(1)} %get-tuple-element.18, f32[8,256]{1,0:T(8,128)S(1)} %collective-permute-done.4), kind=kLoop, calls=%fused_computation.9 | loop fusion | flops 4096 | bytes 32768 | tf_op jit(solution)/shard_map/add | solution.py:376
  (4 shorter events, 0.1 us)
Async XLA Ops:
  0.6 8.1 %copy-start = (f32[16,8,4096]{2,1,0:T(8,128)S(1)}, f32[16,8,4096]{2,1,0:T(8,128)}, u32[]{:S(2)}) copy-start(f32[16,8,4096]{2,1,0:T(8,128)} %param.9) | copy-start | bytes 6291460
  0.6 0.9 %copy-start.1 = (s32[8,512]{1,0:T(8,128)S(1)}, s32[8,512]{1,0:T(8,128)}, u32[]{:S(2)}) copy-start(s32[8,512]{1,0:T(8,128)} %offsets.3) | copy-start | bytes 49156
  1.5 0.7 %copy-start.4 = (s32[8]{0:T(128)S(1)}, s32[8]{0:T(128)}, u32[]{:S(2)}) copy-start(s32[8]{0:T(128)} %sizes.1) | copy-start | bytes 100
  2.2 0.9 %copy-start.6 = (f32[8,13,512]{2,0,1:T(8,128)S(1)}, f32[8,13,512]{2,0,1:T(8,128)}, u32[]{:S(2)}) copy-start(f32[8,13,512]{2,0,1:T(8,128)} %param.11) | copy-start | bytes 638980
  5.3 8.3 %collective-permute-start.1 = (f32[576,128]{1,0:T(8,128)S(1)}, f32[576,128]{1,0:T(8,128)S(1)}, u32[]{:S(2)}, u32[]{:S(2)}) collective-permute-start(f32[576,128]{1,0:T(8,128)S(1)} %get-tuple-element.13.pay), channel_id=1, source_target_pairs={{1,0},{2,1},{3,2},{4,3},{5,4},{6,5},{7,6},{8,7},{9,8},{10,9},{11,1... | collective-permute-start | bytes 884744 | tf_op jit(solution)/shard_map/ppermute | solution.py:315
  8.8 8.3 %collective-permute-start = (f32[576,128]{1,0:T(8,128)S(1)}, f32[576,128]{1,0:T(8,128)S(1)}, u32[]{:S(2)}, u32[]{:S(2)}) collective-permute-start(f32[576,128]{1,0:T(8,128)S(1)} %get-tuple-element.13.pay), channel_id=1, source_target_pairs={{0,1},{1,2},{2,3},{3,4},{4,5},{5,6},{6,7},{7,8},{8,9},{9,10},{10,1... | collective-permute-start | bytes 884744 | tf_op jit(solution)/shard_map/ppermute | solution.py:314
  8.8 0.7 %copy-start.3 = (f32[16]{0:T(128)S(1)}, f32[16]{0:T(128)}, u32[]{:S(2)}) copy-start(f32[16]{0:T(128)} %occ.1) | copy-start | bytes 196
  13.6 9.0 %copy-start.8 = (f32[8,16,13,13]{3,1,2,0:T(8,128)S(1)}, f32[8,16,13,13]{3,1,2,0:T(8,128)}, u32[]{:S(2)}) copy-start(f32[8,16,13,13]{3,1,2,0:T(8,128)} %constant.11.clone) | copy-start | bytes 259588
  13.6 9.0 %copy-start.9 = (f32[9,13,13]{2,1,0:T(8,128)S(1)}, f32[9,13,13]{2,1,0:T(8,128)}, u32[]{:S(2)}) copy-start(f32[9,13,13]{2,1,0:T(8,128)} %param.13) | copy-start | bytes 18256
  17.0 22.6 %copy-start.5 = (s32[8]{0:T(128)S(1)}, s32[8]{0:T(128)}, u32[]{:S(2)}) copy-start(s32[8]{0:T(128)} %sizes.1) | copy-start | bytes 100
  17.0 22.6 %copy-start.10 = (f32[8,9,512]{2,0,1:T(8,128)S(1)}, f32[8,9,512]{2,0,1:T(8,128)}, u32[]{:S(2)}) copy-start(f32[8,9,512]{2,0,1:T(8,128)} %param.12) | copy-start | bytes 442372
  21.1 28.5 %copy-start.2 = (s32[8,512]{1,0:T(8,128)S(1)}, s32[8,512]{1,0:T(8,128)}, u32[]{:S(2)}) copy-start(s32[8,512]{1,0:T(8,128)} %offsets.3) | copy-start | bytes 49156
  21.1 30.1 %copy-start.7 = (f32[8,16,13,13]{3,1,0,2:T(8,128)S(1)}, f32[8,16,13,13]{3,1,0,2:T(8,128)}, u32[]{:S(2)}) copy-start(f32[8,16,13,13]{3,1,0,2:T(8,128)} %constant.17) | copy-start | bytes 259588
  21.1 2.8 %collective-permute-start.2 = (f32[16,128]{1,0:T(8,128)S(1)}, f32[16,128]{1,0:T(8,128)S(1)}, u32[]{:S(2)}, u32[]{:S(2)}) collective-permute-start(f32[16,128]{1,0:T(8,128)S(1)} %get-tuple-element.15), channel_id=1, source_target_pairs={{1,0},{2,1},{3,2},{4,3},{5,4},{6,5},{7,6},{8,7},{9,8},{10,9},{11,1... | collective-permute-start | bytes 24584 | tf_op jit(solution)/shard_map/ppermute | solution.py:343
  22.6 5.2 %collective-permute-start.3 = (f32[16,128]{1,0:T(8,128)S(1)}, f32[16,128]{1,0:T(8,128)S(1)}, u32[]{:S(2)}, u32[]{:S(2)}) collective-permute-start(f32[16,128]{1,0:T(8,128)S(1)} %get-tuple-element.16), channel_id=1, source_target_pairs={{0,1},{1,2},{2,3},{3,4},{4,5},{5,6},{6,7},{7,8},{8,9},{9,10},{10,1... | collective-permute-start | bytes 24584 | tf_op jit(solution)/shard_map/ppermute | solution.py:344
  28.8 20.8 %all-to-all-start = ((f32[16,24,128]{2,1,0:T(8,128)}), f32[16,24,128]{2,1,0:T(8,128)S(1)}, u32[]{:S(2)}, u32[]{:S(2)}) async-start(f32[16,24,128]{2,1,0:T(8,128)} %partial_matrices.1), calls=%async_computation | async-start | bytes 393216 | tf_op jit(solution)/shard_map/all_to_all | solution.py:354
  50.6 2.4 %collective-permute-start.4 = (f32[8,256]{1,0:T(8,128)S(1)}, f32[8,256]{1,0:T(8,128)S(1)}, u32[]{:S(2)}, u32[]{:S(2)}) collective-permute-start(f32[8,256]{1,0:T(8,128)S(1)} %get-tuple-element.19), channel_id=1, source_target_pairs={{1,0},{2,1},{3,2},{4,3},{5,4},{6,5},{7,6},{8,7},{9,8},{10,9},{11,1... | collective-permute-start | bytes 24584 | tf_op jit(solution)/shard_map/ppermute | solution.py:374
  50.7 5.3 %collective-permute-start.5 = (f32[8,256]{1,0:T(8,128)S(1)}, f32[8,256]{1,0:T(8,128)S(1)}, u32[]{:S(2)}, u32[]{:S(2)}) collective-permute-start(f32[8,256]{1,0:T(8,128)S(1)} %get-tuple-element.20), channel_id=1, source_target_pairs={{0,1},{1,2},{2,3},{3,4},{4,5},{5,6},{6,7},{7,8},{8,9},{9,10},{10,1... | collective-permute-start | bytes 24584 | tf_op jit(solution)/shard_map/ppermute | solution.py:375

commit v4 on v3

--- a/solution.py
+++ b/solution.py
@@ -1,6 +1,5 @@
 import jax
 import jax.numpy as jnp
-import numpy as np
 from jax import lax
 from jax.experimental import pallas as pl
 from jax.experimental.pallas import tpu as pltpu
@@ -16,6 +15,7 @@
 BANDS = 16
 LANES = 128
 STEP = 32
+EARLY = 4
 LIST = 16
 TILES = SPHERE // LANES
 SORTED = TILES * ATOM_DEV * 16
@@ -25,6 +25,7 @@
 
 VM = pl.BlockSpec(memory_space=pltpu.VMEM)
 SM = pl.BlockSpec(memory_space=pltpu.SMEM)
+ANY = pl.BlockSpec(memory_space=pl.ANY)
 
 
 def params(limit=48 * 2**20):
@@ -42,13 +43,16 @@
     lax.fori_loop(first, last, body, 0)
 
 
-def project(pay, rows, shift, planes, begin, end):
+def project(pay, rows, shift, planes, begin, end, atoms=range(ATOM_DEV)):
     width = end - begin
     span = len(planes) * 16
     lane_plane = lax.broadcasted_iota(jnp.int32, (16, LANES), 1) % CZ
     sub = lax.broadcasted_iota(jnp.int32, (16, width), 0)
     parts = []
     for a in range(ATOM_DEV):
+        if a not in atoms:
+            parts.append(jnp.zeros((16, LANES), F32))
+            continue
         block = jnp.concatenate(
             [
                 pay[(t * ATOM_DEV + a) * 16 : (t * ATOM_DEV + a + 1) * 16, :]
@@ -90,7 +94,13 @@
         table[cols, :] = x[:, cols].T
 
 
-def sort_kernel(sizes, offsets, projectors, pay, lists):
+def sort_kernel(sizes_in, offsets_in, projectors_in, pay, lists, sizes, offsets, projectors, sems):
+    pairs = ((sizes_in, sizes), (offsets_in, offsets), (projectors_in, projectors))
+    copies = [pltpu.make_async_copy(a, b, sems.at[k]) for k, (a, b) in enumerate(pairs)]
+    for copy in copies:
+        copy.start()
+    for copy in copies:
+        copy.wait()
     sub = lax.broadcasted_iota(jnp.int32, (ATOM_DEV, SPHERE), 0)
     lane = lax.broadcasted_iota(jnp.int32, (ATOM_DEV, SPHERE), 1)
     size = jnp.zeros((ATOM_DEV, SPHERE), jnp.int32)
@@ -160,20 +170,29 @@
     return points[(k // LANES * LIST + row) * LANES + k % LANES]
 
 
-def own_kernel(lists, occ, x, table, pay, pseudo, q, rows):
+def own_points(atoms, lists, table, pay, rows):
     rows[...] = jnp.zeros_like(rows)
+    for a in atoms:
+        first = listed(lists, 8 + a, 0) // STEP
+        last = (listed(lists, 8 + a, SPHERE - 1) + (STEP - 1)) // STEP
+        gather_rows(lists, a, first, last, table, rows, a * SPHERE)
+    return project(pay, rows, -HALO, range(CZ), 0, SPHERE, atoms)
+
+
+def early_kernel(lists, table, pay, q, rows):
+    q[...] = own_points(range(EARLY), lists, table, pay, rows)
+
+
+def late_kernel(lists, occ, x, table, pay, after, packed, q, rows):
+    del after
     for c in range(PLANE // LANES):
         cols = slice(c * LANES, (c + 1) * LANES)
         acc = jnp.zeros((CZ, LANES), F32)
         for n in range(BANDS):
             v = x[n * CZ : (n + 1) * CZ, cols]
             acc = acc + occ[n] * (v * v)
-        pseudo[c // 2, (c % 2) * CZ : (c % 2 + 1) * CZ, :] = acc
-    for a in range(ATOM_DEV):
-        first = listed(lists, 8 + a, 0) // STEP
-        last = (listed(lists, 8 + a, SPHERE - 1) + (STEP - 1)) // STEP
-        gather_rows(lists, a, first, last, table, rows, a * SPHERE)
-    q[...] = project(pay, rows, -HALO, range(CZ), 0, SPHERE)
+        packed[c // 2, (c % 2) * CZ : (c % 2 + 1) * CZ, :] = acc
+    q[...] = own_points(range(EARLY, ATOM_DEV), lists, table, pay, rows)
 
 
 def side_kernel(list_lo, list_hi, table, pay_lo, pay_hi, q_lo, q_hi, rows):
@@ -209,8 +228,9 @@
         q_hi[...] = project(pay_hi, rows, CZ - HALO, range(CZ - HALO, CZ), 0, SPHERE)
 
 
-def matrix_kernel(q0, q1, q2, occ, pseudo, out):
-    proj = q0[...] + q1[...] + q2[...]
+def matrix_kernel(q0, q1, q2, q3, occ, packed, out, block, sem):
+    del packed
+    proj = q0[...] + q1[...] + q2[...] + q3[...]
     weighted = proj * occ[...]
     full = lax.dot_general(
         weighted, proj, (((0,), (0,)), ((), ())), precision=HIGHEST, preferred_element_type=F32
@@ -219,20 +239,18 @@
     acc = jnp.zeros((16, LANES), F32)
     for a in range(ATOM_DEV):
         acc = acc + jnp.where(lane_atom == a, full[a * 16 : (a + 1) * 16, :], 0.0)
-    i = lax.broadcasted_iota(jnp.int32, (8, LANES), 0)
-    j = lax.broadcasted_iota(jnp.int32, (8, LANES), 1) % 16
-    corner = pltpu.roll(pltpu.roll(acc[8:16], 1, 0), LANES - 8, 1)
-    packed = jnp.where(j < i, corner, acc[0:8])
     for b in range(16):
-        out[b, 0:16, :] = pseudo[b]
-        out[b, 16:24, :] = packed
+        block[b] = acc
+    copy = pltpu.make_async_copy(block, out.at[:, pl.ds(16, 16), :], sem)
+    copy.start()
+    copy.wait()
 
 
 def charge_kernel(start, recv, coupling, shapes, offsets, core, down, up, matrices):
     total = recv[0]
     for b in range(1, 16):
         total = total + recv[b]
-    matrix = total[16:24]
+    matrix = total[16:32]
     matrices[...] = matrix
     per_lane = jnp.concatenate(
         [jnp.sum(coupling[l] * matrix, axis=0, keepdims=True) for l in range(NL)], axis=0
@@ -276,15 +294,6 @@
     return jax.ShapeDtypeStruct(dims, F32)
 
 
-def packed_places():
-    places = {}
-    for i in range(NI):
-        for j in range(NI):
-            r, c = min(i, j), max(i, j)
-            places[i, j] = (r, c) if r < 8 else (c - 7, r - 8)
-    return places
-
-
 def local(orbitals, occupations, projectors, shapes, coupling, sphere_offsets, sphere_sizes):
     slabs = lax.axis_size("slab")
     to_next = [(i, (i + 1) % slabs) for i in range(slabs)]
@@ -305,25 +314,33 @@
             shape(SORTED + TILES * LIST, LANES),
             jax.ShapeDtypeStruct((TILES * LIST, LANES), jnp.int32),
         ),
-        in_specs=[SM, VM, VM],
+        in_specs=[ANY] * 3,
         out_specs=(VM, VM),
-        compiler_params=params(),
+        scratch_shapes=[
+            pltpu.SMEM((ATOM_DEV,), jnp.int32),
+            pltpu.VMEM((ATOM_DEV, SPHERE), jnp.int32),
+            pltpu.VMEM((NI, ATOM_DEV, SPHERE), F32),
+            pltpu.SemaphoreType.DMA((3,)),
+        ],
+        compiler_params=params(58 * 2**20),
         cost_estimate=pl.CostEstimate(flops=10**9, bytes_accessed=8 * 2**20, transcendentals=0),
         name="sort_points",
     )(sphere_sizes, sphere_offsets, projectors.transpose(1, 0, 2))
     pay_lo = lax.ppermute(pay, "slab", to_next)
     pay_hi = lax.ppermute(pay, "slab", to_prev)
 
-    pseudo, q_own = pl.pallas_call(
-        own_kernel,
-        out_shape=(shape(16, 16, LANES), shape(BANDS, LANES)),
-        in_specs=[SM, SM, VM, VM, VM],
-        out_specs=(VM, VM),
-        scratch_shapes=[pltpu.VMEM((ATOM_DEV * SPHERE, LANES), F32)],
-        compiler_params=params(),
-        cost_estimate=pl.CostEstimate(flops=2 * 10**9, bytes_accessed=12 * 2**20, transcendentals=0),
-        name="own_points",
-    )(lists.reshape(-1), occupations, grid_values, table, pay)
+    own_list = lists.reshape(-1)
+    scratch = [pltpu.VMEM((ATOM_DEV * SPHERE, LANES), F32)]
+    q_early = pl.pallas_call(
+        early_kernel,
+        out_shape=shape(BANDS, LANES),
+        in_specs=[SM, VM, VM],
+        out_specs=VM,
+        scratch_shapes=scratch,
+        compiler_params=params(),
+        cost_estimate=pl.CostEstimate(flops=10**9, bytes_accessed=8 * 2**20, transcendentals=0),
+        name="own_points_early",
+    )(own_list, table, pay)
 
     q_lo, q_hi = pl.pallas_call(
         side_kernel,
@@ -343,29 +360,44 @@
     back_hi = lax.ppermute(q_lo, "slab", to_prev)
     back_lo = lax.ppermute(q_hi, "slab", to_next)
 
+    packed, q_late = pl.pallas_call(
+        late_kernel,
+        out_shape=(shape(16, 32, LANES), shape(BANDS, LANES)),
+        in_specs=[SM, SM, VM, VM, VM, ANY],
+        out_specs=(VM, VM),
+        scratch_shapes=scratch,
+        compiler_params=params(),
+        cost_estimate=pl.CostEstimate(flops=10**9, bytes_accessed=8 * 2**20, transcendentals=0),
+        name="own_points_late",
+    )(own_list, occupations, grid_values, table, pay, q_lo)
+
     packed = pl.pallas_call(
         matrix_kernel,
-        out_shape=shape(16, 24, LANES),
-        in_specs=[VM] * 5,
-        out_specs=VM,
+        out_shape=shape(16, 32, LANES),
+        in_specs=[VM] * 5 + [ANY],
+        out_specs=ANY,
+        scratch_shapes=[pltpu.VMEM((16, 16, LANES), F32), pltpu.SemaphoreType.DMA],
+        input_output_aliases={5: 0},
         compiler_params=params(),
         name="partial_matrices",
-    )(q_own, back_hi, back_lo, jnp.broadcast_to(occupations[:, None], (BANDS, LANES)), pseudo)
+    )(
+        q_early,
+        q_late,
+        back_hi,
+        back_lo,
+        jnp.broadcast_to(occupations[:, None], (BANDS, LANES)),
+        packed,
+    )
     recv = lax.all_to_all(packed, "band", 0, 0)
 
-    places = packed_places()
-    unpack = np.zeros((8, 16, NI, NI), np.float32)
-    for (i, j), (p, q) in places.items():
-        unpack[p, q, i, j] = 1.0
-    coupling_packed = jnp.einsum("lij,pqij->lpq", coupling, unpack, precision=HIGHEST)
-    coupling_lanes = jnp.tile(coupling_packed, (1, 1, ATOM_DEV))
+    coupling_lanes = jnp.tile(jnp.pad(coupling, ((0, 0), (0, 3), (0, 3))), (1, 1, ATOM_DEV))
     live = jnp.arange(SPHERE, dtype=jnp.int32)[None, :] < sphere_sizes[:, None]
     shapes_live = jnp.where(live[:, None, :], shapes, 0.0).transpose(1, 0, 2)
     width = PLANE // lax.axis_size("band")
     start = (lax.axis_index("band") * width).astype(jnp.int32).reshape(1)
     core, down, up, matrices = pl.pallas_call(
         charge_kernel,
-        out_shape=(shape(CZ, 256), shape(CZ, 256), shape(CZ, 256), shape(8, LANES)),
+        out_shape=(shape(CZ, 256), shape(CZ, 256), shape(CZ, 256), shape(16, LANES)),
         in_specs=[SM, VM, VM, VM, VM],
         out_specs=(VM, VM, VM, VM),
         compiler_params=params(),
@@ -374,9 +406,7 @@
     from_above = lax.ppermute(down, "slab", to_prev)
     from_below = lax.ppermute(up, "slab", to_next)
     density = core + from_above + from_below
-    density_matrices = jnp.einsum(
-        "paq,pqij->aij", matrices.reshape(8, ATOM_DEV, 16), unpack, precision=HIGHEST
-    )
+    density_matrices = matrices.reshape(16, ATOM_DEV, 16)[:NI, :, :NI].transpose(1, 0, 2)
     return (density, density_matrices)
 
 

time: 56.6 us -> 55.6 us (0.982)
  Pallas kernels: 13 us -> 16.4 us
  matrix products: 2.5 us -> 0 us
  local copies, waits for them, and re-layouts: 2.95 us -> 1.43 us
  starting transfers between devices: 16.2 us -> 15.3 us
    dot_general x2 -> x0, matrix products: 2.5 us -> none  [the longest x1 1.7 us: local(): jnp.einsum('paq,pqij->aij', matrices.reshape(8, ATOM_DEV, 16), unpack, pr...]
    ppermute x1, waiting for transfers between devices: 3.82 us -> 1.37 us  [local(): back_lo = lax.ppermute(q_hi, 'slab', to_next)]
    unnamed x22 -> x16, local copies, waits for them, and re-layouts: 2.53 us -> 0.41 us
    pallas_call x2 -> x3, Pallas kernels: 5.14 us -> 6.94 us  [the longest x1 3.35 us: local(): pl.pallas_call(late_kernel, out_shape=(shape(16, 32, LANES), shape(BANDS,...]
    ppermute x1, starting transfers between devices: 1.42 us -> 0.01 us  [local(): back_hi = lax.ppermute(q_lo, 'slab', to_prev)]
    pallas_call x1, Pallas kernels: 2.21 us -> 3.51 us  [local(): pl.pallas_call(sort_kernel, out_shape=(shape(SORTED + TILES * LIST, LANES...]
    ppermute x1, waiting for transfers between devices: 2.99 us -> 3.9 us  [local(): from_below = lax.ppermute(up, 'slab', to_next)]
    ppermute x1, waiting for transfers between devices: 0.03 us -> 0.92 us  [local(): pay_hi = lax.ppermute(pay, 'slab', to_prev)]
  transfers between devices with their start and end apart: 7 -> 7, of which waited for: 5 -> 6; matrix products, arithmetic and copies ran while one was open for 5% -> 2% of each run, Pallas kernels for 8% -> 12%
where the time goes in v4:
time: 55.6 us; the launch traced here: 55.5 us
  waiting for transfers between devices  20.8 us (37%)
  Pallas kernels  16.4 us (29%)
  starting transfers between devices  15.3 us (28%)
  local copies, waits for them, and re-layouts  1.43 us (3%)
  between operations  0.76 us (1%)
  other arithmetic  0.7 us (1%)
    all_to_all x1, starting transfers between devices, local(): recv = lax.all_to_all(packed, 'band', 0, 0)  10.8 us
    all_to_all x1, waiting for transfers between devices, local(): recv = lax.all_to_all(packed, 'band', 0, 0)  10.5 us
    pallas_call x1, Pallas kernels, local(): pl.pallas_call(side_kernel, out_shape=(shape(BANDS, LANES), shape(BANDS,...  4.38 us
    ppermute x1, waiting for transfers between devices, local(): pay_lo = lax.ppermute(pay, 'slab', to_next)  3.9 us
    ppermute x1, waiting for transfers between devices, local(): from_below = lax.ppermute(up, 'slab', to_next)  3.9 us
    pallas_call x1, Pallas kernels, local(): pl.pallas_call(sort_kernel, out_shape=(shape(SORTED + TILES * LIST, LANES...  3.51 us
    ppermute x1, starting transfers between devices, local(): pay_hi = lax.ppermute(pay, 'slab', to_prev)  3.46 us
    pallas_call x1, Pallas kernels, local(): pl.pallas_call(late_kernel, out_shape=(shape(16, 32, LANES), shape(BANDS,...  3.35 us
  transfers between devices with their start and end apart: 7, of which 6 were waited for; matrix products, arithmetic and copies ran while one was open for 2% of the time, Pallas kernels for 12%

profile of v4, /device:TPU:32, one launch (start us, length us, event | category | flops | bytes accessed | tf_op | source)
XLA Modules:
  0.0 55.5 jit_solution(18067045039419267736)
XLA Ops:
  0.6 0.0 copy-start
  0.6 3.5 %sort_points.1 = (f32[576,128]{1,0:T(8,128)}, s32[64,128]{1,0:T(8,128)}) custom-call(s32[8]{0:T(128)} %sizes_in.1, s32[8,512]{1,0:T(8,128)} %offsets.1, f32[13,8,512]{2,1,0:T(8,128)} %bitcast.18), custom_call_target="tpu_custom_call" | custom-call | flops 1000000000 | bytes 8388608 | tf_op jit(solution)/shard_map/sort_points/pallas_call | solution.py:311
  4.2 3.5 %collective-permute-start.1 = (f32[576,128]{1,0:T(8,128)}, f32[576,128]{1,0:T(8,128)S(1)}, u32[]{:S(2)}, u32[]{:S(2)}) collective-permute-start(f32[576,128]{1,0:T(8,128)} %get-tuple-element.13.pay), channel_id=1, source_target_pairs={{1,0},{2,1},{3,2},{4,3},{5,4},{6,5},{7,6},{8,7},{9,8},{10,9},{11,1... | collective-permute-start | bytes 884744 | tf_op jit(solution)/shard_map/ppermute | solution.py:330
  7.6 0.0 collective-permute-start
  7.6 0.0 copy-done
  7.6 0.0 copy-start.1
  7.6 0.0 copy-start.2
  7.6 0.6 %grid_table.1.table = f32[4096,128]{1,0:T(8,128)S(1)} custom-call(f32[128,4096]{1,0:T(8,128)S(1)} %bitcast.14), custom_call_target="tpu_custom_call" | custom-call | bytes 8388608 | tf_op jit(solution)/shard_map/grid_table/pallas_call | solution.py:302
  8.2 0.4 copy-done.1
  8.6 0.0 copy-done.2
  8.6 2.6 %own_points_early.1.q0 = f32[16,128]{1,0:T(8,128)S(1)} custom-call(s32[8192]{0:T(1024)S(1)} %bitcast.16, f32[4096,128]{1,0:T(8,128)S(1)} %grid_table.1.table, f32[576,128]{1,0:T(8,128)S(1)} %copy-done.1), custom_call_target="tpu_custom_call" | custom-call | flops 1000000000 | bytes 8388608 | tf_op jit(solution)/shard_map/own_points_early/pallas_call | solution.py:334
  11.2 0.0 copy-start.4
  11.3 0.9 %collective-permute-done.1.pay_hi = f32[576,128]{1,0:T(8,128)S(1)} collective-permute-done((f32[576,128]{1,0:T(8,128)}, f32[576,128]{1,0:T(8,128)S(1)}, u32[]{:S(2)}, u32[]{:S(2)}) %collective-permute-start.1) | collective-permute-done | bytes 294944 | tf_op jit(solution)/shard_map/ppermute | solution.py:330
  12.2 3.9 %collective-permute-done.pay_lo = f32[576,128]{1,0:T(8,128)S(1)} collective-permute-done((f32[576,128]{1,0:T(8,128)}, f32[576,128]{1,0:T(8,128)S(1)}, u32[]{:S(2)}, u32[]{:S(2)}) %collective-permute-start) | collective-permute-done | bytes 294944 | tf_op jit(solution)/shard_map/ppermute | solution.py:329
  16.1 4.4 %side_points.1 = (f32[16,128]{1,0:T(8,128)S(1)}, f32[16,128]{1,0:T(8,128)S(1)}) custom-call(s32[8192]{0:T(1024)S(1)} %fusion.1.list_lo, s32[8192]{0:T(1024)S(1)} %fusion.list_hi, f32[4096,128]{1,0:T(8,128)S(1)} %grid_table.1.table, f32[576,128]{1,0:T(8,128)S(1)} %collective-permute-done.pay_lo, f32[576,128]{1,0:T(8,128)S(1)} %collective-permute-done.1.pay_hi), custom_call_target="tpu_custom_call" | custom-call | tf_op jit(solution)/shard_map/side_points/pallas_call | solution.py:345
  20.5 0.0 collective-permute-start.2
  20.5 0.0 copy-start.6
  20.5 0.5 collective-permute-start.3
  21.0 0.0 copy-done.4
  21.0 3.3 %own_points_late.1 = (f32[16,32,128]{2,1,0:T(8,128)}, f32[16,128]{1,0:T(8,128)S(1)}) custom-call(s32[8192]{0:T(1024)S(1)} %bitcast.17, f32[16]{0:T(128)S(1)} %copy-done.4, f32[128,4096]{1,0:T(8,128)S(1)} %bitcast.15, f32[4096,128]{1,0:T(8,128)S(1)} %grid_table.1.table, f32[576,128]{1,0:T(8,128)S(1)} %copy-done.1, f32[16,128]{1,0:T(8,128)S(1)} %get-tuple-element.14.after), custom_call_target="tpu_custom_call" | custom-call | flops 1000000000 | bytes 8388608 | tf_op jit(solution)/shard_map/own_points_late/pallas_call | solution.py:363
  24.4 0.0 copy-start.7
  24.4 0.0 copy-start.5
  24.4 0.0 copy-start.3
  24.4 0.0 collective-permute-done.2.q2
  24.4 1.4 %collective-permute-done.3.q3 = f32[16,128]{1,0:T(8,128)S(1)} collective-permute-done((f32[16,128]{1,0:T(8,128)S(1)}, f32[16,128]{1,0:T(8,128)S(1)}, u32[]{:S(2)}, u32[]{:S(2)}) %collective-permute-start.3) | collective-permute-done | bytes 8224 | tf_op jit(solution)/shard_map/ppermute | solution.py:361
  25.7 0.1 broadcast_in_dim.10.occ
  25.8 1.0 %partial_matrices.1 = f32[16,32,128]{2,1,0:T(8,128)} custom-call(f32[16,128]{1,0:T(8,128)S(1)} %own_points_early.1.q0, f32[16,128]{1,0:T(8,128)S(1)} %get-tuple-element.15.q1, f32[16,128]{1,0:T(8,128)S(1)} %collective-permute-done.2.q2, f32[16,128]{1,0:T(8,128)S(1)} %collective-permute-done.3.q3, ...), custom_call_target="tpu_custom_call", output_to_operand_aliasing={{}: (5, {})} | custom-call | tf_op jit(solution)/shard_map/partial_matrices/pallas_call | solution.py:374
  26.8 10.8 %all-to-all-start = ((f32[16,32,128]{2,1,0:T(8,128)}), f32[16,32,128]{2,1,0:T(8,128)S(1)}, u32[]{:S(2)}, u32[]{:S(2)}) async-start(f32[16,32,128]{2,1,0:T(8,128)} %partial_matrices.1), calls=%async_computation | async-start | bytes 524288 | tf_op jit(solution)/shard_map/all_to_all | solution.py:391
  37.5 0.0 copy-done.6
  37.6 0.2 tile.10.coupling
  37.8 0.0 copy-done.7
  37.8 0.1 iota_compare_fusion
  37.9 0.0 copy-done.5
  37.9 10.5 %all-to-all-done.recv = f32[16,32,128]{2,1,0:T(8,128)S(1)} async-done(((f32[16,32,128]{2,1,0:T(8,128)}), f32[16,32,128]{2,1,0:T(8,128)S(1)}, u32[]{:S(2)}, u32[]{:S(2)}) %all-to-all-start) | async-done | bytes 262176 | tf_op jit(solution)/shard_map/all_to_all | solution.py:391
  48.4 0.0 copy-done.3
  48.5 1.0 %charges.1 = (f32[8,256]{1,0:T(8,128)S(1)}, f32[8,256]{1,0:T(8,128)S(1)}, f32[8,256]{1,0:T(8,128)S(1)}, f32[16,128]{1,0:T(8,128)S(1)}) custom-call(s32[1]{0:T(128)} %bitcast.start, f32[16,32,128]{2,1,0:T(8,128)S(1)} %all-to-all-done.recv, f32[9,16,128]{2,1,0:T(8,128)S(1)} %tile.10.coupling, f32[9,8,512]{2,1,0:T(8,128)S(1)} %select_bitcast_fusion.shapes, ...), custom_call_target="tpu_custom_call" | custom-call | tf_op jit(solution)/shard_map/charges/pallas_call | solution.py:398
  49.4 0.1 reshape.49
  49.5 0.1 collective-permute-start.4
  49.6 0.5 collective-permute-start.5
  50.1 0.6 %slice_bitcast_fusion = f32[8,13,13]{2,0,1:T(8,128)} fusion(f32[16,8,16]{2,1,0:T(8,128)S(1)} %reshape.49), kind=kLoop, calls=%fused_computation.1 | loop fusion | bytes 10816 | tf_op jit(solution)/shard_map/transpose | solution.py:409
  50.7 0.2 collective-permute-done.4
  50.9 3.9 %collective-permute-done.5 = f32[8,256]{1,0:T(8,128)S(1)} collective-permute-done((f32[8,256]{1,0:T(8,128)S(1)}, f32[8,256]{1,0:T(8,128)S(1)}, u32[]{:S(2)}, u32[]{:S(2)}) %collective-permute-start.5) | collective-permute-done | bytes 8224 | tf_op jit(solution)/shard_map/ppermute | solution.py:407
  54.9 0.6 %add_add_fusion = f32[8,256]{1,0:T(8,128)} fusion(f32[8,256]{1,0:T(8,128)S(1)} %collective-permute-done.5, f32[8,256]{1,0:T(8,128)S(1)} %get-tuple-element.18, f32[8,256]{1,0:T(8,128)S(1)} %collective-permute-done.4), kind=kLoop, calls=%fused_computation.7 | loop fusion | flops 4096 | bytes 32768 | tf_op jit(solution)/shard_map/add | solution.py:408
  (5 shorter events, 0.1 us)
Async XLA Ops:
  0.6 7.0 %copy-start = (f32[16,8,4096]{2,1,0:T(8,128)S(1)}, f32[16,8,4096]{2,1,0:T(8,128)}, u32[]{:S(2)}) copy-start(f32[16,8,4096]{2,1,0:T(8,128)} %param.7) | copy-start | bytes 6291460
  4.2 8.0 %collective-permute-start.1 = (f32[576,128]{1,0:T(8,128)}, f32[576,128]{1,0:T(8,128)S(1)}, u32[]{:S(2)}, u32[]{:S(2)}) collective-permute-start(f32[576,128]{1,0:T(8,128)} %get-tuple-element.13.pay), channel_id=1, source_target_pairs={{1,0},{2,1},{3,2},{4,3},{5,4},{6,5},{7,6},{8,7},{9,8},{10,9},{11,1... | collective-permute-start | bytes 884744 | tf_op jit(solution)/shard_map/ppermute | solution.py:330
  7.6 8.5 %collective-permute-start = (f32[576,128]{1,0:T(8,128)}, f32[576,128]{1,0:T(8,128)S(1)}, u32[]{:S(2)}, u32[]{:S(2)}) collective-permute-start(f32[576,128]{1,0:T(8,128)} %get-tuple-element.13.pay), channel_id=1, source_target_pairs={{0,1},{1,2},{2,3},{3,4},{4,5},{5,6},{6,7},{7,8},{8,9},{9,10},{10,1... | collective-permute-start | bytes 884744 | tf_op jit(solution)/shard_map/ppermute | solution.py:329
  7.6 1.0 %copy-start.1 = (f32[576,128]{1,0:T(8,128)S(1)}, f32[576,128]{1,0:T(8,128)}, u32[]{:S(2)}) copy-start(f32[576,128]{1,0:T(8,128)} %get-tuple-element.13.pay) | copy-start | bytes 884740
  7.6 1.0 %copy-start.2 = (s32[64,128]{1,0:T(8,128)S(1)}, s32[64,128]{1,0:T(8,128)}, u32[]{:S(2)}) copy-start(s32[64,128]{1,0:T(8,128)} %get-tuple-element.12) | copy-start | bytes 98308
  11.2 9.8 %copy-start.4 = (f32[16]{0:T(128)S(1)}, f32[16]{0:T(128)}, u32[]{:S(2)}) copy-start(f32[16]{0:T(128)} %occ.1) | copy-start | bytes 196
  20.5 3.9 %collective-permute-start.2 = (f32[16,128]{1,0:T(8,128)S(1)}, f32[16,128]{1,0:T(8,128)S(1)}, u32[]{:S(2)}, u32[]{:S(2)}) collective-permute-start(f32[16,128]{1,0:T(8,128)S(1)} %get-tuple-element.14.after), channel_id=1, source_target_pairs={{1,0},{2,1},{3,2},{4,3},{5,4},{6,5},{7,6},{8,7},{9,8},{10,9},{11,1... | collective-permute-start | bytes 24584 | tf_op jit(solution)/shard_map/ppermute | solution.py:360
  20.5 17.1 %copy-start.6 = (f32[9,13,13]{2,1,0:T(8,128)S(1)}, f32[9,13,13]{2,1,0:T(8,128)}, u32[]{:S(2)}) copy-start(f32[9,13,13]{2,1,0:T(8,128)} %param.11) | copy-start | bytes 18256
  20.5 5.3 %collective-permute-start.3 = (f32[16,128]{1,0:T(8,128)S(1)}, f32[16,128]{1,0:T(8,128)S(1)}, u32[]{:S(2)}, u32[]{:S(2)}) collective-permute-start(f32[16,128]{1,0:T(8,128)S(1)} %get-tuple-element.16), channel_id=1, source_target_pairs={{0,1},{1,2},{2,3},{3,4},{4,5},{5,6},{6,7},{7,8},{8,9},{9,10},{10,1... | collective-permute-start | bytes 24584 | tf_op jit(solution)/shard_map/ppermute | solution.py:361
  24.4 13.5 %copy-start.7 = (s32[8]{0:T(128)S(1)}, s32[8]{0:T(128)}, u32[]{:S(2)}) copy-start(s32[8]{0:T(128)} %sizes_in.1) | copy-start | bytes 100
  24.4 13.5 %copy-start.5 = (f32[8,9,512]{2,0,1:T(8,128)S(1)}, f32[8,9,512]{2,0,1:T(8,128)}, u32[]{:S(2)}) copy-start(f32[8,9,512]{2,0,1:T(8,128)} %param.10) | copy-start | bytes 442372
  24.4 24.1 %copy-start.3 = (s32[8,512]{1,0:T(8,128)S(1)}, s32[8,512]{1,0:T(8,128)}, u32[]{:S(2)}) copy-start(s32[8,512]{1,0:T(8,128)} %offsets.1) | copy-start | bytes 49156
  26.8 21.7 %all-to-all-start = ((f32[16,32,128]{2,1,0:T(8,128)}), f32[16,32,128]{2,1,0:T(8,128)S(1)}, u32[]{:S(2)}, u32[]{:S(2)}) async-start(f32[16,32,128]{2,1,0:T(8,128)} %partial_matrices.1), calls=%async_computation | async-start | bytes 524288 | tf_op jit(solution)/shard_map/all_to_all | solution.py:391
  49.5 1.5 %collective-permute-start.4 = (f32[8,256]{1,0:T(8,128)S(1)}, f32[8,256]{1,0:T(8,128)S(1)}, u32[]{:S(2)}, u32[]{:S(2)}) collective-permute-start(f32[8,256]{1,0:T(8,128)S(1)} %get-tuple-element.19), channel_id=1, source_target_pairs={{1,0},{2,1},{3,2},{4,3},{5,4},{6,5},{7,6},{8,7},{9,8},{10,9},{11,1... | collective-permute-start | bytes 24584 | tf_op jit(solution)/shard_map/ppermute | solution.py:406
  49.6 5.3 %collective-permute-start.5 = (f32[8,256]{1,0:T(8,128)S(1)}, f32[8,256]{1,0:T(8,128)S(1)}, u32[]{:S(2)}, u32[]{:S(2)}) collective-permute-start(f32[8,256]{1,0:T(8,128)S(1)} %get-tuple-element.20), channel_id=1, source_target_pairs={{0,1},{1,2},{2,3},{3,4},{4,5},{5,6},{6,7},{7,8},{8,9},{9,10},{10,1... | collective-permute-start | bytes 24584 | tf_op jit(solution)/shard_map/ppermute | solution.py:407

commit v5 on v4

--- a/solution.py
+++ b/solution.py
@@ -14,11 +14,11 @@
 NL = 9
 BANDS = 16
 LANES = 128
-STEP = 32
 EARLY = 4
-LIST = 16
 TILES = SPHERE // LANES
+WORDS = SPHERE // 2
 SORTED = TILES * ATOM_DEV * 16
+LIST = WORDS // LANES * ATOM_DEV + ATOM_DEV
 HIGHEST = lax.Precision.HIGHEST
 F32 = jnp.float32
 BF16 = jnp.bfloat16
@@ -32,19 +32,28 @@
     return pltpu.CompilerParams(vmem_limit_bytes=limit)
 
 
-def gather_rows(points, row, first, last, table, rows, base):
-    def body(step, carry):
-        k = pl.multiple_of(step * STEP, STEP)
-        at = (step >> 2) * (LIST * LANES) + row * LANES + (step & 3) * STEP
-        for u in range(STEP):
-            rows[pl.ds(base + k + u, 1), :] = table[pl.ds(points[at + u], 1), :]
+def gather_rows(points, atom, first, last, step, table, rows):
+    base = atom * SPHERE
+
+    def body(s, carry):
+        i = pl.multiple_of(s * step, step)
+        at = (i >> 7) * (ATOM_DEV * LANES) + atom * LANES + (i & (LANES - 1))
+        for u in range(step):
+            word = points[at + u]
+            rows[pl.ds(base + i + u, 1), :] = table[pl.ds(word & (PLANE - 1), 1), :]
+            rows[pl.ds(base + WORDS + i + u, 1), :] = table[pl.ds(word >> 12, 1), :]
         return carry
 
     lax.fori_loop(first, last, body, 0)
 
 
-def project(pay, rows, shift, planes, begin, end, atoms=range(ATOM_DEV)):
-    width = end - begin
+def counts(points, atom):
+    at = WORDS * ATOM_DEV + atom * LANES
+    return points[at], points[at + LANES - 1]
+
+
+def project(pay, rows, shift, planes, tiles, atoms=range(ATOM_DEV)):
+    width = len(tiles) * LANES
     span = len(planes) * 16
     lane_plane = lax.broadcasted_iota(jnp.int32, (16, LANES), 1) % CZ
     sub = lax.broadcasted_iota(jnp.int32, (16, width), 0)
@@ -54,11 +63,7 @@
             parts.append(jnp.zeros((16, LANES), F32))
             continue
         block = jnp.concatenate(
-            [
-                pay[(t * ATOM_DEV + a) * 16 : (t * ATOM_DEV + a + 1) * 16, :]
-                for t in range(begin // LANES, end // LANES)
-            ],
-            axis=1,
+            [pay[(a * TILES + t) * 16 : (a * TILES + t + 1) * 16, :] for t in tiles], axis=1
         )
         plane = block[15:16, :].astype(jnp.int32) + shift
         proj = jnp.where(sub < NI, block, 0.0)
@@ -69,7 +74,9 @@
             for z in planes:
                 pieces.append(jnp.where(plane == z, piece, 0.0))
         left = jnp.concatenate(pieces, axis=0).astype(BF16)
-        gathered = rows[a * SPHERE + begin : a * SPHERE + end, :]
+        gathered = jnp.concatenate(
+            [rows[a * SPHERE + t * LANES : a * SPHERE + (t + 1) * LANES, :] for t in tiles], axis=0
+        )
         g_high = gathered.astype(BF16)
         g_low = (gathered - g_high.astype(F32)).astype(BF16)
         first = jnp.dot(left, g_high, preferred_element_type=F32)
@@ -94,15 +101,20 @@
         table[cols, :] = x[:, cols].T
 
 
-def sort_kernel(sizes_in, offsets_in, projectors_in, pay, lists, sizes, offsets, projectors, sems):
+def sort_kernel(
+    sizes_in, offsets_in, projectors_in, pay_out, lists, pay, sizes, offsets, projectors, sems
+):
     pairs = ((sizes_in, sizes), (offsets_in, offsets), (projectors_in, projectors))
     copies = [pltpu.make_async_copy(a, b, sems.at[k]) for k, (a, b) in enumerate(pairs)]
     for copy in copies:
         copy.start()
-    for copy in copies:
-        copy.wait()
+    before = lax.broadcasted_iota(jnp.int32, (SPHERE, SPHERE), 0)
+    after = lax.broadcasted_iota(jnp.int32, (SPHERE, SPHERE), 1)
+    until = jnp.where(before <= after, 1.0, 0.0).astype(BF16)
     sub = lax.broadcasted_iota(jnp.int32, (ATOM_DEV, SPHERE), 0)
     lane = lax.broadcasted_iota(jnp.int32, (ATOM_DEV, SPHERE), 1)
+    copies[0].wait()
+    copies[1].wait()
     size = jnp.zeros((ATOM_DEV, SPHERE), jnp.int32)
     for a in range(ATOM_DEV):
         size = jnp.where(sub == a, sizes[a], size)
@@ -117,9 +129,6 @@
         [jnp.where(m, 1.0, 0.0) for m in (below, own, above)] + [jnp.zeros((8, SPHERE), F32)],
         axis=0,
     ).astype(BF16)
-    before = lax.broadcasted_iota(jnp.int32, (SPHERE, SPHERE), 0)
-    after = lax.broadcasted_iota(jnp.int32, (SPHERE, SPHERE), 1)
-    until = jnp.where(before <= after, 1.0, 0.0).astype(BF16)
     rank = jnp.dot(flags, until, preferred_element_type=F32).astype(jnp.int32)
     n_below = jnp.max(rank[0:8], axis=1, keepdims=True)
     n_own = jnp.max(rank[8:16], axis=1, keepdims=True)
@@ -127,8 +136,10 @@
     place = jnp.where(
         below,
         rank[0:8] - 1,
-        jnp.where(own, n_below + rank[8:16] - 1, jnp.where(above, SPHERE - rank[16:24], -1)),
-    )
+        jnp.where(own, n_below + rank[8:16] - 1, SPHERE - rank[16:24]),
+    )
+    place = jnp.where(live, (place >> 1) + (place & 1) * WORDS, -1)
+    copies[2].wait()
     table = jnp.concatenate(
         [
             projectors[...],
@@ -140,6 +151,7 @@
     )
     table = jnp.transpose(table, (1, 0, 2))
     points = []
+    sent = []
     for a in range(ATOM_DEV):
         high = table[a].astype(BF16)
         low = (table[a] - high.astype(F32)).astype(BF16)
@@ -151,32 +163,40 @@
             preferred_element_type=F32,
         )
         moved = moved[0:16] + moved[16:32]
+        first = a * TILES * 16
         for t in range(TILES):
-            first = (t * ATOM_DEV + a) * 16
-            pay[first : first + 16, :] = moved[:, t * LANES : (t + 1) * LANES]
+            pay[first + t * 16 : first + (t + 1) * 16, :] = moved[:, t * LANES : (t + 1) * LANES]
+        block = pl.ds(first, TILES * 16)
+        sent.append(pltpu.make_async_copy(pay.at[block], pay_out.at[block], sems.at[3 + a]))
+        sent[-1].start()
         points.append(moved[13:14] * 64.0 + moved[14:15])
     points = jnp.concatenate(points, axis=0)
-    counts = jnp.where(lane < SPHERE // 2, n_below, n_above).astype(F32)
-    ends = jnp.where(lane < SPHERE // 2, n_below, n_below + n_own)
-    for t in range(TILES):
-        cols = slice(t * LANES, (t + 1) * LANES)
-        for k, (sent, kept) in enumerate(((points, points.astype(jnp.int32)), (counts, ends))):
-            first = t * LIST + k * ATOM_DEV
-            pay[SORTED + first : SORTED + first + ATOM_DEV, :] = sent[:, cols]
-            lists[first : first + ATOM_DEV, :] = kept[:, cols]
-
-
-def listed(points, row, k):
-    return points[(k // LANES * LIST + row) * LANES + k % LANES]
+    words = points[:, :WORDS] + points[:, WORDS:] * float(PLANE)
+    for t in range(WORDS // LANES):
+        part = words[:, t * LANES : (t + 1) * LANES]
+        at = t * ATOM_DEV
+        pay[SORTED + at : SORTED + at + ATOM_DEV, :] = part
+        lists[at : at + ATOM_DEV, :] = part.astype(jnp.int32)
+    at = LIST - ATOM_DEV
+    lead = lane[:, :LANES] < LANES // 2
+    pay[SORTED + at : SORTED + LIST, :] = jnp.where(lead, n_below, n_above).astype(F32)
+    lists[at:LIST, :] = jnp.where(lead, n_below, n_below + n_own)
+    block = pl.ds(SORTED, LIST)
+    sent.append(pltpu.make_async_copy(pay.at[block], pay_out.at[block], sems.at[3 + ATOM_DEV]))
+    sent[-1].start()
+    for copy in sent:
+        copy.wait()
 
 
 def own_points(atoms, lists, table, pay, rows):
     rows[...] = jnp.zeros_like(rows)
+    step = 16
     for a in atoms:
-        first = listed(lists, 8 + a, 0) // STEP
-        last = (listed(lists, 8 + a, SPHERE - 1) + (STEP - 1)) // STEP
-        gather_rows(lists, a, first, last, table, rows, a * SPHERE)
-    return project(pay, rows, -HALO, range(CZ), 0, SPHERE, atoms)
+        begin, end = counts(lists, a)
+        first = begin // (2 * step)
+        last = (end + (2 * step - 1)) // (2 * step)
+        gather_rows(lists, a, first, last, step, table, rows)
+    return project(pay, rows, -HALO, range(CZ), range(TILES), atoms)
 
 
 def early_kernel(lists, table, pay, q, rows):
@@ -197,35 +217,36 @@
 
 def side_kernel(list_lo, list_hi, table, pay_lo, pay_hi, q_lo, q_hi, rows):
     rows[...] = jnp.zeros_like(rows)
-    half = SPHERE // 2
+    step = 8
     most = jnp.int32(0)
     for a in range(ATOM_DEV):
-        most = jnp.maximum(most, listed(list_lo, 8 + a, SPHERE - 1))
-        most = jnp.maximum(most, listed(list_hi, 8 + a, 0))
+        most = jnp.maximum(most, jnp.maximum(counts(list_lo, a)[1], counts(list_hi, a)[0]))
 
     def from_below():
         for a in range(ATOM_DEV):
-            first = (SPHERE - listed(list_lo, 8 + a, SPHERE - 1)) // STEP
-            gather_rows(list_lo, a, first, SPHERE // STEP, table, rows, a * SPHERE)
+            first = (SPHERE - counts(list_lo, a)[1]) // (2 * step)
+            gather_rows(list_lo, a, first, WORDS // step, step, table, rows)
 
     def from_above():
         for a in range(ATOM_DEV):
-            last = (listed(list_hi, 8 + a, 0) + (STEP - 1)) // STEP
-            gather_rows(list_hi, a, 0, last, table, rows, a * SPHERE)
-
-    @pl.when(most <= half)
+            last = (counts(list_hi, a)[0] + (2 * step - 1)) // (2 * step)
+            gather_rows(list_hi, a, 0, last, step, table, rows)
+
+    low, high = range(HALO), range(CZ - HALO, CZ)
+
+    @pl.when(most <= WORDS)
     def _():
         from_below()
         from_above()
-        q_lo[...] = project(pay_lo, rows, -HALO - CZ, range(HALO), half, SPHERE)
-        q_hi[...] = project(pay_hi, rows, CZ - HALO, range(CZ - HALO, CZ), 0, half)
-
-    @pl.when(most > half)
+        q_lo[...] = project(pay_lo, rows, -HALO - CZ, low, (1, 3))
+        q_hi[...] = project(pay_hi, rows, CZ - HALO, high, (0, 2))
+
+    @pl.when(most > WORDS)
     def _():
         from_below()
-        q_lo[...] = project(pay_lo, rows, -HALO - CZ, range(HALO), 0, SPHERE)
+        q_lo[...] = project(pay_lo, rows, -HALO - CZ, low, range(TILES))
         from_above()
-        q_hi[...] = project(pay_hi, rows, CZ - HALO, range(CZ - HALO, CZ), 0, SPHERE)
+        q_hi[...] = project(pay_hi, rows, CZ - HALO, high, range(TILES))
 
 
 def matrix_kernel(q0, q1, q2, q3, occ, packed, out, block, sem):
@@ -311,16 +332,17 @@
     pay, lists = pl.pallas_call(
         sort_kernel,
         out_shape=(
-            shape(SORTED + TILES * LIST, LANES),
-            jax.ShapeDtypeStruct((TILES * LIST, LANES), jnp.int32),
+            shape(SORTED + LIST, LANES),
+            jax.ShapeDtypeStruct((LIST, LANES), jnp.int32),
         ),
         in_specs=[ANY] * 3,
-        out_specs=(VM, VM),
+        out_specs=(ANY, VM),
         scratch_shapes=[
+            pltpu.VMEM((SORTED + LIST, LANES), F32),
             pltpu.SMEM((ATOM_DEV,), jnp.int32),
             pltpu.VMEM((ATOM_DEV, SPHERE), jnp.int32),
             pltpu.VMEM((NI, ATOM_DEV, SPHERE), F32),
-            pltpu.SemaphoreType.DMA((3,)),
+            pltpu.SemaphoreType.DMA((4 + ATOM_DEV,)),
         ],
         compiler_params=params(58 * 2**20),
         cost_estimate=pl.CostEstimate(flops=10**9, bytes_accessed=8 * 2**20, transcendentals=0),

time: 55.6 us -> 55.4 us (level)
  Pallas kernels: 16.4 us -> 15.7 us
    ppermute x1, waiting for transfers between devices: 1.37 us -> 2.05 us  [local(): back_lo = lax.ppermute(q_hi, 'slab', to_next)]
  transfers between devices with their start and end apart: 7 -> 7, of which waited for: 6 -> 6; matrix products, arithmetic and copies ran while one was open for 2% -> 2% of each run, Pallas kernels for 12% -> 11%
where the time goes in v5:
time: 55.4 us; the launch traced here: 55.1 us
  waiting for transfers between devices  21.2 us (38%)
  Pallas kernels  15.7 us (28%)
  starting transfers between devices  15.3 us (28%)
  local copies, waits for them, and re-layouts  1.42 us (3%)
  between operations  0.75 us (1%)
  other arithmetic  0.7 us (1%)
    all_to_all x1, starting transfers between devices, local(): recv = lax.all_to_all(packed, 'band', 0, 0)  10.8 us
    all_to_all x1, waiting for transfers between devices, local(): recv = lax.all_to_all(packed, 'band', 0, 0)  10.2 us
    ppermute x1, waiting for transfers between devices, local(): pay_lo = lax.ppermute(pay, 'slab', to_next)  3.91 us
    ppermute x1, waiting for transfers between devices, local(): from_below = lax.ppermute(up, 'slab', to_next)  3.9 us
    pallas_call x1, Pallas kernels, local(): pl.pallas_call(side_kernel, out_shape=(shape(BANDS, LANES), shape(BANDS,...  3.89 us
    pallas_call x1, Pallas kernels, local(): pl.pallas_call(sort_kernel, out_shape=(shape(SORTED + LIST, LANES), jax.S...  3.87 us
    ppermute x1, starting transfers between devices, local(): pay_hi = lax.ppermute(pay, 'slab', to_prev)  3.46 us
    pallas_call x1, Pallas kernels, local(): pl.pallas_call(late_kernel, out_shape=(shape(16, 32, LANES), shape(BANDS,...  3.05 us
  transfers between devices with their start and end apart: 7, of which 6 were waited for; matrix products, arithmetic and copies ran while one was open for 2% of the time, Pallas kernels for 11%

profile of v5, /device:TPU:32, one launch (start us, length us, event | category | flops | bytes accessed | tf_op | source)
XLA Modules:
  0.0 55.1 jit_solution(5222346482343806754)
XLA Ops:
  0.6 0.0 copy-start
  0.6 3.9 %sort_points.1 = (f32[536,128]{1,0:T(8,128)}, s32[24,128]{1,0:T(8,128)}) custom-call(s32[8]{0:T(128)} %sizes_in.1, s32[8,512]{1,0:T(8,128)} %offsets.1, f32[13,8,512]{2,1,0:T(8,128)} %bitcast.18), custom_call_target="tpu_custom_call" | custom-call | flops 1000000000 | bytes 8388608 | tf_op jit(solution)/shard_map/sort_points/pallas_call | solution.py:332
  4.5 3.5 %collective-permute-start.1 = (f32[536,128]{1,0:T(8,128)}, f32[536,128]{1,0:T(8,128)S(1)}, u32[]{:S(2)}, u32[]{:S(2)}) collective-permute-start(f32[536,128]{1,0:T(8,128)} %get-tuple-element.13.pay), channel_id=1, source_target_pairs={{1,0},{2,1},{3,2},{4,3},{5,4},{6,5},{7,6},{8,7},{9,8},{10,9},{11,1... | collective-permute-start | bytes 823304 | tf_op jit(solution)/shard_map/ppermute | solution.py:352
  8.0 0.0 collective-permute-start
  8.0 0.0 copy-done
  8.0 0.0 copy-start.1
  8.0 0.0 copy-start.3
  8.0 0.6 %grid_table.1.table = f32[4096,128]{1,0:T(8,128)S(1)} custom-call(f32[128,4096]{1,0:T(8,128)S(1)} %bitcast.14), custom_call_target="tpu_custom_call" | custom-call | bytes 8388608 | tf_op jit(solution)/shard_map/grid_table/pallas_call | solution.py:323
  8.6 0.4 copy-done.1
  9.0 0.0 copy-done.3
  9.0 2.4 %own_points_early.1.q0 = f32[16,128]{1,0:T(8,128)S(1)} custom-call(s32[3072]{0:T(1024)S(1)} %bitcast.16, f32[4096,128]{1,0:T(8,128)S(1)} %grid_table.1.table, f32[536,128]{1,0:T(8,128)S(1)} %copy-done.1), custom_call_target="tpu_custom_call" | custom-call | flops 1000000000 | bytes 8388608 | tf_op jit(solution)/shard_map/own_points_early/pallas_call | solution.py:356
  11.4 0.0 copy-start.4
  11.4 0.9 %collective-permute-done.1.pay_hi = f32[536,128]{1,0:T(8,128)S(1)} collective-permute-done((f32[536,128]{1,0:T(8,128)}, f32[536,128]{1,0:T(8,128)S(1)}, u32[]{:S(2)}, u32[]{:S(2)}) %collective-permute-start.1) | collective-permute-done | bytes 274464 | tf_op jit(solution)/shard_map/ppermute | solution.py:352
  12.3 3.9 %collective-permute-done.pay_lo = f32[536,128]{1,0:T(8,128)S(1)} collective-permute-done((f32[536,128]{1,0:T(8,128)}, f32[536,128]{1,0:T(8,128)S(1)}, u32[]{:S(2)}, u32[]{:S(2)}) %collective-permute-start) | collective-permute-done | bytes 274464 | tf_op jit(solution)/shard_map/ppermute | solution.py:351
  16.2 3.9 %side_points.1 = (f32[16,128]{1,0:T(8,128)S(1)}, f32[16,128]{1,0:T(8,128)S(1)}) custom-call(s32[3072]{0:T(1024)S(1)} %fusion.1.list_lo, s32[3072]{0:T(1024)S(1)} %fusion.list_hi, f32[4096,128]{1,0:T(8,128)S(1)} %grid_table.1.table, f32[536,128]{1,0:T(8,128)S(1)} %collective-permute-done.pay_lo, f32[536,128]{1,0:T(8,128)S(1)} %collective-permute-done.1.pay_hi), custom_call_target="tpu_custom_call" | custom-call | tf_op jit(solution)/shard_map/side_points/pallas_call | solution.py:367
  20.1 0.5 collective-permute-start.2
  20.6 0.0 copy-start.6
  20.6 0.1 collective-permute-start.3
  20.7 0.0 copy-done.4
  20.7 3.0 %own_points_late.1 = (f32[16,32,128]{2,1,0:T(8,128)}, f32[16,128]{1,0:T(8,128)S(1)}) custom-call(s32[3072]{0:T(1024)S(1)} %bitcast.17, f32[16]{0:T(128)S(1)} %copy-done.4, f32[128,4096]{1,0:T(8,128)S(1)} %bitcast.15, f32[4096,128]{1,0:T(8,128)S(1)} %grid_table.1.table, f32[536,128]{1,0:T(8,128)S(1)} %copy-done.1, f32[16,128]{1,0:T(8,128)S(1)} %get-tuple-element.14.after), custom_call_target="tpu_custom_call" | custom-call | flops 1000000000 | bytes 8388608 | tf_op jit(solution)/shard_map/own_points_late/pallas_call | solution.py:385
  23.7 0.0 copy-start.7
  23.7 0.0 copy-start.5
  23.7 0.0 copy-start.2
  23.7 0.0 collective-permute-done.2.q2
  23.7 2.1 %collective-permute-done.3.q3 = f32[16,128]{1,0:T(8,128)S(1)} collective-permute-done((f32[16,128]{1,0:T(8,128)S(1)}, f32[16,128]{1,0:T(8,128)S(1)}, u32[]{:S(2)}, u32[]{:S(2)}) %collective-permute-start.3) | collective-permute-done | bytes 8224 | tf_op jit(solution)/shard_map/ppermute | solution.py:383
  25.8 0.1 broadcast_in_dim.10.occ
  25.9 1.0 %partial_matrices.1 = f32[16,32,128]{2,1,0:T(8,128)} custom-call(f32[16,128]{1,0:T(8,128)S(1)} %own_points_early.1.q0, f32[16,128]{1,0:T(8,128)S(1)} %get-tuple-element.15.q1, f32[16,128]{1,0:T(8,128)S(1)} %collective-permute-done.2.q2, f32[16,128]{1,0:T(8,128)S(1)} %collective-permute-done.3.q3, ...), custom_call_target="tpu_custom_call", output_to_operand_aliasing={{}: (5, {})} | custom-call | tf_op jit(solution)/shard_map/partial_matrices/pallas_call | solution.py:396
  26.8 10.8 %all-to-all-start = ((f32[16,32,128]{2,1,0:T(8,128)}), f32[16,32,128]{2,1,0:T(8,128)S(1)}, u32[]{:S(2)}, u32[]{:S(2)}) async-start(f32[16,32,128]{2,1,0:T(8,128)} %partial_matrices.1), calls=%async_computation | async-start | bytes 524288 | tf_op jit(solution)/shard_map/all_to_all | solution.py:413
  37.6 0.0 copy-done.6
  37.6 0.2 tile.10.coupling
  37.9 0.0 copy-done.7
  37.9 0.1 iota_compare_fusion
  37.9 0.0 copy-done.5
  38.0 10.2 %all-to-all-done.recv = f32[16,32,128]{2,1,0:T(8,128)S(1)} async-done(((f32[16,32,128]{2,1,0:T(8,128)}), f32[16,32,128]{2,1,0:T(8,128)S(1)}, u32[]{:S(2)}, u32[]{:S(2)}) %all-to-all-start) | async-done | bytes 262176 | tf_op jit(solution)/shard_map/all_to_all | solution.py:413
  48.1 0.0 copy-done.2
  48.1 1.0 %charges.1 = (f32[8,256]{1,0:T(8,128)S(1)}, f32[8,256]{1,0:T(8,128)S(1)}, f32[8,256]{1,0:T(8,128)S(1)}, f32[16,128]{1,0:T(8,128)S(1)}) custom-call(s32[1]{0:T(128)} %bitcast.start, f32[16,32,128]{2,1,0:T(8,128)S(1)} %all-to-all-done.recv, f32[9,16,128]{2,1,0:T(8,128)S(1)} %tile.10.coupling, f32[9,8,512]{2,1,0:T(8,128)S(1)} %select_bitcast_fusion.shapes, ...), custom_call_target="tpu_custom_call" | custom-call | tf_op jit(solution)/shard_map/charges/pallas_call | solution.py:420
  49.1 0.1 reshape.49
  49.2 0.1 collective-permute-start.4
  49.3 0.5 collective-permute-start.5
  49.8 0.6 %slice_bitcast_fusion = f32[8,13,13]{2,0,1:T(8,128)} fusion(f32[16,8,16]{2,1,0:T(8,128)S(1)} %reshape.49), kind=kLoop, calls=%fused_computation.1 | loop fusion | bytes 10816 | tf_op jit(solution)/shard_map/transpose | solution.py:431
  50.4 0.2 collective-permute-done.4
  50.6 3.9 %collective-permute-done.5 = f32[8,256]{1,0:T(8,128)S(1)} collective-permute-done((f32[8,256]{1,0:T(8,128)S(1)}, f32[8,256]{1,0:T(8,128)S(1)}, u32[]{:S(2)}, u32[]{:S(2)}) %collective-permute-start.5) | collective-permute-done | bytes 8224 | tf_op jit(solution)/shard_map/ppermute | solution.py:429
  54.5 0.6 %add_add_fusion = f32[8,256]{1,0:T(8,128)} fusion(f32[8,256]{1,0:T(8,128)S(1)} %collective-permute-done.5, f32[8,256]{1,0:T(8,128)S(1)} %get-tuple-element.18, f32[8,256]{1,0:T(8,128)S(1)} %collective-permute-done.4), kind=kLoop, calls=%fused_computation.7 | loop fusion | flops 4096 | bytes 32768 | tf_op jit(solution)/shard_map/add | solution.py:430
  (5 shorter events, 0.1 us)
Async XLA Ops:
  0.6 7.3 %copy-start = (f32[16,8,4096]{2,1,0:T(8,128)S(1)}, f32[16,8,4096]{2,1,0:T(8,128)}, u32[]{:S(2)}) copy-start(f32[16,8,4096]{2,1,0:T(8,128)} %param.7) | copy-start | bytes 6291460
  4.5 7.8 %collective-permute-start.1 = (f32[536,128]{1,0:T(8,128)}, f32[536,128]{1,0:T(8,128)S(1)}, u32[]{:S(2)}, u32[]{:S(2)}) collective-permute-start(f32[536,128]{1,0:T(8,128)} %get-tuple-element.13.pay), channel_id=1, source_target_pairs={{1,0},{2,1},{3,2},{4,3},{5,4},{6,5},{7,6},{8,7},{9,8},{10,9},{11,1... | collective-permute-start | bytes 823304 | tf_op jit(solution)/shard_map/ppermute | solution.py:352
  8.0 8.2 %collective-permute-start = (f32[536,128]{1,0:T(8,128)}, f32[536,128]{1,0:T(8,128)S(1)}, u32[]{:S(2)}, u32[]{:S(2)}) collective-permute-start(f32[536,128]{1,0:T(8,128)} %get-tuple-element.13.pay), channel_id=1, source_target_pairs={{0,1},{1,2},{2,3},{3,4},{4,5},{5,6},{6,7},{7,8},{8,9},{9,10},{10,1... | collective-permute-start | bytes 823304 | tf_op jit(solution)/shard_map/ppermute | solution.py:351
  8.0 1.0 %copy-start.1 = (f32[536,128]{1,0:T(8,128)S(1)}, f32[536,128]{1,0:T(8,128)}, u32[]{:S(2)}) copy-start(f32[536,128]{1,0:T(8,128)} %get-tuple-element.13.pay) | copy-start | bytes 823300
  8.0 1.0 %copy-start.3 = (s32[24,128]{1,0:T(8,128)S(1)}, s32[24,128]{1,0:T(8,128)}, u32[]{:S(2)}) copy-start(s32[24,128]{1,0:T(8,128)} %get-tuple-element.12) | copy-start | bytes 36868
  11.4 9.3 %copy-start.4 = (f32[16]{0:T(128)S(1)}, f32[16]{0:T(128)}, u32[]{:S(2)}) copy-start(f32[16]{0:T(128)} %occ.1) | copy-start | bytes 196
  20.1 3.6 %collective-permute-start.2 = (f32[16,128]{1,0:T(8,128)S(1)}, f32[16,128]{1,0:T(8,128)S(1)}, u32[]{:S(2)}, u32[]{:S(2)}) collective-permute-start(f32[16,128]{1,0:T(8,128)S(1)} %get-tuple-element.14.after), channel_id=1, source_target_pairs={{1,0},{2,1},{3,2},{4,3},{5,4},{6,5},{7,6},{8,7},{9,8},{10,9},{11,1... | collective-permute-start | bytes 24584 | tf_op jit(solution)/shard_map/ppermute | solution.py:382
  20.6 17.0 %copy-start.6 = (f32[9,13,13]{2,1,0:T(8,128)S(1)}, f32[9,13,13]{2,1,0:T(8,128)}, u32[]{:S(2)}) copy-start(f32[9,13,13]{2,1,0:T(8,128)} %param.11) | copy-start | bytes 18256
  20.6 5.2 %collective-permute-start.3 = (f32[16,128]{1,0:T(8,128)S(1)}, f32[16,128]{1,0:T(8,128)S(1)}, u32[]{:S(2)}, u32[]{:S(2)}) collective-permute-start(f32[16,128]{1,0:T(8,128)S(1)} %get-tuple-element.16), channel_id=1, source_target_pairs={{0,1},{1,2},{2,3},{3,4},{4,5},{5,6},{6,7},{7,8},{8,9},{9,10},{10,1... | collective-permute-start | bytes 24584 | tf_op jit(solution)/shard_map/ppermute | solution.py:383
  23.7 14.1 %copy-start.7 = (s32[8]{0:T(128)S(1)}, s32[8]{0:T(128)}, u32[]{:S(2)}) copy-start(s32[8]{0:T(128)} %sizes_in.1) | copy-start | bytes 100
  23.7 14.2 %copy-start.5 = (f32[8,9,512]{2,0,1:T(8,128)S(1)}, f32[8,9,512]{2,0,1:T(8,128)}, u32[]{:S(2)}) copy-start(f32[8,9,512]{2,0,1:T(8,128)} %param.10) | copy-start | bytes 442372
  23.7 24.4 %copy-start.2 = (s32[8,512]{1,0:T(8,128)S(1)}, s32[8,512]{1,0:T(8,128)}, u32[]{:S(2)}) copy-start(s32[8,512]{1,0:T(8,128)} %offsets.1) | copy-start | bytes 49156
  26.8 21.3 %all-to-all-start = ((f32[16,32,128]{2,1,0:T(8,128)}), f32[16,32,128]{2,1,0:T(8,128)S(1)}, u32[]{:S(2)}, u32[]{:S(2)}) async-start(f32[16,32,128]{2,1,0:T(8,128)} %partial_matrices.1), calls=%async_computation | async-start | bytes 524288 | tf_op jit(solution)/shard_map/all_to_all | solution.py:413
  49.2 1.5 %collective-permute-start.4 = (f32[8,256]{1,0:T(8,128)S(1)}, f32[8,256]{1,0:T(8,128)S(1)}, u32[]{:S(2)}, u32[]{:S(2)}) collective-permute-start(f32[8,256]{1,0:T(8,128)S(1)} %get-tuple-element.19), channel_id=1, source_target_pairs={{1,0},{2,1},{3,2},{4,3},{5,4},{6,5},{7,6},{8,7},{9,8},{10,9},{11,1... | collective-permute-start | bytes 24584 | tf_op jit(solution)/shard_map/ppermute | solution.py:428
  49.3 5.3 %collective-permute-start.5 = (f32[8,256]{1,0:T(8,128)S(1)}, f32[8,256]{1,0:T(8,128)S(1)}, u32[]{:S(2)}, u32[]{:S(2)}) collective-permute-start(f32[8,256]{1,0:T(8,128)S(1)} %get-tuple-element.20), channel_id=1, source_target_pairs={{0,1},{1,2},{2,3},{3,4},{4,5},{5,6},{6,7},{7,8},{8,9},{9,10},{10,1... | collective-permute-start | bytes 24584 | tf_op jit(solution)/shard_map/ppermute | solution.py:429

commit v6 on v5

--- a/solution.py
+++ b/solution.py
@@ -14,7 +14,7 @@
 NL = 9
 BANDS = 16
 LANES = 128
-EARLY = 4
+EARLY = 6
 TILES = SPHERE // LANES
 WORDS = SPHERE // 2
 SORTED = TILES * ATOM_DEV * 16
@@ -102,7 +102,7 @@
 
 
 def sort_kernel(
-    sizes_in, offsets_in, projectors_in, pay_out, lists, pay, sizes, offsets, projectors, sems
+    sizes_in, offsets_in, projectors_in, pay, lists, sizes, offsets, projectors, sems
 ):
     pairs = ((sizes_in, sizes), (offsets_in, offsets), (projectors_in, projectors))
     copies = [pltpu.make_async_copy(a, b, sems.at[k]) for k, (a, b) in enumerate(pairs)]
@@ -151,7 +151,6 @@
     )
     table = jnp.transpose(table, (1, 0, 2))
     points = []
-    sent = []
     for a in range(ATOM_DEV):
         high = table[a].astype(BF16)
         low = (table[a] - high.astype(F32)).astype(BF16)
@@ -166,26 +165,25 @@
         first = a * TILES * 16
         for t in range(TILES):
             pay[first + t * 16 : first + (t + 1) * 16, :] = moved[:, t * LANES : (t + 1) * LANES]
-        block = pl.ds(first, TILES * 16)
-        sent.append(pltpu.make_async_copy(pay.at[block], pay_out.at[block], sems.at[3 + a]))
-        sent[-1].start()
         points.append(moved[13:14] * 64.0 + moved[14:15])
     points = jnp.concatenate(points, axis=0)
     words = points[:, :WORDS] + points[:, WORDS:] * float(PLANE)
     for t in range(WORDS // LANES):
-        part = words[:, t * LANES : (t + 1) * LANES]
         at = t * ATOM_DEV
-        pay[SORTED + at : SORTED + at + ATOM_DEV, :] = part
-        lists[at : at + ATOM_DEV, :] = part.astype(jnp.int32)
+        lists[at : at + ATOM_DEV, :] = words[:, t * LANES : (t + 1) * LANES].astype(jnp.int32)
+        for start, shift in ((SORTED, 0), (SORTED + LIST, WORDS)):
+            part = points[:, shift + t * LANES : shift + (t + 1) * LANES]
+            pay[start + at : start + at + ATOM_DEV, :] = part
     at = LIST - ATOM_DEV
     lead = lane[:, :LANES] < LANES // 2
     pay[SORTED + at : SORTED + LIST, :] = jnp.where(lead, n_below, n_above).astype(F32)
+    pay[SORTED + LIST + at : SORTED + 2 * LIST, :] = jnp.zeros((ATOM_DEV, LANES), F32)
     lists[at:LIST, :] = jnp.where(lead, n_below, n_below + n_own)
-    block = pl.ds(SORTED, LIST)
-    sent.append(pltpu.make_async_copy(pay.at[block], pay_out.at[block], sems.at[3 + ATOM_DEV]))
-    sent[-1].start()
-    for copy in sent:
-        copy.wait()
+
+
+def words_of(pay):
+    words = pay[SORTED : SORTED + LIST] + pay[SORTED + LIST :] * float(PLANE)
+    return words.astype(jnp.int32).reshape(-1)
 
 
 def own_points(atoms, lists, table, pay, rows):
@@ -332,17 +330,16 @@
     pay, lists = pl.pallas_call(
         sort_kernel,
         out_shape=(
-            shape(SORTED + LIST, LANES),
+            shape(SORTED + 2 * LIST, LANES),
             jax.ShapeDtypeStruct((LIST, LANES), jnp.int32),
         ),
         in_specs=[ANY] * 3,
-        out_specs=(ANY, VM),
+        out_specs=(VM, VM),
         scratch_shapes=[
-            pltpu.VMEM((SORTED + LIST, LANES), F32),
             pltpu.SMEM((ATOM_DEV,), jnp.int32),
             pltpu.VMEM((ATOM_DEV, SPHERE), jnp.int32),
             pltpu.VMEM((NI, ATOM_DEV, SPHERE), F32),
-            pltpu.SemaphoreType.DMA((4 + ATOM_DEV,)),
+            pltpu.SemaphoreType.DMA((3,)),
         ],
         compiler_params=params(58 * 2**20),
         cost_estimate=pl.CostEstimate(flops=10**9, bytes_accessed=8 * 2**20, transcendentals=0),
@@ -373,8 +370,8 @@
         compiler_params=params(),
         name="side_points",
     )(
-        pay_lo[SORTED:].astype(jnp.int32).reshape(-1),
-        pay_hi[SORTED:].astype(jnp.int32).reshape(-1),
+        words_of(pay_lo),
+        words_of(pay_hi),
         table,
         pay_lo,
         pay_hi,

time: 55.4 us -> 54.7 us (0.987)
  Pallas kernels: 15.7 us -> 14.7 us
    ppermute x1, waiting for transfers between devices: 2.05 us -> 3.01 us  [local(): back_lo = lax.ppermute(q_hi, 'slab', to_next)]
    pallas_call x1, Pallas kernels: 3.05 us -> 2.16 us  [local(): pl.pallas_call(late_kernel, out_shape=(shape(16, 32, LANES), shape(BANDS,...]
    pallas_call x1, Pallas kernels: 2.42 us -> 3.13 us  [local(): pl.pallas_call(early_kernel, out_shape=shape(BANDS, LANES), in_specs=[SM,...]
    pallas_call x1, Pallas kernels: 3.87 us -> 3.28 us  [local(): pl.pallas_call(sort_kernel, out_shape=(shape(SORTED + 2 * LIST, LANES), j...]
    ppermute x1, waiting for transfers between devices: 0.92 us -> 0.35 us  [local(): pay_hi = lax.ppermute(pay, 'slab', to_prev)]
where the time goes in v6:
time: 54.7 us; the launch traced here: 54.6 us
  waiting for transfers between devices  21.6 us (39%)
  starting transfers between devices  15.5 us (28%)
  Pallas kernels  14.7 us (27%)
  local copies, waits for them, and re-layouts  1.43 us (3%)
  between operations  0.75 us (1%)
  other arithmetic  0.7 us (1%)
    all_to_all x1, starting transfers between devices, local(): recv = lax.all_to_all(packed, 'band', 0, 0)  10.8 us
    all_to_all x1, waiting for transfers between devices, local(): recv = lax.all_to_all(packed, 'band', 0, 0)  10.2 us
    ppermute x1, waiting for transfers between devices, local(): pay_lo = lax.ppermute(pay, 'slab', to_next)  3.9 us
    ppermute x1, waiting for transfers between devices, local(): from_below = lax.ppermute(up, 'slab', to_next)  3.9 us
    pallas_call x1, Pallas kernels, local(): pl.pallas_call(side_kernel, out_shape=(shape(BANDS, LANES), shape(BANDS,...  3.6 us
    ppermute x1, starting transfers between devices, local(): pay_hi = lax.ppermute(pay, 'slab', to_prev)  3.46 us
    pallas_call x1, Pallas kernels, local(): pl.pallas_call(sort_kernel, out_shape=(shape(SORTED + 2 * LIST, LANES), j...  3.28 us
    pallas_call x1, Pallas kernels, local(): pl.pallas_call(early_kernel, out_shape=shape(BANDS, LANES), in_specs=[SM,...  3.13 us
  transfers between devices with their start and end apart: 7, of which 6 were waited for; matrix products, arithmetic and copies ran while one was open for 2% of the time, Pallas kernels for 11%

profile of v6, /device:TPU:32, one launch (start us, length us, event | category | flops | bytes accessed | tf_op | source)
XLA Modules:
  0.0 54.6 jit_solution(17210517567088710662)
XLA Ops:
  0.6 0.0 copy-start
  0.6 3.3 %sort_points.1 = (f32[560,128]{1,0:T(8,128)}, s32[24,128]{1,0:T(8,128)}) custom-call(s32[8]{0:T(128)} %sizes_in.1, s32[8,512]{1,0:T(8,128)} %offsets.1, f32[13,8,512]{2,1,0:T(8,128)} %bitcast.18), custom_call_target="tpu_custom_call" | custom-call | flops 1000000000 | bytes 8388608 | tf_op jit(solution)/shard_map/sort_points/pallas_call | solution.py:330
  3.9 3.5 %collective-permute-start.1 = (f32[560,128]{1,0:T(8,128)}, f32[560,128]{1,0:T(8,128)S(1)}, u32[]{:S(2)}, u32[]{:S(2)}) collective-permute-start(f32[560,128]{1,0:T(8,128)} %get-tuple-element.13.pay), channel_id=1, source_target_pairs={{1,0},{2,1},{3,2},{4,3},{5,4},{6,5},{7,6},{8,7},{9,8},{10,9},{11,1... | collective-permute-start | bytes 860168 | tf_op jit(solution)/shard_map/ppermute | solution.py:349
  7.4 0.0 collective-permute-start
  7.4 0.0 copy-done
  7.4 0.0 copy-start.1
  7.4 0.0 copy-start.3
  7.4 0.6 %grid_table.1.table = f32[4096,128]{1,0:T(8,128)S(1)} custom-call(f32[128,4096]{1,0:T(8,128)S(1)} %bitcast.14), custom_call_target="tpu_custom_call" | custom-call | bytes 8388608 | tf_op jit(solution)/shard_map/grid_table/pallas_call | solution.py:321
  8.0 0.4 copy-done.1
  8.4 0.0 copy-done.3
  8.4 3.1 %own_points_early.1.q0 = f32[16,128]{1,0:T(8,128)S(1)} custom-call(s32[3072]{0:T(1024)S(1)} %bitcast.16, f32[4096,128]{1,0:T(8,128)S(1)} %grid_table.1.table, f32[560,128]{1,0:T(8,128)S(1)} %copy-done.1), custom_call_target="tpu_custom_call" | custom-call | flops 1000000000 | bytes 8388608 | tf_op jit(solution)/shard_map/own_points_early/pallas_call | solution.py:353
  11.5 0.0 copy-start.4
  11.5 0.3 collective-permute-done.1.pay_hi
  11.9 3.9 %collective-permute-done.pay_lo = f32[560,128]{1,0:T(8,128)S(1)} collective-permute-done((f32[560,128]{1,0:T(8,128)}, f32[560,128]{1,0:T(8,128)S(1)}, u32[]{:S(2)}, u32[]{:S(2)}) %collective-permute-start) | collective-permute-done | bytes 286752 | tf_op jit(solution)/shard_map/ppermute | solution.py:348
  15.8 3.6 %side_points.1 = (f32[16,128]{1,0:T(8,128)S(1)}, f32[16,128]{1,0:T(8,128)S(1)}) custom-call(s32[3072]{0:T(1024)S(1)} %fusion.5.list_lo, s32[3072]{0:T(1024)S(1)} %fusion.2.list_hi, f32[4096,128]{1,0:T(8,128)S(1)} %grid_table.1.table, f32[560,128]{1,0:T(8,128)S(1)} %collective-permute-done.pay_lo, f32[560,128]{1,0:T(8,128)S(1)} %collective-permute-done.1.pay_hi), custom_call_target="tpu_custom_call" | custom-call | tf_op jit(solution)/shard_map/side_points/pallas_call | solution.py:364
  19.4 0.6 %collective-permute-start.2 = (f32[16,128]{1,0:T(8,128)S(1)}, f32[16,128]{1,0:T(8,128)S(1)}, u32[]{:S(2)}, u32[]{:S(2)}) collective-permute-start(f32[16,128]{1,0:T(8,128)S(1)} %get-tuple-element.14.after), channel_id=1, source_target_pairs={{1,0},{2,1},{3,2},{4,3},{5,4},{6,5},{7,6},{8,7},{9,8},{10,9},{11,1... | collective-permute-start | bytes 24584 | tf_op jit(solution)/shard_map/ppermute | solution.py:379
  20.0 0.0 copy-start.6
  20.0 0.0 collective-permute-start.3
  20.0 0.0 copy-done.4
  20.0 2.2 %own_points_late.1 = (f32[16,32,128]{2,1,0:T(8,128)}, f32[16,128]{1,0:T(8,128)S(1)}) custom-call(s32[3072]{0:T(1024)S(1)} %bitcast.17, f32[16]{0:T(128)S(1)} %copy-done.4, f32[128,4096]{1,0:T(8,128)S(1)} %bitcast.15, f32[4096,128]{1,0:T(8,128)S(1)} %grid_table.1.table, f32[560,128]{1,0:T(8,128)S(1)} %copy-done.1, f32[16,128]{1,0:T(8,128)S(1)} %get-tuple-element.14.after), custom_call_target="tpu_custom_call" | custom-call | flops 1000000000 | bytes 8388608 | tf_op jit(solution)/shard_map/own_points_late/pallas_call | solution.py:382
  22.2 0.0 copy-start.7
  22.2 0.0 copy-start.5
  22.2 0.0 copy-start.2
  22.2 0.0 collective-permute-done.2.q2
  22.2 3.0 %collective-permute-done.3.q3 = f32[16,128]{1,0:T(8,128)S(1)} collective-permute-done((f32[16,128]{1,0:T(8,128)S(1)}, f32[16,128]{1,0:T(8,128)S(1)}, u32[]{:S(2)}, u32[]{:S(2)}) %collective-permute-start.3) | collective-permute-done | bytes 8224 | tf_op jit(solution)/shard_map/ppermute | solution.py:380
  25.2 0.1 broadcast_in_dim.10.occ
  25.3 1.0 %partial_matrices.1 = f32[16,32,128]{2,1,0:T(8,128)} custom-call(f32[16,128]{1,0:T(8,128)S(1)} %own_points_early.1.q0, f32[16,128]{1,0:T(8,128)S(1)} %get-tuple-element.15.q1, f32[16,128]{1,0:T(8,128)S(1)} %collective-permute-done.2.q2, f32[16,128]{1,0:T(8,128)S(1)} %collective-permute-done.3.q3, ...), custom_call_target="tpu_custom_call", output_to_operand_aliasing={{}: (5, {})} | custom-call | tf_op jit(solution)/shard_map/partial_matrices/pallas_call | solution.py:393
  26.2 10.8 %all-to-all-start = ((f32[16,32,128]{2,1,0:T(8,128)}), f32[16,32,128]{2,1,0:T(8,128)S(1)}, u32[]{:S(2)}, u32[]{:S(2)}) async-start(f32[16,32,128]{2,1,0:T(8,128)} %partial_matrices.1), calls=%async_computation | async-start | bytes 524288 | tf_op jit(solution)/shard_map/all_to_all | solution.py:410
  37.0 0.0 copy-done.6
  37.1 0.2 tile.10.coupling
  37.3 0.0 copy-done.7
  37.3 0.1 iota_compare_fusion
  37.4 0.0 copy-done.5
  37.4 10.2 %all-to-all-done.recv = f32[16,32,128]{2,1,0:T(8,128)S(1)} async-done(((f32[16,32,128]{2,1,0:T(8,128)}), f32[16,32,128]{2,1,0:T(8,128)S(1)}, u32[]{:S(2)}, u32[]{:S(2)}) %all-to-all-start) | async-done | bytes 262176 | tf_op jit(solution)/shard_map/all_to_all | solution.py:410
  47.6 0.0 copy-done.2
  47.6 1.0 %charges.1 = (f32[8,256]{1,0:T(8,128)S(1)}, f32[8,256]{1,0:T(8,128)S(1)}, f32[8,256]{1,0:T(8,128)S(1)}, f32[16,128]{1,0:T(8,128)S(1)}) custom-call(s32[1]{0:T(128)} %bitcast.start, f32[16,32,128]{2,1,0:T(8,128)S(1)} %all-to-all-done.recv, f32[9,16,128]{2,1,0:T(8,128)S(1)} %tile.10.coupling, f32[9,8,512]{2,1,0:T(8,128)S(1)} %select_bitcast_fusion.shapes, ...), custom_call_target="tpu_custom_call" | custom-call | tf_op jit(solution)/shard_map/charges/pallas_call | solution.py:417
  48.5 0.1 reshape.49
  48.6 0.1 collective-permute-start.4
  48.7 0.5 collective-permute-start.5
  49.2 0.6 %slice_bitcast_fusion = f32[8,13,13]{2,0,1:T(8,128)} fusion(f32[16,8,16]{2,1,0:T(8,128)S(1)} %reshape.49), kind=kLoop, calls=%fused_computation.1 | loop fusion | bytes 10816 | tf_op jit(solution)/shard_map/transpose | solution.py:428
  49.8 0.2 collective-permute-done.4
  50.1 3.9 %collective-permute-done.5 = f32[8,256]{1,0:T(8,128)S(1)} collective-permute-done((f32[8,256]{1,0:T(8,128)S(1)}, f32[8,256]{1,0:T(8,128)S(1)}, u32[]{:S(2)}, u32[]{:S(2)}) %collective-permute-start.5) | collective-permute-done | bytes 8224 | tf_op jit(solution)/shard_map/ppermute | solution.py:426
  54.0 0.6 %add_add_fusion = f32[8,256]{1,0:T(8,128)} fusion(f32[8,256]{1,0:T(8,128)S(1)} %collective-permute-done.5, f32[8,256]{1,0:T(8,128)S(1)} %get-tuple-element.18, f32[8,256]{1,0:T(8,128)S(1)} %collective-permute-done.4), kind=kLoop, calls=%fused_computation.11 | loop fusion | flops 4096 | bytes 32768 | tf_op jit(solution)/shard_map/add | solution.py:427
  (5 shorter events, 0.1 us)
Async XLA Ops:
  0.6 6.8 %copy-start = (f32[16,8,4096]{2,1,0:T(8,128)S(1)}, f32[16,8,4096]{2,1,0:T(8,128)}, u32[]{:S(2)}) copy-start(f32[16,8,4096]{2,1,0:T(8,128)} %param.7) | copy-start | bytes 6291460
  3.9 7.9 %collective-permute-start.1 = (f32[560,128]{1,0:T(8,128)}, f32[560,128]{1,0:T(8,128)S(1)}, u32[]{:S(2)}, u32[]{:S(2)}) collective-permute-start(f32[560,128]{1,0:T(8,128)} %get-tuple-element.13.pay), channel_id=1, source_target_pairs={{1,0},{2,1},{3,2},{4,3},{5,4},{6,5},{7,6},{8,7},{9,8},{10,9},{11,1... | collective-permute-start | bytes 860168 | tf_op jit(solution)/shard_map/ppermute | solution.py:349
  7.4 8.4 %collective-permute-start = (f32[560,128]{1,0:T(8,128)}, f32[560,128]{1,0:T(8,128)S(1)}, u32[]{:S(2)}, u32[]{:S(2)}) collective-permute-start(f32[560,128]{1,0:T(8,128)} %get-tuple-element.13.pay), channel_id=1, source_target_pairs={{0,1},{1,2},{2,3},{3,4},{4,5},{5,6},{6,7},{7,8},{8,9},{9,10},{10,1... | collective-permute-start | bytes 860168 | tf_op jit(solution)/shard_map/ppermute | solution.py:348
  7.4 1.0 %copy-start.1 = (f32[560,128]{1,0:T(8,128)S(1)}, f32[560,128]{1,0:T(8,128)}, u32[]{:S(2)}) copy-start(f32[560,128]{1,0:T(8,128)} %get-tuple-element.13.pay) | copy-start | bytes 860164
  7.4 1.0 %copy-start.3 = (s32[24,128]{1,0:T(8,128)S(1)}, s32[24,128]{1,0:T(8,128)}, u32[]{:S(2)}) copy-start(s32[24,128]{1,0:T(8,128)} %get-tuple-element.12) | copy-start | bytes 36868
  11.5 8.5 %copy-start.4 = (f32[16]{0:T(128)S(1)}, f32[16]{0:T(128)}, u32[]{:S(2)}) copy-start(f32[16]{0:T(128)} %occ.1) | copy-start | bytes 196
  19.4 2.8 %collective-permute-start.2 = (f32[16,128]{1,0:T(8,128)S(1)}, f32[16,128]{1,0:T(8,128)S(1)}, u32[]{:S(2)}, u32[]{:S(2)}) collective-permute-start(f32[16,128]{1,0:T(8,128)S(1)} %get-tuple-element.14.after), channel_id=1, source_target_pairs={{1,0},{2,1},{3,2},{4,3},{5,4},{6,5},{7,6},{8,7},{9,8},{10,9},{11,1... | collective-permute-start | bytes 24584 | tf_op jit(solution)/shard_map/ppermute | solution.py:379
  20.0 17.0 %copy-start.6 = (f32[9,13,13]{2,1,0:T(8,128)S(1)}, f32[9,13,13]{2,1,0:T(8,128)}, u32[]{:S(2)}) copy-start(f32[9,13,13]{2,1,0:T(8,128)} %param.11) | copy-start | bytes 18256
  20.0 5.2 %collective-permute-start.3 = (f32[16,128]{1,0:T(8,128)S(1)}, f32[16,128]{1,0:T(8,128)S(1)}, u32[]{:S(2)}, u32[]{:S(2)}) collective-permute-start(f32[16,128]{1,0:T(8,128)S(1)} %get-tuple-element.16), channel_id=1, source_target_pairs={{0,1},{1,2},{2,3},{3,4},{4,5},{5,6},{6,7},{7,8},{8,9},{9,10},{10,1... | collective-permute-start | bytes 24584 | tf_op jit(solution)/shard_map/ppermute | solution.py:380
  22.2 15.1 %copy-start.7 = (s32[8]{0:T(128)S(1)}, s32[8]{0:T(128)}, u32[]{:S(2)}) copy-start(s32[8]{0:T(128)} %sizes_in.1) | copy-start | bytes 100
  22.2 15.2 %copy-start.5 = (f32[8,9,512]{2,0,1:T(8,128)S(1)}, f32[8,9,512]{2,0,1:T(8,128)}, u32[]{:S(2)}) copy-start(f32[8,9,512]{2,0,1:T(8,128)} %param.10) | copy-start | bytes 442372
  22.2 25.4 %copy-start.2 = (s32[8,512]{1,0:T(8,128)S(1)}, s32[8,512]{1,0:T(8,128)}, u32[]{:S(2)}) copy-start(s32[8,512]{1,0:T(8,128)} %offsets.1) | copy-start | bytes 49156
  26.2 21.3 %all-to-all-start = ((f32[16,32,128]{2,1,0:T(8,128)}), f32[16,32,128]{2,1,0:T(8,128)S(1)}, u32[]{:S(2)}, u32[]{:S(2)}) async-start(f32[16,32,128]{2,1,0:T(8,128)} %partial_matrices.1), calls=%async_computation | async-start | bytes 524288 | tf_op jit(solution)/shard_map/all_to_all | solution.py:410
  48.6 1.5 %collective-permute-start.4 = (f32[8,256]{1,0:T(8,128)S(1)}, f32[8,256]{1,0:T(8,128)S(1)}, u32[]{:S(2)}, u32[]{:S(2)}) collective-permute-start(f32[8,256]{1,0:T(8,128)S(1)} %get-tuple-element.19), channel_id=1, source_target_pairs={{1,0},{2,1},{3,2},{4,3},{5,4},{6,5},{7,6},{8,7},{9,8},{10,9},{11,1... | collective-permute-start | bytes 24584 | tf_op jit(solution)/shard_map/ppermute | solution.py:425
  48.7 5.3 %collective-permute-start.5 = (f32[8,256]{1,0:T(8,128)S(1)}, f32[8,256]{1,0:T(8,128)S(1)}, u32[]{:S(2)}, u32[]{:S(2)}) collective-permute-start(f32[8,256]{1,0:T(8,128)S(1)} %get-tuple-element.20), channel_id=1, source_target_pairs={{0,1},{1,2},{2,3},{3,4},{4,5},{5,6},{6,7},{7,8},{8,9},{9,10},{10,1... | collective-permute-start | bytes 24584 | tf_op jit(solution)/shard_map/ppermute | solution.py:426

commit v7 on v6

--- a/solution.py
+++ b/solution.py
@@ -14,7 +14,6 @@
 NL = 9
 BANDS = 16
 LANES = 128
-EARLY = 6
 TILES = SPHERE // LANES
 WORDS = SPHERE // 2
 SORTED = TILES * ATOM_DEV * 16
@@ -197,11 +196,11 @@
     return project(pay, rows, -HALO, range(CZ), range(TILES), atoms)
 
 
-def early_kernel(lists, table, pay, q, rows):
-    q[...] = own_points(range(EARLY), lists, table, pay, rows)
-
-
-def late_kernel(lists, occ, x, table, pay, after, packed, q, rows):
+def own_kernel(lists, table, pay, q, rows):
+    q[...] = own_points(range(ATOM_DEV), lists, table, pay, rows)
+
+
+def pseudo_kernel(sizes, occ, x, offsets, shapes, after, packed, place):
     del after
     for c in range(PLANE // LANES):
         cols = slice(c * LANES, (c + 1) * LANES)
@@ -210,10 +209,17 @@
             v = x[n * CZ : (n + 1) * CZ, cols]
             acc = acc + occ[n] * (v * v)
         packed[c // 2, (c % 2) * CZ : (c % 2 + 1) * CZ, :] = acc
-    q[...] = own_points(range(EARLY, ATOM_DEV), lists, table, pay, rows)
-
-
-def side_kernel(list_lo, list_hi, table, pay_lo, pay_hi, q_lo, q_hi, rows):
+    sub = lax.broadcasted_iota(jnp.int32, (ATOM_DEV, SPHERE), 0)
+    lane = lax.broadcasted_iota(jnp.int32, (ATOM_DEV, SPHERE), 1)
+    size = jnp.zeros((ATOM_DEV, SPHERE), jnp.int32)
+    for a in range(ATOM_DEV):
+        size = jnp.where(sub == a, sizes[a], size)
+    for l in range(NL):
+        place[l] = jnp.where(lane < size, shapes[l], 0.0)
+    place[NL] = offsets[...].astype(F32)
+
+
+def side_kernel(list_lo, list_hi, table, pay_lo, pay_hi, q, q_lo, q_hi, to_prev, to_next, rows):
     rows[...] = jnp.zeros_like(rows)
     step = 8
     most = jnp.int32(0)
@@ -246,18 +252,40 @@
         from_above()
         q_hi[...] = project(pay_hi, rows, CZ - HALO, high, range(TILES))
 
-
-def matrix_kernel(q0, q1, q2, q3, occ, packed, out, block, sem):
+    to_prev[0:16, :] = q[...]
+    to_prev[16:32, :] = q_lo[...]
+    to_next[0:16, :] = q[...]
+    to_next[16:32, :] = q_hi[...]
+
+
+def matrix_kernel(
+    q, q_lo, q_hi, prev, following, prev2, following2, occ, coupling, packed, out, block, sem
+):
     del packed
-    proj = q0[...] + q1[...] + q2[...] + q3[...]
-    weighted = proj * occ[...]
-    full = lax.dot_general(
-        weighted, proj, (((0,), (0,)), ((), ())), precision=HIGHEST, preferred_element_type=F32
-    )
     lane_atom = lax.broadcasted_iota(jnp.int32, (16, LANES), 1) // 16
-    acc = jnp.zeros((16, LANES), F32)
-    for a in range(ATOM_DEV):
-        acc = acc + jnp.where(lane_atom == a, full[a * 16 : (a + 1) * 16, :], 0.0)
+    matrices = []
+    for proj in (
+        q[...] + prev[16:32, :] + following[16:32, :],
+        q_lo[...] + prev[0:16, :] + prev2[...],
+        q_hi[...] + following[0:16, :] + following2[...],
+    ):
+        full = lax.dot_general(
+            proj * occ[...],
+            proj,
+            (((0,), (0,)), ((), ())),
+            precision=HIGHEST,
+            preferred_element_type=F32,
+        )
+        acc = jnp.zeros((16, LANES), F32)
+        for a in range(ATOM_DEV):
+            acc = acc + jnp.where(lane_atom == a, full[a * 16 : (a + 1) * 16, :], 0.0)
+        matrices.append(acc)
+    lanes = jnp.concatenate([per_lane(coupling, m) for m in matrices[1:]], axis=1)
+    row = lax.broadcasted_iota(jnp.int32, (2 * LANES, LANES), 0)
+    col = lax.broadcasted_iota(jnp.int32, (2 * LANES, LANES), 1)
+    column = (row % LANES) // 16 * 16 + NI + row // LANES
+    spread = jnp.where(col == column, 1.0, 0.0)
+    acc = matrices[0] + jnp.dot(lanes, spread, precision=HIGHEST, preferred_element_type=F32)
     for b in range(16):
         block[b] = acc
     copy = pltpu.make_async_copy(block, out.at[:, pl.ds(16, 16), :], sem)
@@ -265,48 +293,57 @@
     copy.wait()
 
 
-def charge_kernel(start, recv, coupling, shapes, offsets, core, down, up, matrices):
+def per_lane(coupling, matrix):
+    rows = [jnp.sum(coupling[l] * matrix, axis=0, keepdims=True) for l in range(NL)]
+    return jnp.concatenate(rows + [jnp.zeros((16 - NL, LANES), F32)], axis=0)
+
+
+def charge_kernel(start, recv, coupling, place, place_lo, place_hi, density, matrices):
     total = recv[0]
     for b in range(1, 16):
         total = total + recv[b]
     matrix = total[16:32]
     matrices[...] = matrix
-    per_lane = jnp.concatenate(
-        [jnp.sum(coupling[l] * matrix, axis=0, keepdims=True) for l in range(NL)], axis=0
-    )
     atom = lax.broadcasted_iota(jnp.int32, (ATOM_DEV, LANES), 0)
-    lane_atom = lax.broadcasted_iota(jnp.int32, (ATOM_DEV, LANES), 1) // 16
-    pick = (atom == lane_atom).astype(F32)
-    charges = lax.dot_general(
-        pick, per_lane, (((1,), (1,)), ((), ())), precision=HIGHEST, preferred_element_type=F32
-    )
-    comp = jnp.zeros((ATOM_DEV, SPHERE), F32)
-    for l in range(NL):
-        comp = comp + charges[:, l : l + 1] * shapes[l]
-    c1 = comp.astype(BF16).astype(F32)
-    c2 = (comp - c1).astype(BF16).astype(F32)
-    c3 = comp - c1 - c2
-    plane = offsets[...] >> 12
-    column = (offsets[...] & (PLANE - 1)) - start[0]
-    row = lax.broadcasted_iota(jnp.int32, (24, SPHERE), 0)
-    target = jnp.where(row < 8, row + HALO, jnp.where(row < 16, row - 11, row - 3))
+    lane = lax.broadcasted_iota(jnp.int32, (ATOM_DEV, LANES), 1)
+    row = lax.broadcasted_iota(jnp.int32, (CZ, SPHERE), 0)
     col = lax.broadcasted_iota(jnp.int32, (256, SPHERE), 0)
-    acc = jnp.zeros((80, 256), F32)
-    for a in range(ATOM_DEV):
-        here = target == plane[a : a + 1, :]
-        left = jnp.concatenate(
-            [jnp.where(here, c[a : a + 1, :], 0.0) for c in (c1, c2, c3)]
-            + [jnp.zeros((8, SPHERE), F32)],
-            axis=0,
-        ).astype(BF16)
-        right = jnp.where(col == column[a : a + 1, :], 1.0, 0.0).astype(BF16)
-        acc = acc + lax.dot_general(
-            left, right, (((1,), (1,)), ((), ())), preferred_element_type=F32
+    acc = jnp.zeros((32, 256), F32)
+    for terms, pick, here, shift in (
+        (per_lane(coupling, matrix), lane // 16 == atom, place, -HALO),
+        (matrix, lane == atom * 16 + NI, place_lo, -HALO - CZ),
+        (matrix, lane == atom * 16 + NI + 1, place_hi, CZ - HALO),
+    ):
+        charges = lax.dot_general(
+            pick.astype(F32),
+            terms,
+            (((1,), (1,)), ((), ())),
+            precision=HIGHEST,
+            preferred_element_type=F32,
         )
-    placed = acc[0:24] + acc[24:48] + acc[48:72]
-    core[...] = placed[0:8] + jnp.concatenate([total[0:8], total[8:16]], axis=1)
-    down[...] = placed[8:16]
-    up[...] = placed[16:24]
+        comp = jnp.zeros((ATOM_DEV, SPHERE), F32)
+        for l in range(NL):
+            comp = comp + charges[:, l : l + 1] * here[l]
+        c1 = comp.astype(BF16).astype(F32)
+        c2 = (comp - c1).astype(BF16).astype(F32)
+        c3 = comp - c1 - c2
+        offsets = here[NL].astype(jnp.int32)
+        plane = (offsets >> 12) + shift
+        column = (offsets & (PLANE - 1)) - start[0]
+        for a in range(ATOM_DEV):
+            on = row == plane[a : a + 1, :]
+            left = jnp.concatenate(
+                [jnp.where(on, c[a : a + 1, :], 0.0) for c in (c1, c2, c3)]
+                + [jnp.zeros((8, SPHERE), F32)],
+                axis=0,
+            ).astype(BF16)
+            right = jnp.where(col == column[a : a + 1, :], 1.0, 0.0).astype(BF16)
+            acc = acc + lax.dot_general(
+                left, right, (((1,), (1,)), ((), ())), preferred_element_type=F32
+            )
+    density[...] = (acc[0:8] + acc[8:16] + acc[16:24]) + jnp.concatenate(
+        [total[0:8], total[8:16]], axis=1
+    )
 
 
 def shape(*dims):
@@ -317,6 +354,8 @@
     slabs = lax.axis_size("slab")
     to_next = [(i, (i + 1) % slabs) for i in range(slabs)]
     to_prev = [((i + 1) % slabs, i) for i in range(slabs)]
+    to_next2 = [(i, (i + 2) % slabs) for i in range(slabs)]
+    to_prev2 = [((i + 2) % slabs, i) for i in range(slabs)]
     grid_values = orbitals.reshape(BANDS * CZ, PLANE)
     table = pl.pallas_call(
         table_kernel,
@@ -350,81 +389,89 @@
 
     own_list = lists.reshape(-1)
     scratch = [pltpu.VMEM((ATOM_DEV * SPHERE, LANES), F32)]
-    q_early = pl.pallas_call(
-        early_kernel,
+    q = pl.pallas_call(
+        own_kernel,
         out_shape=shape(BANDS, LANES),
         in_specs=[SM, VM, VM],
         out_specs=VM,
         scratch_shapes=scratch,
         compiler_params=params(),
-        cost_estimate=pl.CostEstimate(flops=10**9, bytes_accessed=8 * 2**20, transcendentals=0),
-        name="own_points_early",
+        cost_estimate=pl.CostEstimate(flops=2 * 10**9, bytes_accessed=8 * 2**20, transcendentals=0),
+        name="own_points",
     )(own_list, table, pay)
 
-    q_lo, q_hi = pl.pallas_call(
+    q_lo, q_hi, for_prev, for_next = pl.pallas_call(
         side_kernel,
-        out_shape=(shape(BANDS, LANES), shape(BANDS, LANES)),
-        in_specs=[SM, SM, VM, VM, VM],
-        out_specs=(VM, VM),
-        scratch_shapes=[pltpu.VMEM((ATOM_DEV * SPHERE, LANES), F32)],
+        out_shape=(
+            shape(BANDS, LANES),
+            shape(BANDS, LANES),
+            shape(2 * BANDS, LANES),
+            shape(2 * BANDS, LANES),
+        ),
+        in_specs=[SM, SM, VM, VM, VM, VM],
+        out_specs=(VM, VM, VM, VM),
+        scratch_shapes=scratch,
         compiler_params=params(),
         name="side_points",
-    )(
-        words_of(pay_lo),
-        words_of(pay_hi),
-        table,
-        pay_lo,
-        pay_hi,
-    )
-    back_hi = lax.ppermute(q_lo, "slab", to_prev)
-    back_lo = lax.ppermute(q_hi, "slab", to_next)
-
-    packed, q_late = pl.pallas_call(
-        late_kernel,
-        out_shape=(shape(16, 32, LANES), shape(BANDS, LANES)),
+    )(words_of(pay_lo), words_of(pay_hi), table, pay_lo, pay_hi, q)
+    prev = lax.ppermute(for_next, "slab", to_next)
+    following = lax.ppermute(for_prev, "slab", to_prev)
+    prev2 = lax.ppermute(q_hi, "slab", to_next2)
+    following2 = lax.ppermute(q_lo, "slab", to_prev2)
+
+    packed, place = pl.pallas_call(
+        pseudo_kernel,
+        out_shape=(shape(16, 32, LANES), shape(NL + 1, ATOM_DEV, SPHERE)),
         in_specs=[SM, SM, VM, VM, VM, ANY],
         out_specs=(VM, VM),
-        scratch_shapes=scratch,
-        compiler_params=params(),
-        cost_estimate=pl.CostEstimate(flops=10**9, bytes_accessed=8 * 2**20, transcendentals=0),
-        name="own_points_late",
-    )(own_list, occupations, grid_values, table, pay, q_lo)
-
+        compiler_params=params(),
+        cost_estimate=pl.CostEstimate(flops=10**8, bytes_accessed=3 * 2**20, transcendentals=0),
+        name="pseudo_density",
+    )(
+        sphere_sizes,
+        occupations,
+        grid_values,
+        sphere_offsets,
+        shapes.transpose(1, 0, 2),
+        q_lo,
+    )
+    place_lo = lax.ppermute(place, "slab", to_next)
+    place_hi = lax.ppermute(place, "slab", to_prev)
+
+    coupling_lanes = jnp.tile(jnp.pad(coupling, ((0, 0), (0, 3), (0, 3))), (1, 1, ATOM_DEV))
     packed = pl.pallas_call(
         matrix_kernel,
         out_shape=shape(16, 32, LANES),
-        in_specs=[VM] * 5 + [ANY],
+        in_specs=[VM] * 9 + [ANY],
         out_specs=ANY,
         scratch_shapes=[pltpu.VMEM((16, 16, LANES), F32), pltpu.SemaphoreType.DMA],
-        input_output_aliases={5: 0},
+        input_output_aliases={9: 0},
         compiler_params=params(),
         name="partial_matrices",
     )(
-        q_early,
-        q_late,
-        back_hi,
-        back_lo,
+        q,
+        q_lo,
+        q_hi,
+        prev,
+        following,
+        prev2,
+        following2,
         jnp.broadcast_to(occupations[:, None], (BANDS, LANES)),
+        coupling_lanes,
         packed,
     )
     recv = lax.all_to_all(packed, "band", 0, 0)
 
-    coupling_lanes = jnp.tile(jnp.pad(coupling, ((0, 0), (0, 3), (0, 3))), (1, 1, ATOM_DEV))
-    live = jnp.arange(SPHERE, dtype=jnp.int32)[None, :] < sphere_sizes[:, None]
-    shapes_live = jnp.where(live[:, None, :], shapes, 0.0).transpose(1, 0, 2)
     width = PLANE // lax.axis_size("band")
     start = (lax.axis_index("band") * width).astype(jnp.int32).reshape(1)
-    core, down, up, matrices = pl.pallas_call(
+    density, matrices = pl.pallas_call(
         charge_kernel,
-        out_shape=(shape(CZ, 256), shape(CZ, 256), shape(CZ, 256), shape(16, LANES)),
-        in_specs=[SM, VM, VM, VM, VM],
-        out_specs=(VM, VM, VM, VM),
+        out_shape=(shape(CZ, 256), shape(16, LANES)),
+        in_specs=[SM, VM, VM, VM, VM, VM],
+        out_specs=(VM, VM),
         compiler_params=params(),
         name="charges",
-    )(start, recv, coupling_lanes, shapes_live, sphere_offsets)
-    from_above = lax.ppermute(down, "slab", to_prev)
-    from_below = lax.ppermute(up, "slab", to_next)
-    density = core + from_above + from_below
+    )(start, recv, coupling_lanes, place, place_lo, place_hi)
     density_matrices = matrices.reshape(16, ATOM_DEV, 16)[:NI, :, :NI].transpose(1, 0, 2)
     return (density, density_matrices)
 

time: 54.7 us -> 57.7 us (1.055); the launches traced: 54.6 us -> 57 us
  waiting for transfers between devices: 21.6 us -> 12.8 us
  starting transfers between devices: 15.5 us -> 24 us
  Pallas kernels: 14.7 us -> 17.9 us
  other arithmetic: 0.7 us -> 0.04 us
    ppermute x4 -> x6, starting transfers between devices: 1.23 us -> 9.81 us  [the longest x1 3.86 us: local(): following = lax.ppermute(for_prev, 'slab', to_prev)]
    all_to_all x1, waiting for transfers between devices: 10.2 us -> 3.23 us  [local(): recv = lax.all_to_all(packed, 'band', 0, 0)]
    pallas_call x3, Pallas kernels: 6.24 us -> 9.46 us  [the longest x1 4.01 us: local(): pl.pallas_call(own_kernel, out_shape=shape(BANDS, LANES), in_specs=[SM, V...]
    ppermute x4 -> x6, waiting for transfers between devices: 7.15 us -> 6.22 us  [the longest x1 3.69 us: local(): place_lo = lax.ppermute(place, 'slab', to_next)]
    add x1 -> x0, other arithmetic: 0.6 us -> none  [local(): density = core + from_above + from_below]
  transfers between devices with their start and end apart: 7 -> 9, of which waited for: 6 -> 5; matrix products, arithmetic and copies ran while one was open for 2% -> 0% of each run, Pallas kernels for 11% -> 11%
where the time goes in v7:
time: 57.7 us; the launch traced here: 57 us
  starting transfers between devices  24 us (42%)
  Pallas kernels  17.9 us (31%)
  waiting for transfers between devices  12.8 us (22%)
  local copies, waits for them, and re-layouts  1.44 us (2%)
  between operations  0.79 us (1%)
    all_to_all x1, starting transfers between devices, local(): recv = lax.all_to_all(packed, 'band', 0, 0)  10.8 us
    pallas_call x1, Pallas kernels, local(): pl.pallas_call(own_kernel, out_shape=shape(BANDS, LANES), in_specs=[SM, V...  4.01 us
    pallas_call x1, Pallas kernels, local(): pl.pallas_call(charge_kernel, out_shape=(shape(CZ, 256), shape(16, LANES)...  3.99 us
    ppermute x1, starting transfers between devices, local(): following = lax.ppermute(for_prev, 'slab', to_prev)  3.86 us
    ppermute x1, starting transfers between devices, local(): place_hi = lax.ppermute(place, 'slab', to_prev)  3.85 us
    ppermute x1, waiting for transfers between devices, local(): place_lo = lax.ppermute(place, 'slab', to_next)  3.69 us
    ppermute x1, starting transfers between devices, local(): pay_hi = lax.ppermute(pay, 'slab', to_prev)  3.46 us
    ppermute x1, waiting for transfers between devices, local(): pay_lo = lax.ppermute(pay, 'slab', to_next)  3.33 us
  transfers between devices with their start and end apart: 9, of which 5 were waited for; matrix products, arithmetic and copies ran while one was open for 0% of the time, Pallas kernels for 11%

profile of v7, /device:TPU:32, one launch (start us, length us, event | category | flops | bytes accessed | tf_op | source)
XLA Modules:
  0.0 57.0 jit_solution(16106999591153327576)
XLA Ops:
  0.6 0.0 copy-start
  0.6 3.3 %sort_points.1 = (f32[560,128]{1,0:T(8,128)}, s32[24,128]{1,0:T(8,128)}) custom-call(s32[8]{0:T(128)} %sizes.1, s32[8,512]{1,0:T(8,128)} %offsets.1, f32[13,8,512]{2,1,0:T(8,128)} %bitcast.17), custom_call_target="tpu_custom_call" | custom-call | flops 1000000000 | bytes 8388608 | tf_op jit(solution)/shard_map/sort_points/pallas_call | solution.py:369
  3.9 3.5 %collective-permute-start.1 = (f32[560,128]{1,0:T(8,128)}, f32[560,128]{1,0:T(8,128)S(1)}, u32[]{:S(2)}, u32[]{:S(2)}) collective-permute-start(f32[560,128]{1,0:T(8,128)} %get-tuple-element.13.pay), channel_id=1, source_target_pairs={{1,0},{2,1},{3,2},{4,3},{5,4},{6,5},{7,6},{8,7},{9,8},{10,9},{11,1... | collective-permute-start | bytes 860168 | tf_op jit(solution)/shard_map/ppermute | solution.py:388
  7.4 0.0 collective-permute-start
  7.4 0.0 copy-done
  7.4 0.0 copy-start.5
  7.4 0.0 copy-start.6
  7.4 0.6 %grid_table.1.table = f32[4096,128]{1,0:T(8,128)S(1)} custom-call(f32[128,4096]{1,0:T(8,128)S(1)} %bitcast.13), custom_call_target="tpu_custom_call" | custom-call | bytes 8388608 | tf_op jit(solution)/shard_map/grid_table/pallas_call | solution.py:360
  8.0 0.4 copy-done.5
  8.4 0.0 copy-done.6
  8.4 4.0 %own_points.1.q = f32[16,128]{1,0:T(8,128)S(1)} custom-call(s32[3072]{0:T(1024)S(1)} %bitcast.16, f32[4096,128]{1,0:T(8,128)S(1)} %grid_table.1.table, f32[560,128]{1,0:T(8,128)S(1)} %copy-done.5), custom_call_target="tpu_custom_call" | custom-call | flops 2000000000 | bytes 8388608 | tf_op jit(solution)/shard_map/own_points/pallas_call | solution.py:392
  12.4 0.0 copy-start.7
  12.4 0.0 collective-permute-done.1.pay_hi
  12.4 3.3 %collective-permute-done.pay_lo = f32[560,128]{1,0:T(8,128)S(1)} collective-permute-done((f32[560,128]{1,0:T(8,128)}, f32[560,128]{1,0:T(8,128)S(1)}, u32[]{:S(2)}, u32[]{:S(2)}) %collective-permute-start) | collective-permute-done | bytes 286752 | tf_op jit(solution)/shard_map/ppermute | solution.py:387
  15.8 0.0 copy-start.1
  15.8 0.0 copy-start.2
  15.8 0.0 copy-start.3
  15.8 0.0 copy-start.4
  15.8 3.3 %side_points.1 = (f32[16,128]{1,0:T(8,128)S(1)}, f32[16,128]{1,0:T(8,128)S(1)}, f32[32,128]{1,0:T(8,128)S(1)}, f32[32,128]{1,0:T(8,128)S(1)}) custom-call(s32[3072]{0:T(1024)S(1)} %fusion.5.list_lo, s32[3072]{0:T(1024)S(1)} %fusion.2.list_hi, f32[4096,128]{1,0:T(8,128)S(1)} %grid_table.1.table, f32[560,128]{1,0:T(8,128)S(1)} %collective-permute-done.pay_lo, ...), custom_call_target="tpu_custom_call" | custom-call | tf_op jit(solution)/shard_map/side_points/pallas_call | solution.py:403
  19.1 0.0 collective-permute-start.2
  19.1 3.9 %collective-permute-start.3 = (f32[32,128]{1,0:T(8,128)S(1)}, f32[32,128]{1,0:T(8,128)S(1)}, u32[]{:S(2)}, u32[]{:S(2)}) collective-permute-start(f32[32,128]{1,0:T(8,128)S(1)} %get-tuple-element.17), channel_id=1, source_target_pairs={{1,0},{2,1},{3,2},{4,3},{5,4},{6,5},{7,6},{8,7},{9,8},{10,9},{11,1... | collective-permute-start | bytes 49160 | tf_op jit(solution)/shard_map/ppermute | solution.py:418
  23.0 0.0 copy-done.7
  23.0 0.2 tile.10.coupling
  23.2 0.1 collective-permute-start.5
  23.3 2.0 %collective-permute-start.4 = (f32[16,128]{1,0:T(8,128)S(1)}, f32[16,128]{1,0:T(8,128)S(1)}, u32[]{:S(2)}, u32[]{:S(2)}) collective-permute-start(f32[16,128]{1,0:T(8,128)S(1)} %get-tuple-element.15.q_hi), channel_id=1, source_target_pairs={{0,2},{1,3},{2,4},{3,5},{4,6},{5,7},{6,8},{7,9},{8,10},{9,11},{10,... | collective-permute-start | bytes 24584 | tf_op jit(solution)/shard_map/ppermute | solution.py:419
  25.4 0.0 copy-done.1
  25.4 0.0 copy-done.2
  25.4 0.0 copy-done.3
  25.4 0.0 copy-done.4
  25.4 1.5 %pseudo_density.1 = (f32[16,32,128]{2,1,0:T(8,128)}, f32[10,8,512]{2,1,0:T(8,128)S(1)}) custom-call(s32[8]{0:T(128)S(1)} %copy-done.4, f32[16]{0:T(128)S(1)} %copy-done.3, f32[128,4096]{1,0:T(8,128)S(1)} %bitcast.14, s32[8,512]{1,0:T(8,128)S(1)} %copy-done.2, f32[9,8,512]{2,1,0:T(8,128)S(1)} %bitcast.15, f32[16,128]{1,0:T(8,128)S(1)} %get-tuple-element.14.after.q_lo), custom_call_target="tpu_custom_call" | custom-call | flops 100000000 | bytes 3145728 | tf_op jit(solution)/shard_map/pseudo_density/pallas_call | solution.py:422
  26.8 0.1 collective-permute-done.5.following2
  27.0 2.4 %collective-permute-done.4.prev2 = f32[16,128]{1,0:T(8,128)S(1)} collective-permute-done((f32[16,128]{1,0:T(8,128)S(1)}, f32[16,128]{1,0:T(8,128)S(1)}, u32[]{:S(2)}, u32[]{:S(2)}) %collective-permute-start.4) | collective-permute-done | bytes 8224 | tf_op jit(solution)/shard_map/ppermute | solution.py:419
  29.4 0.0 collective-permute-done.2.prev
  29.4 0.0 collective-permute-done.3.following
  29.4 0.1 broadcast_in_dim.2.occ
  29.4 1.3 %partial_matrices.1 = f32[16,32,128]{2,1,0:T(8,128)} custom-call(f32[16,128]{1,0:T(8,128)S(1)} %own_points.1.q, f32[16,128]{1,0:T(8,128)S(1)} %get-tuple-element.14.after.q_lo, f32[16,128]{1,0:T(8,128)S(1)} %get-tuple-element.15.q_hi, f32[32,128]{1,0:T(8,128)S(1)} %collective-permute-done.2.prev, ...), custom_call_target="tpu_custom_call", output_to_operand_aliasing={{}: (9, {})} | custom-call | tf_op jit(solution)/shard_map/partial_matrices/pallas_call | solution.py:442
  30.7 10.8 %all-to-all-start = ((f32[16,32,128]{2,1,0:T(8,128)}), f32[16,32,128]{2,1,0:T(8,128)S(1)}, u32[]{:S(2)}, u32[]{:S(2)}) async-start(f32[16,32,128]{2,1,0:T(8,128)} %partial_matrices.1), calls=%async_computation | async-start | bytes 524288 | tf_op jit(solution)/shard_map/all_to_all | solution.py:463
  41.5 0.0 collective-permute-start.6
  41.5 3.8 %collective-permute-start.7 = (f32[10,8,512]{2,1,0:T(8,128)S(1)}, f32[10,8,512]{2,1,0:T(8,128)S(1)}, u32[]{:S(2)}, u32[]{:S(2)}) collective-permute-start(f32[10,8,512]{2,1,0:T(8,128)S(1)} %get-tuple-element.19.place), channel_id=1, source_target_pairs={{1,0},{2,1},{3,2},{4,3},{5,4},{6,5},{7,6},{8,7},{9,8},{10,9},{11,1... | collective-permute-start | bytes 491528 | tf_op jit(solution)/shard_map/ppermute | solution.py:439
  45.4 3.7 %collective-permute-done.6.place_lo = f32[10,8,512]{2,1,0:T(8,128)S(1)} collective-permute-done((f32[10,8,512]{2,1,0:T(8,128)S(1)}, f32[10,8,512]{2,1,0:T(8,128)S(1)}, u32[]{:S(2)}, u32[]{:S(2)}) %collective-permute-start.6) | collective-permute-done | bytes 163872 | tf_op jit(solution)/shard_map/ppermute | solution.py:438
  49.0 0.0 collective-permute-done.7.place_hi
  49.1 3.2 %all-to-all-done.recv = f32[16,32,128]{2,1,0:T(8,128)S(1)} async-done(((f32[16,32,128]{2,1,0:T(8,128)}), f32[16,32,128]{2,1,0:T(8,128)S(1)}, u32[]{:S(2)}, u32[]{:S(2)}) %all-to-all-start) | async-done | bytes 262176 | tf_op jit(solution)/shard_map/all_to_all | solution.py:463
  52.3 4.0 %charges.1 = (f32[8,256]{1,0:T(8,128)}, f32[16,128]{1,0:T(8,128)S(1)}) custom-call(s32[1]{0:T(128)} %bitcast.start, f32[16,32,128]{2,1,0:T(8,128)S(1)} %all-to-all-done.recv, f32[9,16,128]{2,1,0:T(8,128)S(1)} %tile.10.coupling, f32[10,8,512]{2,1,0:T(8,128)S(1)} %get-tuple-element.19.place, f32[10,8,512]{2,1,0:T(8,128)S(1)} %collective-permute-done.6.place_lo, ...), custom_call_target="tpu_custom_call" | custom-call | tf_op jit(solution)/shard_map/charges/pallas_call | solution.py:467
  56.3 0.1 reshape.32
  56.4 0.6 %slice_bitcast_fusion = f32[8,13,13]{2,0,1:T(8,128)} fusion(f32[16,8,16]{2,1,0:T(8,128)S(1)} %reshape.32), kind=kLoop, calls=%fused_computation | loop fusion | bytes 10816 | tf_op jit(solution)/shard_map/transpose | solution.py:475
  (4 shorter events, 0.1 us)
Async XLA Ops:
  0.6 6.8 %copy-start = (f32[16,8,4096]{2,1,0:T(8,128)S(1)}, f32[16,8,4096]{2,1,0:T(8,128)}, u32[]{:S(2)}) copy-start(f32[16,8,4096]{2,1,0:T(8,128)} %param.7) | copy-start | bytes 6291460
  3.9 8.5 %collective-permute-start.1 = (f32[560,128]{1,0:T(8,128)}, f32[560,128]{1,0:T(8,128)S(1)}, u32[]{:S(2)}, u32[]{:S(2)}) collective-permute-start(f32[560,128]{1,0:T(8,128)} %get-tuple-element.13.pay), channel_id=1, source_target_pairs={{1,0},{2,1},{3,2},{4,3},{5,4},{6,5},{7,6},{8,7},{9,8},{10,9},{11,1... | collective-permute-start | bytes 860168 | tf_op jit(solution)/shard_map/ppermute | solution.py:388
  7.4 8.4 %collective-permute-start = (f32[560,128]{1,0:T(8,128)}, f32[560,128]{1,0:T(8,128)S(1)}, u32[]{:S(2)}, u32[]{:S(2)}) collective-permute-start(f32[560,128]{1,0:T(8,128)} %get-tuple-element.13.pay), channel_id=1, source_target_pairs={{0,1},{1,2},{2,3},{3,4},{4,5},{5,6},{6,7},{7,8},{8,9},{9,10},{10,1... | collective-permute-start | bytes 860168 | tf_op jit(solution)/shard_map/ppermute | solution.py:387
  7.4 1.0 %copy-start.5 = (f32[560,128]{1,0:T(8,128)S(1)}, f32[560,128]{1,0:T(8,128)}, u32[]{:S(2)}) copy-start(f32[560,128]{1,0:T(8,128)} %get-tuple-element.13.pay) | copy-start | bytes 860164
  7.4 1.0 %copy-start.6 = (s32[24,128]{1,0:T(8,128)S(1)}, s32[24,128]{1,0:T(8,128)}, u32[]{:S(2)}) copy-start(s32[24,128]{1,0:T(8,128)} %get-tuple-element.12) | copy-start | bytes 36868
  12.4 10.6 %copy-start.7 = (f32[9,13,13]{2,1,0:T(8,128)S(1)}, f32[9,13,13]{2,1,0:T(8,128)}, u32[]{:S(2)}) copy-start(f32[9,13,13]{2,1,0:T(8,128)} %param.11) | copy-start | bytes 18256
  15.8 9.6 %copy-start.1 = (f32[8,9,512]{2,0,1:T(8,128)S(1)}, f32[8,9,512]{2,0,1:T(8,128)}, u32[]{:S(2)}) copy-start(f32[8,9,512]{2,0,1:T(8,128)} %param.10) | copy-start | bytes 442372
  15.8 9.6 %copy-start.2 = (s32[8,512]{1,0:T(8,128)S(1)}, s32[8,512]{1,0:T(8,128)}, u32[]{:S(2)}) copy-start(s32[8,512]{1,0:T(8,128)} %offsets.1) | copy-start | bytes 49156
  15.8 9.6 %copy-start.3 = (f32[16]{0:T(128)S(1)}, f32[16]{0:T(128)}, u32[]{:S(2)}) copy-start(f32[16]{0:T(128)} %occ.1) | copy-start | bytes 196
  15.8 9.5 %copy-start.4 = (s32[8]{0:T(128)S(1)}, s32[8]{0:T(128)}, u32[]{:S(2)}) copy-start(s32[8]{0:T(128)} %sizes.1) | copy-start | bytes 100
  19.1 10.3 %collective-permute-start.2 = (f32[32,128]{1,0:T(8,128)S(1)}, f32[32,128]{1,0:T(8,128)S(1)}, u32[]{:S(2)}, u32[]{:S(2)}) collective-permute-start(f32[32,128]{1,0:T(8,128)S(1)} %get-tuple-element.16), channel_id=1, source_target_pairs={{0,1},{1,2},{2,3},{3,4},{4,5},{5,6},{6,7},{7,8},{8,9},{9,10},{10,1... | collective-permute-start | bytes 49160 | tf_op jit(solution)/shard_map/ppermute | solution.py:417
  19.1 10.2 %collective-permute-start.3 = (f32[32,128]{1,0:T(8,128)S(1)}, f32[32,128]{1,0:T(8,128)S(1)}, u32[]{:S(2)}, u32[]{:S(2)}) collective-permute-start(f32[32,128]{1,0:T(8,128)S(1)} %get-tuple-element.17), channel_id=1, source_target_pairs={{1,0},{2,1},{3,2},{4,3},{5,4},{6,5},{7,6},{8,7},{9,8},{10,9},{11,1... | collective-permute-start | bytes 49160 | tf_op jit(solution)/shard_map/ppermute | solution.py:418
  23.2 3.7 %collective-permute-start.5 = (f32[16,128]{1,0:T(8,128)S(1)}, f32[16,128]{1,0:T(8,128)S(1)}, u32[]{:S(2)}, u32[]{:S(2)}) collective-permute-start(f32[16,128]{1,0:T(8,128)S(1)} %get-tuple-element.14.after.q_lo), channel_id=1, source_target_pairs={{2,0},{3,1},{4,2},{5,3},{6,4},{7,5},{8,6},{9,7},{10,8},{11,9},{12,... | collective-permute-start | bytes 24584 | tf_op jit(solution)/shard_map/ppermute | solution.py:420
  23.3 6.0 %collective-permute-start.4 = (f32[16,128]{1,0:T(8,128)S(1)}, f32[16,128]{1,0:T(8,128)S(1)}, u32[]{:S(2)}, u32[]{:S(2)}) collective-permute-start(f32[16,128]{1,0:T(8,128)S(1)} %get-tuple-element.15.q_hi), channel_id=1, source_target_pairs={{0,2},{1,3},{2,4},{3,5},{4,6},{5,7},{6,8},{7,9},{8,10},{9,11},{10,... | collective-permute-start | bytes 24584 | tf_op jit(solution)/shard_map/ppermute | solution.py:419
  30.7 21.5 %all-to-all-start = ((f32[16,32,128]{2,1,0:T(8,128)}), f32[16,32,128]{2,1,0:T(8,128)S(1)}, u32[]{:S(2)}, u32[]{:S(2)}) async-start(f32[16,32,128]{2,1,0:T(8,128)} %partial_matrices.1), calls=%async_computation | async-start | bytes 524288 | tf_op jit(solution)/shard_map/all_to_all | solution.py:463
  41.5 7.5 %collective-permute-start.6 = (f32[10,8,512]{2,1,0:T(8,128)S(1)}, f32[10,8,512]{2,1,0:T(8,128)S(1)}, u32[]{:S(2)}, u32[]{:S(2)}) collective-permute-start(f32[10,8,512]{2,1,0:T(8,128)S(1)} %get-tuple-element.19.place), channel_id=1, source_target_pairs={{0,1},{1,2},{2,3},{3,4},{4,5},{5,6},{6,7},{7,8},{8,9},{9,10},{10,1... | collective-permute-start | bytes 491528 | tf_op jit(solution)/shard_map/ppermute | solution.py:438
  41.5 7.5 %collective-permute-start.7 = (f32[10,8,512]{2,1,0:T(8,128)S(1)}, f32[10,8,512]{2,1,0:T(8,128)S(1)}, u32[]{:S(2)}, u32[]{:S(2)}) collective-permute-start(f32[10,8,512]{2,1,0:T(8,128)S(1)} %get-tuple-element.19.place), channel_id=1, source_target_pairs={{1,0},{2,1},{3,2},{4,3},{5,4},{6,5},{7,6},{8,7},{9,8},{10,9},{11,1... | collective-permute-start | bytes 491528 | tf_op jit(solution)/shard_map/ppermute | solution.py:439

commit v8 on v6

--- a/solution.py
+++ b/solution.py
@@ -1,5 +1,6 @@
 import jax
 import jax.numpy as jnp
+import numpy as np
 from jax import lax
 from jax.experimental import pallas as pl
 from jax.experimental.pallas import tpu as pltpu
@@ -79,9 +80,9 @@
         )
         g_high = gathered.astype(BF16)
         g_low = (gathered - g_high.astype(F32)).astype(BF16)
-        first = jnp.dot(left, g_high, preferred_element_type=F32)
-        second = jnp.dot(left[:span], g_low, preferred_element_type=F32)
-        total = first[:span] + first[span:] + second
+        both = jnp.concatenate([g_high, g_low], axis=1)
+        product = jnp.dot(left, both, preferred_element_type=F32)
+        total = product[:span, :LANES] + product[span:, :LANES] + product[:span, LANES:]
         acc = jnp.zeros((16, LANES), F32)
         for k, z in enumerate(planes):
             acc = acc + jnp.where(lane_plane == z, total[k * 16 : (k + 1) * 16, :], 0.0)
@@ -258,9 +259,13 @@
     acc = jnp.zeros((16, LANES), F32)
     for a in range(ATOM_DEV):
         acc = acc + jnp.where(lane_atom == a, full[a * 16 : (a + 1) * 16, :], 0.0)
+    i = lax.broadcasted_iota(jnp.int32, (8, LANES), 0)
+    j = lax.broadcasted_iota(jnp.int32, (8, LANES), 1) % 16
+    corner = pltpu.roll(pltpu.roll(acc[8:16], 1, 0), LANES - 8, 1)
+    half = jnp.where(j < i, corner, acc[0:8])
     for b in range(16):
-        block[b] = acc
-    copy = pltpu.make_async_copy(block, out.at[:, pl.ds(16, 16), :], sem)
+        block[b] = half
+    copy = pltpu.make_async_copy(block, out.at[:, pl.ds(16, 8), :], sem)
     copy.start()
     copy.wait()
 
@@ -269,7 +274,7 @@
     total = recv[0]
     for b in range(1, 16):
         total = total + recv[b]
-    matrix = total[16:32]
+    matrix = total[16:24]
     matrices[...] = matrix
     per_lane = jnp.concatenate(
         [jnp.sum(coupling[l] * matrix, axis=0, keepdims=True) for l in range(NL)], axis=0
@@ -381,7 +386,7 @@
 
     packed, q_late = pl.pallas_call(
         late_kernel,
-        out_shape=(shape(16, 32, LANES), shape(BANDS, LANES)),
+        out_shape=(shape(16, 24, LANES), shape(BANDS, LANES)),
         in_specs=[SM, SM, VM, VM, VM, ANY],
         out_specs=(VM, VM),
         scratch_shapes=scratch,
@@ -392,10 +397,10 @@
 
     packed = pl.pallas_call(
         matrix_kernel,
-        out_shape=shape(16, 32, LANES),
+        out_shape=shape(16, 24, LANES),
         in_specs=[VM] * 5 + [ANY],
         out_specs=ANY,
-        scratch_shapes=[pltpu.VMEM((16, 16, LANES), F32), pltpu.SemaphoreType.DMA],
+        scratch_shapes=[pltpu.VMEM((16, 8, LANES), F32), pltpu.SemaphoreType.DMA],
         input_output_aliases={5: 0},
         compiler_params=params(),
         name="partial_matrices",
@@ -407,16 +412,24 @@
         jnp.broadcast_to(occupations[:, None], (BANDS, LANES)),
         packed,
     )
+    packed, coupling = lax.optimization_barrier((packed, coupling))
     recv = lax.all_to_all(packed, "band", 0, 0)
 
-    coupling_lanes = jnp.tile(jnp.pad(coupling, ((0, 0), (0, 3), (0, 3))), (1, 1, ATOM_DEV))
+    unpack = np.zeros((8, 16, NI, NI), np.float32)
+    for i in range(NI):
+        for j in range(NI):
+            r, c = min(i, j), max(i, j)
+            p, q = (r, c) if r < 8 else (c - 7, r - 8)
+            unpack[p, q, i, j] = 1.0
+    coupling_packed = jnp.einsum("lij,pqij->lpq", coupling, unpack, precision=HIGHEST)
+    coupling_lanes = jnp.tile(coupling_packed, (1, 1, ATOM_DEV))
     live = jnp.arange(SPHERE, dtype=jnp.int32)[None, :] < sphere_sizes[:, None]
     shapes_live = jnp.where(live[:, None, :], shapes, 0.0).transpose(1, 0, 2)
     width = PLANE // lax.axis_size("band")
     start = (lax.axis_index("band") * width).astype(jnp.int32).reshape(1)
     core, down, up, matrices = pl.pallas_call(
         charge_kernel,
-        out_shape=(shape(CZ, 256), shape(CZ, 256), shape(CZ, 256), shape(16, LANES)),
+        out_shape=(shape(CZ, 256), shape(CZ, 256), shape(CZ, 256), shape(8, LANES)),
         in_specs=[SM, VM, VM, VM, VM],
         out_specs=(VM, VM, VM, VM),
         compiler_params=params(),
@@ -425,7 +438,9 @@
     from_above = lax.ppermute(down, "slab", to_prev)
     from_below = lax.ppermute(up, "slab", to_next)
     density = core + from_above + from_below
-    density_matrices = matrices.reshape(16, ATOM_DEV, 16)[:NI, :, :NI].transpose(1, 0, 2)
+    density_matrices = jnp.einsum(
+        "paq,pqij->aij", matrices.reshape(8, ATOM_DEV, 16), unpack, precision=HIGHEST
+    )
     return (density, density_matrices)
 
 

time: 54.7 us -> 53.8 us (0.984)
  matrix products: 0 us -> 4.98 us
  waiting for transfers between devices: 21.6 us -> 17.4 us
  local copies, waits for them, and re-layouts: 1.43 us -> 0.65 us
  Pallas kernels: 14.7 us -> 14 us
    dot_general x0 -> x2, matrix products: none -> 4.98 us  [the longest x1 3.29 us: local(): jnp.einsum('lij,pqij->lpq', coupling, unpack, precision=HIGHEST)]
    all_to_all x1, waiting for transfers between devices: 10.2 us -> 6.49 us  [local(): recv = lax.all_to_all(packed, 'band', 0, 0)]
    ppermute x1, waiting for transfers between devices: 3.9 us -> 3.07 us  [local(): from_below = lax.ppermute(up, 'slab', to_next)]
    transpose x1 -> x0, local copies, waits for them, and re-layouts: 0.63 us -> none  [local(): matrices.reshape(16, ATOM_DEV, 16)[:NI, :, :NI].transpose(1, 0, 2)]
    pallas_call x1, Pallas kernels: 3.13 us -> 2.54 us  [local(): pl.pallas_call(early_kernel, out_shape=shape(BANDS, LANES), in_specs=[SM,...]
    ppermute x1, waiting for transfers between devices: 0.35 us -> 0.93 us  [local(): pay_hi = lax.ppermute(pay, 'slab', to_prev)]
  transfers between devices with their start and end apart: 7 -> 7, of which waited for: 6 -> 5; matrix products, arithmetic and copies ran while one was open for 2% -> 10% of each run, Pallas kernels for 11% -> 10%
where the time goes in v8:
time: 53.8 us
  waiting for transfers between devices  17.4 us (32%)
  starting transfers between devices  15.3 us (28%)
  Pallas kernels  14 us (26%)
  matrix products  4.98 us (9%)
  between operations  0.77 us (1%)
  other arithmetic  0.7 us (1%)
  local copies, waits for them, and re-layouts  0.65 us (1%)
    all_to_all x1, starting transfers between devices, local(): recv = lax.all_to_all(packed, 'band', 0, 0)  10.8 us
    all_to_all x1, waiting for transfers between devices, local(): recv = lax.all_to_all(packed, 'band', 0, 0)  6.49 us
    ppermute x1, waiting for transfers between devices, local(): pay_lo = lax.ppermute(pay, 'slab', to_next)  3.9 us
    pallas_call x1, Pallas kernels, local(): pl.pallas_call(side_kernel, out_shape=(shape(BANDS, LANES), shape(BANDS,...  3.52 us
    ppermute x1, starting transfers between devices, local(): pay_hi = lax.ppermute(pay, 'slab', to_prev)  3.46 us
    dot_general x1, matrix products, local(): jnp.einsum('lij,pqij->lpq', coupling, unpack, precision=HIGHEST)  3.29 us
    pallas_call x1, Pallas kernels, local(): pl.pallas_call(sort_kernel, out_shape=(shape(SORTED + 2 * LIST, LANES), j...  3.28 us
    ppermute x1, waiting for transfers between devices, local(): from_below = lax.ppermute(up, 'slab', to_next)  3.07 us
  transfers between devices with their start and end apart: 7, of which 5 were waited for; matrix products, arithmetic and copies ran while one was open for 10% of the time, Pallas kernels for 10%

profile of v8, /device:TPU:32, one launch (start us, length us, event | category | flops | bytes accessed | tf_op | source)
XLA Modules:
  0.0 53.8 jit_solution(6172224782436821226)
XLA Ops:
  0.6 0.0 copy-start
  0.6 3.3 %sort_points.1 = (f32[560,128]{1,0:T(8,128)}, s32[24,128]{1,0:T(8,128)}) custom-call(s32[8]{0:T(128)} %sizes_in.1, s32[8,512]{1,0:T(8,128)} %offsets.1, f32[13,8,512]{2,1,0:T(8,128)} %bitcast.28), custom_call_target="tpu_custom_call" | custom-call | flops 1000000000 | bytes 8388608 | tf_op jit(solution)/shard_map/sort_points/pallas_call | solution.py:335
  3.9 3.5 %collective-permute-start.1 = (f32[560,128]{1,0:T(8,128)}, f32[560,128]{1,0:T(8,128)S(1)}, u32[]{:S(2)}, u32[]{:S(2)}) collective-permute-start(f32[560,128]{1,0:T(8,128)} %get-tuple-element.15.pay), channel_id=1, source_target_pairs={{1,0},{2,1},{3,2},{4,3},{5,4},{6,5},{7,6},{8,7},{9,8},{10,9},{11,1... | collective-permute-start | bytes 860168 | tf_op jit(solution)/shard_map/ppermute | solution.py:354
  7.4 0.0 collective-permute-start
  7.4 0.0 copy-done
  7.4 0.0 copy-start.10
  7.4 0.0 copy-start.2
  7.4 0.0 copy-start.4
  7.4 0.6 %grid_table.1.table = f32[4096,128]{1,0:T(8,128)S(1)} custom-call(f32[128,4096]{1,0:T(8,128)S(1)} %bitcast.24), custom_call_target="tpu_custom_call" | custom-call | bytes 8388608 | tf_op jit(solution)/shard_map/grid_table/pallas_call | solution.py:326
  8.0 0.0 copy-done.10
  8.0 0.1 iota_compare_fusion
  8.1 0.3 copy-done.2
  8.4 0.0 copy-done.4
  8.4 2.5 %own_points_early.1.q0 = f32[16,128]{1,0:T(8,128)S(1)} custom-call(s32[3072]{0:T(1024)S(1)} %bitcast.26, f32[4096,128]{1,0:T(8,128)S(1)} %grid_table.1.table, f32[560,128]{1,0:T(8,128)S(1)} %copy-done.2), custom_call_target="tpu_custom_call" | custom-call | flops 1000000000 | bytes 8388608 | tf_op jit(solution)/shard_map/own_points_early/pallas_call | solution.py:358
  10.9 0.0 copy-start.1
  10.9 0.0 copy-start.5
  10.9 0.9 %collective-permute-done.1.pay_hi = f32[560,128]{1,0:T(8,128)S(1)} collective-permute-done((f32[560,128]{1,0:T(8,128)}, f32[560,128]{1,0:T(8,128)S(1)}, u32[]{:S(2)}, u32[]{:S(2)}) %collective-permute-start.1) | collective-permute-done | bytes 286752 | tf_op jit(solution)/shard_map/ppermute | solution.py:354
  11.9 3.9 %collective-permute-done.pay_lo = f32[560,128]{1,0:T(8,128)S(1)} collective-permute-done((f32[560,128]{1,0:T(8,128)}, f32[560,128]{1,0:T(8,128)S(1)}, u32[]{:S(2)}, u32[]{:S(2)}) %collective-permute-start) | collective-permute-done | bytes 286752 | tf_op jit(solution)/shard_map/ppermute | solution.py:353
  15.8 3.5 %side_points.1 = (f32[16,128]{1,0:T(8,128)S(1)}, f32[16,128]{1,0:T(8,128)S(1)}) custom-call(s32[3072]{0:T(1024)S(1)} %fusion.5.list_lo, s32[3072]{0:T(1024)S(1)} %fusion.2.list_hi, f32[4096,128]{1,0:T(8,128)S(1)} %grid_table.1.table, f32[560,128]{1,0:T(8,128)S(1)} %collective-permute-done.pay_lo, f32[560,128]{1,0:T(8,128)S(1)} %collective-permute-done.1.pay_hi), custom_call_target="tpu_custom_call" | custom-call | tf_op jit(solution)/shard_map/side_points/pallas_call | solution.py:369
  19.3 0.5 collective-permute-start.2
  19.8 0.0 copy-start.9
  19.8 0.0 copy-start.7
  19.8 0.0 copy-start.8
  19.8 0.0 collective-permute-start.3
  19.8 0.0 copy-done.1
  19.8 0.0 copy-done.5
  19.9 2.1 %own_points_late.1 = (f32[16,24,128]{2,1,0:T(8,128)}, f32[16,128]{1,0:T(8,128)S(1)}) custom-call(s32[3072]{0:T(1024)S(1)} %bitcast.27, f32[16]{0:T(128)S(1)} %copy-done.5, f32[128,4096]{1,0:T(8,128)S(1)} %bitcast.25, f32[4096,128]{1,0:T(8,128)S(1)} %grid_table.1.table, f32[560,128]{1,0:T(8,128)S(1)} %copy-done.2, f32[16,128]{1,0:T(8,128)S(1)} %get-tuple-element.16.after), custom_call_target="tpu_custom_call" | custom-call | flops 1000000000 | bytes 8388608 | tf_op jit(solution)/shard_map/own_points_late/pallas_call | solution.py:387
  22.0 0.0 copy-start.3
  22.0 0.0 copy-start.6
  22.0 0.0 collective-permute-done.2.q2
  22.0 3.0 %collective-permute-done.3.q3 = f32[16,128]{1,0:T(8,128)S(1)} collective-permute-done((f32[16,128]{1,0:T(8,128)S(1)}, f32[16,128]{1,0:T(8,128)S(1)}, u32[]{:S(2)}, u32[]{:S(2)}) %collective-permute-start.3) | collective-permute-done | bytes 8224 | tf_op jit(solution)/shard_map/ppermute | solution.py:385
  25.0 0.1 broadcast_in_dim.10.occ
  25.1 1.0 %partial_matrices.1 = f32[16,24,128]{2,1,0:T(8,128)} custom-call(f32[16,128]{1,0:T(8,128)S(1)} %own_points_early.1.q0, f32[16,128]{1,0:T(8,128)S(1)} %get-tuple-element.17.q1, f32[16,128]{1,0:T(8,128)S(1)} %collective-permute-done.2.q2, f32[16,128]{1,0:T(8,128)S(1)} %collective-permute-done.3.q3, ...), custom_call_target="tpu_custom_call", output_to_operand_aliasing={{}: (5, {})} | custom-call | tf_op jit(solution)/shard_map/partial_matrices/pallas_call | solution.py:398
  26.0 10.8 %all-to-all-start = ((f32[16,24,128]{2,1,0:T(8,128)}), f32[16,24,128]{2,1,0:T(8,128)S(1)}, u32[]{:S(2)}, u32[]{:S(2)}) async-start(f32[16,24,128]{2,1,0:T(8,128)} %partial_matrices.1), calls=%async_computation | async-start | bytes 393216 | tf_op jit(solution)/shard_map/all_to_all | solution.py:416
  36.8 0.0 copy-done.9
  36.8 0.0 copy-done.7
  36.8 0.0 copy-done.8
  36.9 3.3 %convolution_bitcast_fusion = f32[9,8,16]{2,0,1:T(8,128)S(1)} fusion(f32[8,16,13,13]{3,1,2,0:T(8,128)S(1)} %copy-done.7, f32[9,13,13]{2,1,0:T(8,128)S(1)} %copy-done.8), kind=kOutput, calls=%fused_computation | convolution fusion | flops 2336256 | bytes 97220 | tf_op jit(solution)/shard_map/lij,pqij->lpq/dot_general | solution.py:424
  40.2 0.1 tile.10.coupling
  40.3 6.5 %all-to-all-done.recv = f32[16,24,128]{2,1,0:T(8,128)S(1)} async-done(((f32[16,24,128]{2,1,0:T(8,128)}), f32[16,24,128]{2,1,0:T(8,128)S(1)}, u32[]{:S(2)}, u32[]{:S(2)}) %all-to-all-start) | async-done | bytes 196640 | tf_op jit(solution)/shard_map/all_to_all | solution.py:416
  46.8 0.0 copy-done.3
  46.8 1.0 %charges.1 = (f32[8,256]{1,0:T(8,128)S(1)}, f32[8,256]{1,0:T(8,128)S(1)}, f32[8,256]{1,0:T(8,128)S(1)}, f32[8,128]{1,0:T(8,128)S(1)}) custom-call(s32[1]{0:T(128)} %bitcast.start, f32[16,24,128]{2,1,0:T(8,128)S(1)} %all-to-all-done.recv, f32[9,8,128]{2,1,0:T(8,128)S(1)} %tile.10.coupling, f32[9,8,512]{2,1,0:T(8,128)S(1)} %select_bitcast_fusion.shapes, ...), custom_call_target="tpu_custom_call" | custom-call | tf_op jit(solution)/shard_map/charges/pallas_call | solution.py:430
  47.8 0.1 reshape.52
  47.9 0.0 collective-permute-start.4
  47.9 0.5 collective-permute-start.5
  48.4 0.0 copy-done.6
  48.4 1.7 %convolution_bitcast_fusion.1 = f32[8,13,13]{2,0,1:T(8,128)} fusion(f32[8,8,16,1]{2,1,0,3:T(8,128)S(1)} %reshape.52, f32[8,16,13,13]{3,1,0,2:T(8,128)S(1)} %copy-done.6), kind=kOutput, calls=%fused_computation.1 | convolution fusion | flops 2076672 | bytes 96032 | tf_op jit(solution)/shard_map/paq,pqij->aij/dot_general | solution.py:441
  50.1 0.0 collective-permute-done.4
  50.1 3.1 %collective-permute-done.5 = f32[8,256]{1,0:T(8,128)S(1)} collective-permute-done((f32[8,256]{1,0:T(8,128)S(1)}, f32[8,256]{1,0:T(8,128)S(1)}, u32[]{:S(2)}, u32[]{:S(2)}) %collective-permute-start.5) | collective-permute-done | bytes 8224 | tf_op jit(solution)/shard_map/ppermute | solution.py:439
  53.2 0.6 %add_add_fusion = f32[8,256]{1,0:T(8,128)} fusion(f32[8,256]{1,0:T(8,128)S(1)} %collective-permute-done.5, f32[8,256]{1,0:T(8,128)S(1)} %get-tuple-element.22, f32[8,256]{1,0:T(8,128)S(1)} %collective-permute-done.4), kind=kLoop, calls=%fused_computation.13 | loop fusion | flops 4096 | bytes 32768 | tf_op jit(solution)/shard_map/add | solution.py:440
  (5 shorter events, 0.1 us)
Async XLA Ops:
  0.6 6.8 %copy-start = (f32[16,8,4096]{2,1,0:T(8,128)S(1)}, f32[16,8,4096]{2,1,0:T(8,128)}, u32[]{:S(2)}) copy-start(f32[16,8,4096]{2,1,0:T(8,128)} %param.9) | copy-start | bytes 6291460
  3.9 7.9 %collective-permute-start.1 = (f32[560,128]{1,0:T(8,128)}, f32[560,128]{1,0:T(8,128)S(1)}, u32[]{:S(2)}, u32[]{:S(2)}) collective-permute-start(f32[560,128]{1,0:T(8,128)} %get-tuple-element.15.pay), channel_id=1, source_target_pairs={{1,0},{2,1},{3,2},{4,3},{5,4},{6,5},{7,6},{8,7},{9,8},{10,9},{11,1... | collective-permute-start | bytes 860168 | tf_op jit(solution)/shard_map/ppermute | solution.py:354
  7.4 8.4 %collective-permute-start = (f32[560,128]{1,0:T(8,128)}, f32[560,128]{1,0:T(8,128)S(1)}, u32[]{:S(2)}, u32[]{:S(2)}) collective-permute-start(f32[560,128]{1,0:T(8,128)} %get-tuple-element.15.pay), channel_id=1, source_target_pairs={{0,1},{1,2},{2,3},{3,4},{4,5},{5,6},{6,7},{7,8},{8,9},{9,10},{10,1... | collective-permute-start | bytes 860168 | tf_op jit(solution)/shard_map/ppermute | solution.py:353
  7.4 0.7 %copy-start.10 = (s32[8]{0:T(128)S(1)}, s32[8]{0:T(128)}, u32[]{:S(2)}) copy-start(s32[8]{0:T(128)} %sizes_in.1) | copy-start | bytes 100
  7.4 1.0 %copy-start.2 = (f32[560,128]{1,0:T(8,128)S(1)}, f32[560,128]{1,0:T(8,128)}, u32[]{:S(2)}) copy-start(f32[560,128]{1,0:T(8,128)} %get-tuple-element.15.pay) | copy-start | bytes 860164
  7.4 1.0 %copy-start.4 = (s32[24,128]{1,0:T(8,128)S(1)}, s32[24,128]{1,0:T(8,128)}, u32[]{:S(2)}) copy-start(s32[24,128]{1,0:T(8,128)} %get-tuple-element.14) | copy-start | bytes 36868
  10.9 8.9 %copy-start.1 = (f32[16,8,4096]{2,1,0:T(8,128)S(1)}, f32[16,8,4096]{2,1,0:T(8,128)}, u32[]{:S(2)}) copy-start(f32[16,8,4096]{2,1,0:T(8,128)} %param.9) | copy-start | bytes 6291460
  10.9 8.9 %copy-start.5 = (f32[16]{0:T(128)S(1)}, f32[16]{0:T(128)}, u32[]{:S(2)}) copy-start(f32[16]{0:T(128)} %occ.1) | copy-start | bytes 196
  19.3 2.7 %collective-permute-start.2 = (f32[16,128]{1,0:T(8,128)S(1)}, f32[16,128]{1,0:T(8,128)S(1)}, u32[]{:S(2)}, u32[]{:S(2)}) collective-permute-start(f32[16,128]{1,0:T(8,128)S(1)} %get-tuple-element.16.after), channel_id=1, source_target_pairs={{1,0},{2,1},{3,2},{4,3},{5,4},{6,5},{7,6},{8,7},{9,8},{10,9},{11,1... | collective-permute-start | bytes 24584 | tf_op jit(solution)/shard_map/ppermute | solution.py:384
  19.8 17.0 %copy-start.9 = (f32[8,9,512]{2,0,1:T(8,128)S(1)}, f32[8,9,512]{2,0,1:T(8,128)}, u32[]{:S(2)}) copy-start(f32[8,9,512]{2,0,1:T(8,128)} %param.12) | copy-start | bytes 442372
  19.8 17.0 %copy-start.7 = (f32[8,16,13,13]{3,1,2,0:T(8,128)S(1)}, f32[8,16,13,13]{3,1,2,0:T(8,128)}, u32[]{:S(2)}) copy-start(f32[8,16,13,13]{3,1,2,0:T(8,128)} %constant.13.clone) | copy-start | bytes 259588
  19.8 17.0 %copy-start.8 = (f32[9,13,13]{2,1,0:T(8,128)S(1)}, f32[9,13,13]{2,1,0:T(8,128)}, u32[]{:S(2)}) copy-start(f32[9,13,13]{2,1,0:T(8,128)} %param.13) | copy-start | bytes 18256
  19.8 5.2 %collective-permute-start.3 = (f32[16,128]{1,0:T(8,128)S(1)}, f32[16,128]{1,0:T(8,128)S(1)}, u32[]{:S(2)}, u32[]{:S(2)}) collective-permute-start(f32[16,128]{1,0:T(8,128)S(1)} %get-tuple-element.18), channel_id=1, source_target_pairs={{0,1},{1,2},{2,3},{3,4},{4,5},{5,6},{6,7},{7,8},{8,9},{9,10},{10,1... | collective-permute-start | bytes 24584 | tf_op jit(solution)/shard_map/ppermute | solution.py:385
  22.0 24.8 %copy-start.3 = (s32[8,512]{1,0:T(8,128)S(1)}, s32[8,512]{1,0:T(8,128)}, u32[]{:S(2)}) copy-start(s32[8,512]{1,0:T(8,128)} %offsets.1) | copy-start | bytes 49156
  22.0 26.4 %copy-start.6 = (f32[8,16,13,13]{3,1,0,2:T(8,128)S(1)}, f32[8,16,13,13]{3,1,0,2:T(8,128)}, u32[]{:S(2)}) copy-start(f32[8,16,13,13]{3,1,0,2:T(8,128)} %constant.19) | copy-start | bytes 259588
  26.0 20.8 %all-to-all-start = ((f32[16,24,128]{2,1,0:T(8,128)}), f32[16,24,128]{2,1,0:T(8,128)S(1)}, u32[]{:S(2)}, u32[]{:S(2)}) async-start(f32[16,24,128]{2,1,0:T(8,128)} %partial_matrices.1), calls=%async_computation | async-start | bytes 393216 | tf_op jit(solution)/shard_map/all_to_all | solution.py:416
  47.9 2.2 %collective-permute-start.4 = (f32[8,256]{1,0:T(8,128)S(1)}, f32[8,256]{1,0:T(8,128)S(1)}, u32[]{:S(2)}, u32[]{:S(2)}) collective-permute-start(f32[8,256]{1,0:T(8,128)S(1)} %get-tuple-element.23), channel_id=1, source_target_pairs={{1,0},{2,1},{3,2},{4,3},{5,4},{6,5},{7,6},{8,7},{9,8},{10,9},{11,1... | collective-permute-start | bytes 24584 | tf_op jit(solution)/shard_map/ppermute | solution.py:438
  47.9 5.3 %collective-permute-start.5 = (f32[8,256]{1,0:T(8,128)S(1)}, f32[8,256]{1,0:T(8,128)S(1)}, u32[]{:S(2)}, u32[]{:S(2)}) collective-permute-start(f32[8,256]{1,0:T(8,128)S(1)} %get-tuple-element.24), channel_id=1, source_target_pairs={{0,1},{1,2},{2,3},{3,4},{4,5},{5,6},{6,7},{7,8},{8,9},{9,10},{10,1... | collective-permute-start | bytes 24584 | tf_op jit(solution)/shard_map/ppermute | solution.py:439

commit v9 on v8

--- a/solution.py
+++ b/solution.py
@@ -15,7 +15,7 @@
 NL = 9
 BANDS = 16
 LANES = 128
-EARLY = 6
+EARLY = 5
 TILES = SPHERE // LANES
 WORDS = SPHERE // 2
 SORTED = TILES * ATOM_DEV * 16
@@ -412,7 +412,6 @@
         jnp.broadcast_to(occupations[:, None], (BANDS, LANES)),
         packed,
     )
-    packed, coupling = lax.optimization_barrier((packed, coupling))
     recv = lax.all_to_all(packed, "band", 0, 0)
 
     unpack = np.zeros((8, 16, NI, NI), np.float32)
@@ -421,7 +420,10 @@
             r, c = min(i, j), max(i, j)
             p, q = (r, c) if r < 8 else (c - 7, r - 8)
             unpack[p, q, i, j] = 1.0
-    coupling_packed = jnp.einsum("lij,pqij->lpq", coupling, unpack, precision=HIGHEST)
+    both_ways = jnp.where(np.eye(NI, dtype=bool), coupling, coupling + coupling.transpose(0, 2, 1))
+    top = jnp.pad(both_ways[:, :8], ((0, 0), (0, 0), (0, 3)))
+    low = jnp.pad(both_ways[:, 8:, 8:], ((0, 0), (1, 2), (0, 11)))
+    coupling_packed = jnp.where(np.tri(8, 16, -1, dtype=bool), low, top)
     coupling_lanes = jnp.tile(coupling_packed, (1, 1, ATOM_DEV))
     live = jnp.arange(SPHERE, dtype=jnp.int32)[None, :] < sphere_sizes[:, None]
     shapes_live = jnp.where(live[:, None, :], shapes, 0.0).transpose(1, 0, 2)

time: 53.8 us -> 54 us (level)
  matrix products: 4.98 us -> 1.69 us
  waiting for transfers between devices: 17.4 us -> 20 us
    all_to_all x1, waiting for transfers between devices: 6.49 us -> 9.94 us  [local(): recv = lax.all_to_all(packed, 'band', 0, 0)]
    dot_general x1 -> x0, matrix products: 3.29 us -> none  [local(): jnp.einsum('lij,pqij->lpq', coupling, unpack, precision=HIGHEST)]
  transfers between devices with their start and end apart: 7 -> 7, of which waited for: 5 -> 5; matrix products, arithmetic and copies ran while one was open for 10% -> 4% of each run, Pallas kernels for 10% -> 10%
where the time goes in v9:
time: 54 us; the launch traced here: 53.8 us
  waiting for transfers between devices  20 us (37%)
  starting transfers between devices  15.4 us (29%)
  Pallas kernels  14.2 us (26%)
  matrix products  1.69 us (3%)
  local copies, waits for them, and re-layouts  0.89 us (2%)
  other arithmetic  0.8 us (1%)
  between operations  0.8 us (1%)
    all_to_all x1, starting transfers between devices, local(): recv = lax.all_to_all(packed, 'band', 0, 0)  10.8 us
    all_to_all x1, waiting for transfers between devices, local(): recv = lax.all_to_all(packed, 'band', 0, 0)  9.94 us
    ppermute x1, waiting for transfers between devices, local(): pay_lo = lax.ppermute(pay, 'slab', to_next)  3.9 us
    ppermute x1, starting transfers between devices, local(): pay_hi = lax.ppermute(pay, 'slab', to_prev)  3.46 us
    pallas_call x1, Pallas kernels, local(): pl.pallas_call(side_kernel, out_shape=(shape(BANDS, LANES), shape(BANDS,...  3.37 us
    pallas_call x1, Pallas kernels, local(): pl.pallas_call(sort_kernel, out_shape=(shape(SORTED + 2 * LIST, LANES), j...  3.29 us
    ppermute x1, waiting for transfers between devices, local(): from_below = lax.ppermute(up, 'slab', to_next)  3.07 us
    ppermute x1, waiting for transfers between devices, local(): back_lo = lax.ppermute(q_hi, 'slab', to_next)  2.67 us
  transfers between devices with their start and end apart: 7, of which 5 were waited for; matrix products, arithmetic and copies ran while one was open for 4% of the time, Pallas kernels for 10%

profile of v9, /device:TPU:32, one launch (start us, length us, event | category | flops | bytes accessed | tf_op | source)
XLA Modules:
  0.0 53.8 jit_solution(6652645994154873831)
XLA Ops:
  0.6 0.0 copy-start
  0.6 3.3 %sort_points.1 = (f32[560,128]{1,0:T(8,128)}, s32[24,128]{1,0:T(8,128)}) custom-call(s32[8]{0:T(128)} %sizes_in.1, s32[8,512]{1,0:T(8,128)} %offsets.1, f32[13,8,512]{2,1,0:T(8,128)} %bitcast.25), custom_call_target="tpu_custom_call" | custom-call | flops 1000000000 | bytes 8388608 | tf_op jit(solution)/shard_map/sort_points/pallas_call | solution.py:335
  3.9 3.5 %collective-permute-start.1 = (f32[560,128]{1,0:T(8,128)}, f32[560,128]{1,0:T(8,128)S(1)}, u32[]{:S(2)}, u32[]{:S(2)}) collective-permute-start(f32[560,128]{1,0:T(8,128)} %get-tuple-element.13.pay), channel_id=1, source_target_pairs={{1,0},{2,1},{3,2},{4,3},{5,4},{6,5},{7,6},{8,7},{9,8},{10,9},{11,1... | collective-permute-start | bytes 860168 | tf_op jit(solution)/shard_map/ppermute | solution.py:354
  7.4 0.0 collective-permute-start
  7.4 0.0 copy-done
  7.4 0.0 copy-start.7
  7.4 0.0 copy-start.9
  7.4 0.0 copy-start.10
  7.4 0.0 copy-start.2
  7.4 0.0 copy-start.4
  7.4 0.6 %grid_table.1.table = f32[4096,128]{1,0:T(8,128)S(1)} custom-call(f32[128,4096]{1,0:T(8,128)S(1)} %bitcast.20), custom_call_target="tpu_custom_call" | custom-call | bytes 8388608 | tf_op jit(solution)/shard_map/grid_table/pallas_call | solution.py:326
  8.1 0.2 copy-done.7
  8.3 0.1 copy.14
  8.4 0.0 copy-done.9
  8.5 0.1 slice.28
  8.5 0.0 copy-done.10
  8.5 0.1 pad_select_fusion
  8.6 0.1 copy.15
  8.7 0.1 tile.10.coupling
  8.9 0.0 copy-done.2
  8.9 0.0 copy-done.4
  8.9 2.6 %own_points_early.1.q0 = f32[16,128]{1,0:T(8,128)S(1)} custom-call(s32[3072]{0:T(1024)S(1)} %bitcast.22, f32[4096,128]{1,0:T(8,128)S(1)} %grid_table.1.table, f32[560,128]{1,0:T(8,128)S(1)} %copy-done.2), custom_call_target="tpu_custom_call" | custom-call | flops 1000000000 | bytes 8388608 | tf_op jit(solution)/shard_map/own_points_early/pallas_call | solution.py:358
  11.5 0.0 copy-start.1
  11.5 0.0 copy-start.5
  11.5 0.4 collective-permute-done.1.pay_hi
  11.9 3.9 %collective-permute-done.pay_lo = f32[560,128]{1,0:T(8,128)S(1)} collective-permute-done((f32[560,128]{1,0:T(8,128)}, f32[560,128]{1,0:T(8,128)S(1)}, u32[]{:S(2)}, u32[]{:S(2)}) %collective-permute-start) | collective-permute-done | bytes 286752 | tf_op jit(solution)/shard_map/ppermute | solution.py:353
  15.8 3.4 %side_points.1 = (f32[16,128]{1,0:T(8,128)S(1)}, f32[16,128]{1,0:T(8,128)S(1)}) custom-call(s32[3072]{0:T(1024)S(1)} %fusion.5.list_lo, s32[3072]{0:T(1024)S(1)} %fusion.2.list_hi, f32[4096,128]{1,0:T(8,128)S(1)} %grid_table.1.table, f32[560,128]{1,0:T(8,128)S(1)} %collective-permute-done.pay_lo, f32[560,128]{1,0:T(8,128)S(1)} %collective-permute-done.1.pay_hi), custom_call_target="tpu_custom_call" | custom-call | tf_op jit(solution)/shard_map/side_points/pallas_call | solution.py:369
  19.2 0.6 %collective-permute-start.2 = (f32[16,128]{1,0:T(8,128)S(1)}, f32[16,128]{1,0:T(8,128)S(1)}, u32[]{:S(2)}, u32[]{:S(2)}) collective-permute-start(f32[16,128]{1,0:T(8,128)S(1)} %get-tuple-element.14.after), channel_id=1, source_target_pairs={{1,0},{2,1},{3,2},{4,3},{5,4},{6,5},{7,6},{8,7},{9,8},{10,9},{11,1... | collective-permute-start | bytes 24584 | tf_op jit(solution)/shard_map/ppermute | solution.py:384
  19.7 0.0 copy-start.11
  19.8 0.0 copy-start.8
  19.8 0.0 copy-start.3
  19.8 0.0 copy-start.6
  19.8 0.1 collective-permute-start.3
  19.9 0.0 copy-done.1
  19.9 0.0 copy-done.5
  19.9 2.5 %own_points_late.1 = (f32[16,24,128]{2,1,0:T(8,128)}, f32[16,128]{1,0:T(8,128)S(1)}) custom-call(s32[3072]{0:T(1024)S(1)} %bitcast.23, f32[16]{0:T(128)S(1)} %copy-done.5, f32[128,4096]{1,0:T(8,128)S(1)} %bitcast.21, f32[4096,128]{1,0:T(8,128)S(1)} %grid_table.1.table, f32[560,128]{1,0:T(8,128)S(1)} %copy-done.2, f32[16,128]{1,0:T(8,128)S(1)} %get-tuple-element.14.after), custom_call_target="tpu_custom_call" | custom-call | flops 1000000000 | bytes 8388608 | tf_op jit(solution)/shard_map/own_points_late/pallas_call | solution.py:387
  22.4 0.0 collective-permute-done.2.q2
  22.4 2.7 %collective-permute-done.3.q3 = f32[16,128]{1,0:T(8,128)S(1)} collective-permute-done((f32[16,128]{1,0:T(8,128)S(1)}, f32[16,128]{1,0:T(8,128)S(1)}, u32[]{:S(2)}, u32[]{:S(2)}) %collective-permute-start.3) | collective-permute-done | bytes 8224 | tf_op jit(solution)/shard_map/ppermute | solution.py:385
  25.0 0.1 broadcast_in_dim.29.occ
  25.1 1.0 %partial_matrices.1 = f32[16,24,128]{2,1,0:T(8,128)} custom-call(f32[16,128]{1,0:T(8,128)S(1)} %own_points_early.1.q0, f32[16,128]{1,0:T(8,128)S(1)} %get-tuple-element.15.q1, f32[16,128]{1,0:T(8,128)S(1)} %collective-permute-done.2.q2, f32[16,128]{1,0:T(8,128)S(1)} %collective-permute-done.3.q3, ...), custom_call_target="tpu_custom_call", output_to_operand_aliasing={{}: (5, {})} | custom-call | tf_op jit(solution)/shard_map/partial_matrices/pallas_call | solution.py:398
  26.1 10.8 %all-to-all-start = ((f32[16,24,128]{2,1,0:T(8,128)}), f32[16,24,128]{2,1,0:T(8,128)S(1)}, u32[]{:S(2)}, u32[]{:S(2)}) async-start(f32[16,24,128]{2,1,0:T(8,128)} %partial_matrices.1), calls=%async_computation | async-start | bytes 393216 | tf_op jit(solution)/shard_map/all_to_all | solution.py:415
  36.8 0.0 copy-done.11
  36.9 0.1 iota_compare_fusion
  36.9 0.0 copy-done.8
  36.9 9.9 %all-to-all-done.recv = f32[16,24,128]{2,1,0:T(8,128)S(1)} async-done(((f32[16,24,128]{2,1,0:T(8,128)}), f32[16,24,128]{2,1,0:T(8,128)S(1)}, u32[]{:S(2)}, u32[]{:S(2)}) %all-to-all-start) | async-done | bytes 196640 | tf_op jit(solution)/shard_map/all_to_all | solution.py:415
  46.9 0.0 copy-done.3
  46.9 0.9 %charges.1 = (f32[8,256]{1,0:T(8,128)S(1)}, f32[8,256]{1,0:T(8,128)S(1)}, f32[8,256]{1,0:T(8,128)S(1)}, f32[8,128]{1,0:T(8,128)S(1)}) custom-call(s32[1]{0:T(128)} %bitcast.start, f32[16,24,128]{2,1,0:T(8,128)S(1)} %all-to-all-done.recv, f32[9,8,128]{2,1,0:T(8,128)S(1)} %tile.10.coupling, f32[9,8,512]{2,1,0:T(8,128)S(1)} %select_bitcast_fusion.shapes, ...), custom_call_target="tpu_custom_call" | custom-call | tf_op jit(solution)/shard_map/charges/pallas_call | solution.py:432
  47.8 0.1 reshape.50
  47.9 0.0 collective-permute-start.4
  48.0 0.5 collective-permute-start.5
  48.5 0.0 copy-done.6
  48.5 1.7 %convolution_bitcast_fusion = f32[8,13,13]{2,0,1:T(8,128)} fusion(f32[8,8,16,1]{2,1,0,3:T(8,128)S(1)} %reshape.50, f32[8,16,13,13]{3,1,0,2:T(8,128)S(1)} %copy-done.6), kind=kOutput, calls=%fused_computation | convolution fusion | flops 2076672 | bytes 96032 | tf_op jit(solution)/shard_map/paq,pqij->aij/dot_general | solution.py:443
  50.1 0.0 collective-permute-done.4
  50.1 3.1 %collective-permute-done.5 = f32[8,256]{1,0:T(8,128)S(1)} collective-permute-done((f32[8,256]{1,0:T(8,128)S(1)}, f32[8,256]{1,0:T(8,128)S(1)}, u32[]{:S(2)}, u32[]{:S(2)}) %collective-permute-start.5) | collective-permute-done | bytes 8224 | tf_op jit(solution)/shard_map/ppermute | solution.py:441
  53.2 0.6 %add_add_fusion = f32[8,256]{1,0:T(8,128)} fusion(f32[8,256]{1,0:T(8,128)S(1)} %collective-permute-done.5, f32[8,256]{1,0:T(8,128)S(1)} %get-tuple-element.18, f32[8,256]{1,0:T(8,128)S(1)} %collective-permute-done.4), kind=kLoop, calls=%fused_computation.13 | loop fusion | flops 4096 | bytes 32768 | tf_op jit(solution)/shard_map/add | solution.py:442
  (5 shorter events, 0.1 us)
Async XLA Ops:
  0.6 6.8 %copy-start = (f32[16,8,4096]{2,1,0:T(8,128)S(1)}, f32[16,8,4096]{2,1,0:T(8,128)}, u32[]{:S(2)}) copy-start(f32[16,8,4096]{2,1,0:T(8,128)} %param.10) | copy-start | bytes 6291460
  3.9 7.9 %collective-permute-start.1 = (f32[560,128]{1,0:T(8,128)}, f32[560,128]{1,0:T(8,128)S(1)}, u32[]{:S(2)}, u32[]{:S(2)}) collective-permute-start(f32[560,128]{1,0:T(8,128)} %get-tuple-element.13.pay), channel_id=1, source_target_pairs={{1,0},{2,1},{3,2},{4,3},{5,4},{6,5},{7,6},{8,7},{9,8},{10,9},{11,1... | collective-permute-start | bytes 860168 | tf_op jit(solution)/shard_map/ppermute | solution.py:354
  7.4 8.4 %collective-permute-start = (f32[560,128]{1,0:T(8,128)}, f32[560,128]{1,0:T(8,128)S(1)}, u32[]{:S(2)}, u32[]{:S(2)}) collective-permute-start(f32[560,128]{1,0:T(8,128)} %get-tuple-element.13.pay), channel_id=1, source_target_pairs={{0,1},{1,2},{2,3},{3,4},{4,5},{5,6},{6,7},{7,8},{8,9},{9,10},{10,1... | collective-permute-start | bytes 860168 | tf_op jit(solution)/shard_map/ppermute | solution.py:353
  7.4 0.9 %copy-start.7 = (f32[9,13,13]{2,1,0:T(8,128)S(1)}, f32[9,13,13]{2,1,0:T(8,128)}, u32[]{:S(2)}) copy-start(f32[9,13,13]{2,1,0:T(8,128)} %param.14) | copy-start | bytes 18256
  7.4 1.0 %copy-start.9 = (pred[13,13]{0,1:T(8,128)(4,1)S(1)}, pred[13,13]{0,1:T(8,128)(4,1)}, u32[]{:S(2)}) copy-start(pred[13,13]{0,1:T(8,128)(4,1)} %constant.19.clone) | copy-start | bytes 511
  7.4 1.1 %copy-start.10 = (pred[8,16]{0,1:T(8,128)(4,1)S(1)}, pred[8,16]{0,1:T(8,128)(4,1)}, u32[]{:S(2)}) copy-start(pred[8,16]{0,1:T(8,128)(4,1)} %constant.20.clone) | copy-start | bytes 388
  7.4 1.5 %copy-start.2 = (f32[560,128]{1,0:T(8,128)S(1)}, f32[560,128]{1,0:T(8,128)}, u32[]{:S(2)}) copy-start(f32[560,128]{1,0:T(8,128)} %get-tuple-element.13.pay) | copy-start | bytes 860164
  7.4 1.5 %copy-start.4 = (s32[24,128]{1,0:T(8,128)S(1)}, s32[24,128]{1,0:T(8,128)}, u32[]{:S(2)}) copy-start(s32[24,128]{1,0:T(8,128)} %get-tuple-element.12) | copy-start | bytes 36868
  11.5 8.4 %copy-start.1 = (f32[16,8,4096]{2,1,0:T(8,128)S(1)}, f32[16,8,4096]{2,1,0:T(8,128)}, u32[]{:S(2)}) copy-start(f32[16,8,4096]{2,1,0:T(8,128)} %param.10) | copy-start | bytes 6291460
  11.5 8.4 %copy-start.5 = (f32[16]{0:T(128)S(1)}, f32[16]{0:T(128)}, u32[]{:S(2)}) copy-start(f32[16]{0:T(128)} %occ.1) | copy-start | bytes 196
  19.2 3.2 %collective-permute-start.2 = (f32[16,128]{1,0:T(8,128)S(1)}, f32[16,128]{1,0:T(8,128)S(1)}, u32[]{:S(2)}, u32[]{:S(2)}) collective-permute-start(f32[16,128]{1,0:T(8,128)S(1)} %get-tuple-element.14.after), channel_id=1, source_target_pairs={{1,0},{2,1},{3,2},{4,3},{5,4},{6,5},{7,6},{8,7},{9,8},{10,9},{11,1... | collective-permute-start | bytes 24584 | tf_op jit(solution)/shard_map/ppermute | solution.py:384
  19.7 17.1 %copy-start.11 = (s32[8]{0:T(128)S(1)}, s32[8]{0:T(128)}, u32[]{:S(2)}) copy-start(s32[8]{0:T(128)} %sizes_in.1) | copy-start | bytes 100
  19.8 17.2 %copy-start.8 = (f32[8,9,512]{2,0,1:T(8,128)S(1)}, f32[8,9,512]{2,0,1:T(8,128)}, u32[]{:S(2)}) copy-start(f32[8,9,512]{2,0,1:T(8,128)} %param.13) | copy-start | bytes 442372
  19.8 27.1 %copy-start.3 = (s32[8,512]{1,0:T(8,128)S(1)}, s32[8,512]{1,0:T(8,128)}, u32[]{:S(2)}) copy-start(s32[8,512]{1,0:T(8,128)} %offsets.1) | copy-start | bytes 49156
  19.8 28.7 %copy-start.6 = (f32[8,16,13,13]{3,1,0,2:T(8,128)S(1)}, f32[8,16,13,13]{3,1,0,2:T(8,128)}, u32[]{:S(2)}) copy-start(f32[8,16,13,13]{3,1,0,2:T(8,128)} %constant.21.clone) | copy-start | bytes 259588
  19.8 5.3 %collective-permute-start.3 = (f32[16,128]{1,0:T(8,128)S(1)}, f32[16,128]{1,0:T(8,128)S(1)}, u32[]{:S(2)}, u32[]{:S(2)}) collective-permute-start(f32[16,128]{1,0:T(8,128)S(1)} %get-tuple-element.16), channel_id=1, source_target_pairs={{0,1},{1,2},{2,3},{3,4},{4,5},{5,6},{6,7},{7,8},{8,9},{9,10},{10,1... | collective-permute-start | bytes 24584 | tf_op jit(solution)/shard_map/ppermute | solution.py:385
  26.1 20.8 %all-to-all-start = ((f32[16,24,128]{2,1,0:T(8,128)}), f32[16,24,128]{2,1,0:T(8,128)S(1)}, u32[]{:S(2)}, u32[]{:S(2)}) async-start(f32[16,24,128]{2,1,0:T(8,128)} %partial_matrices.1), calls=%async_computation | async-start | bytes 393216 | tf_op jit(solution)/shard_map/all_to_all | solution.py:415
  47.9 2.2 %collective-permute-start.4 = (f32[8,256]{1,0:T(8,128)S(1)}, f32[8,256]{1,0:T(8,128)S(1)}, u32[]{:S(2)}, u32[]{:S(2)}) collective-permute-start(f32[8,256]{1,0:T(8,128)S(1)} %get-tuple-element.19), channel_id=1, source_target_pairs={{1,0},{2,1},{3,2},{4,3},{5,4},{6,5},{7,6},{8,7},{9,8},{10,9},{11,1... | collective-permute-start | bytes 24584 | tf_op jit(solution)/shard_map/ppermute | solution.py:440
  48.0 5.3 %collective-permute-start.5 = (f32[8,256]{1,0:T(8,128)S(1)}, f32[8,256]{1,0:T(8,128)S(1)}, u32[]{:S(2)}, u32[]{:S(2)}) collective-permute-start(f32[8,256]{1,0:T(8,128)S(1)} %get-tuple-element.20), channel_id=1, source_target_pairs={{0,1},{1,2},{2,3},{3,4},{4,5},{5,6},{6,7},{7,8},{8,9},{9,10},{10,1... | collective-permute-start | bytes 24584 | tf_op jit(solution)/shard_map/ppermute | solution.py:441

commit v10 on v9

--- a/solution.py
+++ b/solution.py
@@ -53,6 +53,16 @@
     return points[at], points[at + LANES - 1]
 
 
+def one_hot(values):
+    wide = jnp.broadcast_to(values, (16, values.shape[1])).astype(BF16)
+    row = lax.broadcasted_iota(jnp.int32, wide.shape, 0)
+    one, zero = jnp.ones_like(wide), jnp.zeros_like(wide)
+    return jnp.concatenate(
+        [jnp.where(wide == (row + k).astype(F32).astype(BF16), one, zero) for k in range(0, 256, 16)],
+        axis=0,
+    )
+
+
 def project(pay, rows, shift, planes, tiles, atoms=range(ATOM_DEV)):
     width = len(tiles) * LANES
     span = len(planes) * 16
@@ -66,15 +76,15 @@
         block = jnp.concatenate(
             [pay[(a * TILES + t) * 16 : (a * TILES + t + 1) * 16, :] for t in tiles], axis=1
         )
-        plane = block[15:16, :].astype(jnp.int32) + shift
+        plane = jnp.broadcast_to(block[15:16, :] + float(shift), (16, width)).astype(BF16)
         proj = jnp.where(sub < NI, block, 0.0)
-        high = proj.astype(BF16).astype(F32)
-        low = proj - high
+        high = proj.astype(BF16)
+        low = (proj - high.astype(F32)).astype(BF16)
         pieces = []
         for piece in (high, low):
             for z in planes:
-                pieces.append(jnp.where(plane == z, piece, 0.0))
-        left = jnp.concatenate(pieces, axis=0).astype(BF16)
+                pieces.append(jnp.where(plane == jnp.full_like(plane, z), piece, jnp.zeros_like(piece)))
+        left = jnp.concatenate(pieces, axis=0)
         gathered = jnp.concatenate(
             [rows[a * SPHERE + t * LANES : a * SPHERE + (t + 1) * LANES, :] for t in tiles], axis=0
         )
@@ -140,6 +150,7 @@
         jnp.where(own, n_below + rank[8:16] - 1, SPHERE - rank[16:24]),
     )
     place = jnp.where(live, (place >> 1) + (place & 1) * WORDS, -1)
+    halves = [jnp.where(place >> 8 == h, place & 255, -1).astype(F32) for h in range(SPHERE // 256)]
     copies[2].wait()
     table = jnp.concatenate(
         [
@@ -155,7 +166,7 @@
     for a in range(ATOM_DEV):
         high = table[a].astype(BF16)
         low = (table[a] - high.astype(F32)).astype(BF16)
-        move = jnp.where(before == place[a : a + 1, :], 1.0, 0.0).astype(BF16)
+        move = jnp.concatenate([one_hot(v[a : a + 1, :]) for v in halves], axis=0)
         moved = lax.dot_general(
             jnp.concatenate([high, low], axis=0),
             move,
@@ -293,9 +304,9 @@
     c3 = comp - c1 - c2
     plane = offsets[...] >> 12
     column = (offsets[...] & (PLANE - 1)) - start[0]
+    column = jnp.where((column >= 0) & (column < 256), column, -1).astype(F32)
     row = lax.broadcasted_iota(jnp.int32, (24, SPHERE), 0)
     target = jnp.where(row < 8, row + HALO, jnp.where(row < 16, row - 11, row - 3))
-    col = lax.broadcasted_iota(jnp.int32, (256, SPHERE), 0)
     acc = jnp.zeros((80, 256), F32)
     for a in range(ATOM_DEV):
         here = target == plane[a : a + 1, :]
@@ -304,7 +315,7 @@
             + [jnp.zeros((8, SPHERE), F32)],
             axis=0,
         ).astype(BF16)
-        right = jnp.where(col == column[a : a + 1, :], 1.0, 0.0).astype(BF16)
+        right = one_hot(column[a : a + 1, :])
         acc = acc + lax.dot_general(
             left, right, (((1,), (1,)), ((), ())), preferred_element_type=F32
         )

time: 54 us -> 53.8 us (level)
  Pallas kernels: 14.2 us -> 15.1 us
  waiting for transfers between devices: 20 us -> 19.2 us
    ppermute x1, waiting for transfers between devices: 2.67 us -> 1.97 us  [local(): back_lo = lax.ppermute(q_hi, 'slab', to_next)]
    ppermute x1, starting transfers between devices: 0.59 us -> 0.01 us  [local(): back_hi = lax.ppermute(q_lo, 'slab', to_prev)]
  transfers between devices with their start and end apart: 7 -> 7, of which waited for: 5 -> 5; matrix products, arithmetic and copies ran while one was open for 4% -> 4% of each run, Pallas kernels for 10% -> 11%
where the time goes in v10:
time: 53.8 us; the launch traced here: 53.7 us
  waiting for transfers between devices  19.2 us (36%)
  starting transfers between devices  15.3 us (28%)
  Pallas kernels  15.1 us (28%)
  matrix products  1.69 us (3%)
  local copies, waits for them, and re-layouts  0.92 us (2%)
  other arithmetic  0.8 us (1%)
  between operations  0.8 us (1%)
    all_to_all x1, starting transfers between devices, local(): recv = lax.all_to_all(packed, 'band', 0, 0)  10.8 us
    all_to_all x1, waiting for transfers between devices, local(): recv = lax.all_to_all(packed, 'band', 0, 0)  9.94 us
    ppermute x1, waiting for transfers between devices, local(): pay_lo = lax.ppermute(pay, 'slab', to_next)  3.9 us
    pallas_call x1, Pallas kernels, local(): pl.pallas_call(side_kernel, out_shape=(shape(BANDS, LANES), shape(BANDS,...  3.84 us
    ppermute x1, starting transfers between devices, local(): pay_hi = lax.ppermute(pay, 'slab', to_prev)  3.46 us
    pallas_call x1, Pallas kernels, local(): pl.pallas_call(sort_kernel, out_shape=(shape(SORTED + 2 * LIST, LANES), j...  3.28 us
    ppermute x1, waiting for transfers between devices, local(): from_below = lax.ppermute(up, 'slab', to_next)  3.07 us
    pallas_call x1, Pallas kernels, local(): pl.pallas_call(late_kernel, out_shape=(shape(16, 24, LANES), shape(BANDS,...  2.72 us
  transfers between devices with their start and end apart: 7, of which 5 were waited for; matrix products, arithmetic and copies ran while one was open for 4% of the time, Pallas kernels for 11%

profile of v10, /device:TPU:32, one launch (start us, length us, event | category | flops | bytes accessed | tf_op | source)
XLA Modules:
  0.0 53.7 jit_solution(15538242872021841848)
XLA Ops:
  0.6 0.0 copy-start
  0.6 3.3 %sort_points.1 = (f32[560,128]{1,0:T(8,128)}, s32[24,128]{1,0:T(8,128)}) custom-call(s32[8]{0:T(128)} %sizes_in.1, s32[8,512]{1,0:T(8,128)} %offsets.1, f32[13,8,512]{2,1,0:T(8,128)} %bitcast.25), custom_call_target="tpu_custom_call" | custom-call | flops 1000000000 | bytes 8388608 | tf_op jit(solution)/shard_map/sort_points/pallas_call | solution.py:346
  3.9 3.5 %collective-permute-start.1 = (f32[560,128]{1,0:T(8,128)}, f32[560,128]{1,0:T(8,128)S(1)}, u32[]{:S(2)}, u32[]{:S(2)}) collective-permute-start(f32[560,128]{1,0:T(8,128)} %get-tuple-element.13.pay), channel_id=1, source_target_pairs={{1,0},{2,1},{3,2},{4,3},{5,4},{6,5},{7,6},{8,7},{9,8},{10,9},{11,1... | collective-permute-start | bytes 860168 | tf_op jit(solution)/shard_map/ppermute | solution.py:365
  7.4 0.0 collective-permute-start
  7.4 0.0 copy-done
  7.4 0.0 copy-start.7
  7.4 0.0 copy-start.9
  7.4 0.0 copy-start.10
  7.4 0.0 copy-start.2
  7.4 0.0 copy-start.4
  7.4 0.6 %grid_table.1.table = f32[4096,128]{1,0:T(8,128)S(1)} custom-call(f32[128,4096]{1,0:T(8,128)S(1)} %bitcast.20), custom_call_target="tpu_custom_call" | custom-call | bytes 8388608 | tf_op jit(solution)/shard_map/grid_table/pallas_call | solution.py:337
  8.0 0.2 copy-done.7
  8.3 0.1 copy.14
  8.4 0.0 copy-done.9
  8.4 0.1 slice.28
  8.5 0.0 copy-done.10
  8.5 0.1 pad_select_fusion
  8.6 0.1 copy.15
  8.7 0.1 tile.10.coupling
  8.9 0.0 copy-done.2
  8.9 0.0 copy-done.4
  8.9 2.7 %own_points_early.1.q0 = f32[16,128]{1,0:T(8,128)S(1)} custom-call(s32[3072]{0:T(1024)S(1)} %bitcast.22, f32[4096,128]{1,0:T(8,128)S(1)} %grid_table.1.table, f32[560,128]{1,0:T(8,128)S(1)} %copy-done.2), custom_call_target="tpu_custom_call" | custom-call | flops 1000000000 | bytes 8388608 | tf_op jit(solution)/shard_map/own_points_early/pallas_call | solution.py:369
  11.6 0.0 copy-start.1
  11.6 0.0 copy-start.5
  11.6 0.3 collective-permute-done.1.pay_hi
  11.9 3.9 %collective-permute-done.pay_lo = f32[560,128]{1,0:T(8,128)S(1)} collective-permute-done((f32[560,128]{1,0:T(8,128)}, f32[560,128]{1,0:T(8,128)S(1)}, u32[]{:S(2)}, u32[]{:S(2)}) %collective-permute-start) | collective-permute-done | bytes 286752 | tf_op jit(solution)/shard_map/ppermute | solution.py:364
  15.8 3.8 %side_points.1 = (f32[16,128]{1,0:T(8,128)S(1)}, f32[16,128]{1,0:T(8,128)S(1)}) custom-call(s32[3072]{0:T(1024)S(1)} %fusion.5.list_lo, s32[3072]{0:T(1024)S(1)} %fusion.2.list_hi, f32[4096,128]{1,0:T(8,128)S(1)} %grid_table.1.table, f32[560,128]{1,0:T(8,128)S(1)} %collective-permute-done.pay_lo, f32[560,128]{1,0:T(8,128)S(1)} %collective-permute-done.1.pay_hi), custom_call_target="tpu_custom_call" | custom-call | tf_op jit(solution)/shard_map/side_points/pallas_call | solution.py:380
  19.6 0.0 collective-permute-start.2
  19.6 0.0 copy-start.11
  19.6 0.0 copy-start.8
  19.7 0.0 copy-start.3
  19.7 0.0 copy-start.6
  19.7 0.6 %collective-permute-start.3 = (f32[16,128]{1,0:T(8,128)S(1)}, f32[16,128]{1,0:T(8,128)S(1)}, u32[]{:S(2)}, u32[]{:S(2)}) collective-permute-start(f32[16,128]{1,0:T(8,128)S(1)} %get-tuple-element.16), channel_id=1, source_target_pairs={{0,1},{1,2},{2,3},{3,4},{4,5},{5,6},{6,7},{7,8},{8,9},{9,10},{10,1... | collective-permute-start | bytes 24584 | tf_op jit(solution)/shard_map/ppermute | solution.py:396
  20.2 0.0 copy-done.1
  20.2 0.0 copy-done.5
  20.2 2.7 %own_points_late.1 = (f32[16,24,128]{2,1,0:T(8,128)}, f32[16,128]{1,0:T(8,128)S(1)}) custom-call(s32[3072]{0:T(1024)S(1)} %bitcast.23, f32[16]{0:T(128)S(1)} %copy-done.5, f32[128,4096]{1,0:T(8,128)S(1)} %bitcast.21, f32[4096,128]{1,0:T(8,128)S(1)} %grid_table.1.table, f32[560,128]{1,0:T(8,128)S(1)} %copy-done.2, f32[16,128]{1,0:T(8,128)S(1)} %get-tuple-element.14.after), custom_call_target="tpu_custom_call" | custom-call | flops 1000000000 | bytes 8388608 | tf_op jit(solution)/shard_map/own_points_late/pallas_call | solution.py:398
  23.0 0.0 collective-permute-done.2.q2
  23.0 2.0 %collective-permute-done.3.q3 = f32[16,128]{1,0:T(8,128)S(1)} collective-permute-done((f32[16,128]{1,0:T(8,128)S(1)}, f32[16,128]{1,0:T(8,128)S(1)}, u32[]{:S(2)}, u32[]{:S(2)}) %collective-permute-start.3) | collective-permute-done | bytes 8224 | tf_op jit(solution)/shard_map/ppermute | solution.py:396
  24.9 0.1 broadcast_in_dim.29.occ
  25.0 1.0 %partial_matrices.1 = f32[16,24,128]{2,1,0:T(8,128)} custom-call(f32[16,128]{1,0:T(8,128)S(1)} %own_points_early.1.q0, f32[16,128]{1,0:T(8,128)S(1)} %get-tuple-element.15.q1, f32[16,128]{1,0:T(8,128)S(1)} %collective-permute-done.2.q2, f32[16,128]{1,0:T(8,128)S(1)} %collective-permute-done.3.q3, ...), custom_call_target="tpu_custom_call", output_to_operand_aliasing={{}: (5, {})} | custom-call | tf_op jit(solution)/shard_map/partial_matrices/pallas_call | solution.py:409
  26.0 10.8 %all-to-all-start = ((f32[16,24,128]{2,1,0:T(8,128)}), f32[16,24,128]{2,1,0:T(8,128)S(1)}, u32[]{:S(2)}, u32[]{:S(2)}) async-start(f32[16,24,128]{2,1,0:T(8,128)} %partial_matrices.1), calls=%async_computation | async-start | bytes 393216 | tf_op jit(solution)/shard_map/all_to_all | solution.py:426
  36.8 0.0 copy-done.11
  36.8 0.1 iota_compare_fusion
  36.8 0.0 copy-done.8
  36.9 9.9 %all-to-all-done.recv = f32[16,24,128]{2,1,0:T(8,128)S(1)} async-done(((f32[16,24,128]{2,1,0:T(8,128)}), f32[16,24,128]{2,1,0:T(8,128)S(1)}, u32[]{:S(2)}, u32[]{:S(2)}) %all-to-all-start) | async-done | bytes 196640 | tf_op jit(solution)/shard_map/all_to_all | solution.py:426
  46.8 0.0 copy-done.3
  46.8 0.9 %charges.1 = (f32[8,256]{1,0:T(8,128)S(1)}, f32[8,256]{1,0:T(8,128)S(1)}, f32[8,256]{1,0:T(8,128)S(1)}, f32[8,128]{1,0:T(8,128)S(1)}) custom-call(s32[1]{0:T(128)} %bitcast.start, f32[16,24,128]{2,1,0:T(8,128)S(1)} %all-to-all-done.recv, f32[9,8,128]{2,1,0:T(8,128)S(1)} %tile.10.coupling, f32[9,8,512]{2,1,0:T(8,128)S(1)} %select_bitcast_fusion.shapes, ...), custom_call_target="tpu_custom_call" | custom-call | tf_op jit(solution)/shard_map/charges/pallas_call | solution.py:443
  47.8 0.1 reshape.50
  47.8 0.0 collective-permute-start.4
  47.9 0.5 collective-permute-start.5
  48.4 0.0 copy-done.6
  48.4 1.7 %convolution_bitcast_fusion = f32[8,13,13]{2,0,1:T(8,128)} fusion(f32[8,8,16,1]{2,1,0,3:T(8,128)S(1)} %reshape.50, f32[8,16,13,13]{3,1,0,2:T(8,128)S(1)} %copy-done.6), kind=kOutput, calls=%fused_computation | convolution fusion | flops 2076672 | bytes 96032 | tf_op jit(solution)/shard_map/paq,pqij->aij/dot_general | solution.py:454
  50.1 0.0 collective-permute-done.4
  50.1 3.1 %collective-permute-done.5 = f32[8,256]{1,0:T(8,128)S(1)} collective-permute-done((f32[8,256]{1,0:T(8,128)S(1)}, f32[8,256]{1,0:T(8,128)S(1)}, u32[]{:S(2)}, u32[]{:S(2)}) %collective-permute-start.5) | collective-permute-done | bytes 8224 | tf_op jit(solution)/shard_map/ppermute | solution.py:452
  53.1 0.6 %add_add_fusion = f32[8,256]{1,0:T(8,128)} fusion(f32[8,256]{1,0:T(8,128)S(1)} %collective-permute-done.5, f32[8,256]{1,0:T(8,128)S(1)} %get-tuple-element.18, f32[8,256]{1,0:T(8,128)S(1)} %collective-permute-done.4), kind=kLoop, calls=%fused_computation.13 | loop fusion | flops 4096 | bytes 32768 | tf_op jit(solution)/shard_map/add | solution.py:453
  (5 shorter events, 0.1 us)
Async XLA Ops:
  0.6 6.8 %copy-start = (f32[16,8,4096]{2,1,0:T(8,128)S(1)}, f32[16,8,4096]{2,1,0:T(8,128)}, u32[]{:S(2)}) copy-start(f32[16,8,4096]{2,1,0:T(8,128)} %param.10) | copy-start | bytes 6291460
  3.9 7.9 %collective-permute-start.1 = (f32[560,128]{1,0:T(8,128)}, f32[560,128]{1,0:T(8,128)S(1)}, u32[]{:S(2)}, u32[]{:S(2)}) collective-permute-start(f32[560,128]{1,0:T(8,128)} %get-tuple-element.13.pay), channel_id=1, source_target_pairs={{1,0},{2,1},{3,2},{4,3},{5,4},{6,5},{7,6},{8,7},{9,8},{10,9},{11,1... | collective-permute-start | bytes 860168 | tf_op jit(solution)/shard_map/ppermute | solution.py:365
  7.4 8.4 %collective-permute-start = (f32[560,128]{1,0:T(8,128)}, f32[560,128]{1,0:T(8,128)S(1)}, u32[]{:S(2)}, u32[]{:S(2)}) collective-permute-start(f32[560,128]{1,0:T(8,128)} %get-tuple-element.13.pay), channel_id=1, source_target_pairs={{0,1},{1,2},{2,3},{3,4},{4,5},{5,6},{6,7},{7,8},{8,9},{9,10},{10,1... | collective-permute-start | bytes 860168 | tf_op jit(solution)/shard_map/ppermute | solution.py:364
  7.4 0.9 %copy-start.7 = (f32[9,13,13]{2,1,0:T(8,128)S(1)}, f32[9,13,13]{2,1,0:T(8,128)}, u32[]{:S(2)}) copy-start(f32[9,13,13]{2,1,0:T(8,128)} %param.14) | copy-start | bytes 18256
  7.4 1.0 %copy-start.9 = (pred[13,13]{0,1:T(8,128)(4,1)S(1)}, pred[13,13]{0,1:T(8,128)(4,1)}, u32[]{:S(2)}) copy-start(pred[13,13]{0,1:T(8,128)(4,1)} %constant.19.clone) | copy-start | bytes 511
  7.4 1.1 %copy-start.10 = (pred[8,16]{0,1:T(8,128)(4,1)S(1)}, pred[8,16]{0,1:T(8,128)(4,1)}, u32[]{:S(2)}) copy-start(pred[8,16]{0,1:T(8,128)(4,1)} %constant.20.clone) | copy-start | bytes 388
  7.4 1.5 %copy-start.2 = (f32[560,128]{1,0:T(8,128)S(1)}, f32[560,128]{1,0:T(8,128)}, u32[]{:S(2)}) copy-start(f32[560,128]{1,0:T(8,128)} %get-tuple-element.13.pay) | copy-start | bytes 860164
  7.4 1.5 %copy-start.4 = (s32[24,128]{1,0:T(8,128)S(1)}, s32[24,128]{1,0:T(8,128)}, u32[]{:S(2)}) copy-start(s32[24,128]{1,0:T(8,128)} %get-tuple-element.12) | copy-start | bytes 36868
  11.6 8.7 %copy-start.1 = (f32[16,8,4096]{2,1,0:T(8,128)S(1)}, f32[16,8,4096]{2,1,0:T(8,128)}, u32[]{:S(2)}) copy-start(f32[16,8,4096]{2,1,0:T(8,128)} %param.10) | copy-start | bytes 6291460
  11.6 8.7 %copy-start.5 = (f32[16]{0:T(128)S(1)}, f32[16]{0:T(128)}, u32[]{:S(2)}) copy-start(f32[16]{0:T(128)} %occ.1) | copy-start | bytes 196
  19.6 3.4 %collective-permute-start.2 = (f32[16,128]{1,0:T(8,128)S(1)}, f32[16,128]{1,0:T(8,128)S(1)}, u32[]{:S(2)}, u32[]{:S(2)}) collective-permute-start(f32[16,128]{1,0:T(8,128)S(1)} %get-tuple-element.14.after), channel_id=1, source_target_pairs={{1,0},{2,1},{3,2},{4,3},{5,4},{6,5},{7,6},{8,7},{9,8},{10,9},{11,1... | collective-permute-start | bytes 24584 | tf_op jit(solution)/shard_map/ppermute | solution.py:395
  19.6 17.1 %copy-start.11 = (s32[8]{0:T(128)S(1)}, s32[8]{0:T(128)}, u32[]{:S(2)}) copy-start(s32[8]{0:T(128)} %sizes_in.1) | copy-start | bytes 100
  19.6 17.2 %copy-start.8 = (f32[8,9,512]{2,0,1:T(8,128)S(1)}, f32[8,9,512]{2,0,1:T(8,128)}, u32[]{:S(2)}) copy-start(f32[8,9,512]{2,0,1:T(8,128)} %param.13) | copy-start | bytes 442372
  19.7 27.1 %copy-start.3 = (s32[8,512]{1,0:T(8,128)S(1)}, s32[8,512]{1,0:T(8,128)}, u32[]{:S(2)}) copy-start(s32[8,512]{1,0:T(8,128)} %offsets.1) | copy-start | bytes 49156
  19.7 28.7 %copy-start.6 = (f32[8,16,13,13]{3,1,0,2:T(8,128)S(1)}, f32[8,16,13,13]{3,1,0,2:T(8,128)}, u32[]{:S(2)}) copy-start(f32[8,16,13,13]{3,1,0,2:T(8,128)} %constant.21.clone) | copy-start | bytes 259588
  19.7 5.3 %collective-permute-start.3 = (f32[16,128]{1,0:T(8,128)S(1)}, f32[16,128]{1,0:T(8,128)S(1)}, u32[]{:S(2)}, u32[]{:S(2)}) collective-permute-start(f32[16,128]{1,0:T(8,128)S(1)} %get-tuple-element.16), channel_id=1, source_target_pairs={{0,1},{1,2},{2,3},{3,4},{4,5},{5,6},{6,7},{7,8},{8,9},{9,10},{10,1... | collective-permute-start | bytes 24584 | tf_op jit(solution)/shard_map/ppermute | solution.py:396
  26.0 20.8 %all-to-all-start = ((f32[16,24,128]{2,1,0:T(8,128)}), f32[16,24,128]{2,1,0:T(8,128)S(1)}, u32[]{:S(2)}, u32[]{:S(2)}) async-start(f32[16,24,128]{2,1,0:T(8,128)} %partial_matrices.1), calls=%async_computation | async-start | bytes 393216 | tf_op jit(solution)/shard_map/all_to_all | solution.py:426
  47.8 2.2 %collective-permute-start.4 = (f32[8,256]{1,0:T(8,128)S(1)}, f32[8,256]{1,0:T(8,128)S(1)}, u32[]{:S(2)}, u32[]{:S(2)}) collective-permute-start(f32[8,256]{1,0:T(8,128)S(1)} %get-tuple-element.19), channel_id=1, source_target_pairs={{1,0},{2,1},{3,2},{4,3},{5,4},{6,5},{7,6},{8,7},{9,8},{10,9},{11,1... | collective-permute-start | bytes 24584 | tf_op jit(solution)/shard_map/ppermute | solution.py:451
  47.9 5.3 %collective-permute-start.5 = (f32[8,256]{1,0:T(8,128)S(1)}, f32[8,256]{1,0:T(8,128)S(1)}, u32[]{:S(2)}, u32[]{:S(2)}) collective-permute-start(f32[8,256]{1,0:T(8,128)S(1)} %get-tuple-element.20), channel_id=1, source_target_pairs={{0,1},{1,2},{2,3},{3,4},{4,5},{5,6},{6,7},{7,8},{8,9},{9,10},{10,1... | collective-permute-start | bytes 24584 | tf_op jit(solution)/shard_map/ppermute | solution.py:452

commit v11 on v10

--- a/solution.py
+++ b/solution.py
@@ -53,14 +53,9 @@
     return points[at], points[at + LANES - 1]
 
 
-def one_hot(values):
-    wide = jnp.broadcast_to(values, (16, values.shape[1])).astype(BF16)
-    row = lax.broadcasted_iota(jnp.int32, wide.shape, 0)
-    one, zero = jnp.ones_like(wide), jnp.zeros_like(wide)
-    return jnp.concatenate(
-        [jnp.where(wide == (row + k).astype(F32).astype(BF16), one, zero) for k in range(0, 256, 16)],
-        axis=0,
-    )
+def one_hot(column, width):
+    place = lax.broadcasted_iota(jnp.int32, (column.shape[0], width), 1).astype(F32)
+    return jnp.where(column == place, 1.0, 0.0).astype(BF16)
 
 
 def project(pay, rows, shift, planes, tiles, atoms=range(ATOM_DEV)):
@@ -150,7 +145,7 @@
         jnp.where(own, n_below + rank[8:16] - 1, SPHERE - rank[16:24]),
     )
     place = jnp.where(live, (place >> 1) + (place & 1) * WORDS, -1)
-    halves = [jnp.where(place >> 8 == h, place & 255, -1).astype(F32) for h in range(SPHERE // 256)]
+    place = jnp.transpose(place.astype(F32))
     copies[2].wait()
     table = jnp.concatenate(
         [
@@ -166,12 +161,9 @@
     for a in range(ATOM_DEV):
         high = table[a].astype(BF16)
         low = (table[a] - high.astype(F32)).astype(BF16)
-        move = jnp.concatenate([one_hot(v[a : a + 1, :]) for v in halves], axis=0)
-        moved = lax.dot_general(
-            jnp.concatenate([high, low], axis=0),
-            move,
-            (((1,), (1,)), ((), ())),
-            preferred_element_type=F32,
+        move = one_hot(place[:, a : a + 1], SPHERE)
+        moved = jnp.dot(
+            jnp.concatenate([high, low], axis=0), move, preferred_element_type=F32
         )
         moved = moved[0:16] + moved[16:32]
         first = a * TILES * 16
@@ -304,7 +296,7 @@
     c3 = comp - c1 - c2
     plane = offsets[...] >> 12
     column = (offsets[...] & (PLANE - 1)) - start[0]
-    column = jnp.where((column >= 0) & (column < 256), column, -1).astype(F32)
+    column = jnp.transpose(column.astype(F32))
     row = lax.broadcasted_iota(jnp.int32, (24, SPHERE), 0)
     target = jnp.where(row < 8, row + HALO, jnp.where(row < 16, row - 11, row - 3))
     acc = jnp.zeros((80, 256), F32)
@@ -315,10 +307,8 @@
             + [jnp.zeros((8, SPHERE), F32)],
             axis=0,
         ).astype(BF16)
-        right = one_hot(column[a : a + 1, :])
-        acc = acc + lax.dot_general(
-            left, right, (((1,), (1,)), ((), ())), preferred_element_type=F32
-        )
+        right = one_hot(column[:, a : a + 1], 256)
+        acc = acc + jnp.dot(left, right, preferred_element_type=F32)
     placed = acc[0:24] + acc[24:48] + acc[48:72]
     core[...] = placed[0:8] + jnp.concatenate([total[0:8], total[8:16]], axis=1)
     down[...] = placed[8:16]

time: 53.8 us -> 53.5 us (level)
  no operation moved by 1% of the time
where the time goes in v11:
time: 53.5 us; the launch traced here: 53.4 us
  waiting for transfers between devices  19.3 us (36%)
  starting transfers between devices  15.4 us (29%)
  Pallas kernels  14.6 us (27%)
  matrix products  1.69 us (3%)
  local copies, waits for them, and re-layouts  0.89 us (2%)
  other arithmetic  0.8 us (1%)
  between operations  0.78 us (1%)
    all_to_all x1, starting transfers between devices, local(): recv = lax.all_to_all(packed, 'band', 0, 0)  10.8 us
    all_to_all x1, waiting for transfers between devices, local(): recv = lax.all_to_all(packed, 'band', 0, 0)  9.94 us
    ppermute x1, waiting for transfers between devices, local(): pay_lo = lax.ppermute(pay, 'slab', to_next)  3.9 us
    pallas_call x1, Pallas kernels, local(): pl.pallas_call(side_kernel, out_shape=(shape(BANDS, LANES), shape(BANDS,...  3.65 us
    ppermute x1, starting transfers between devices, local(): pay_hi = lax.ppermute(pay, 'slab', to_prev)  3.46 us
    ppermute x1, waiting for transfers between devices, local(): from_below = lax.ppermute(up, 'slab', to_next)  3.07 us
    pallas_call x1, Pallas kernels, local(): pl.pallas_call(sort_kernel, out_shape=(shape(SORTED + 2 * LIST, LANES), j...  2.94 us
    pallas_call x1, Pallas kernels, local(): pl.pallas_call(late_kernel, out_shape=(shape(16, 24, LANES), shape(BANDS,...  2.76 us
  transfers between devices with their start and end apart: 7, of which 5 were waited for; matrix products, arithmetic and copies ran while one was open for 4% of the time, Pallas kernels for 11%

profile of v11, /device:TPU:32, one launch (start us, length us, event | category | flops | bytes accessed | tf_op | source)
XLA Modules:
  0.0 53.4 jit_solution(10831804267923738860)
XLA Ops:
  0.6 0.0 copy-start
  0.6 2.9 %sort_points.1 = (f32[560,128]{1,0:T(8,128)}, s32[24,128]{1,0:T(8,128)}) custom-call(s32[8]{0:T(128)} %sizes_in.1, s32[8,512]{1,0:T(8,128)} %offsets.1, f32[13,8,512]{2,1,0:T(8,128)} %bitcast.25), custom_call_target="tpu_custom_call" | custom-call | flops 1000000000 | bytes 8388608 | tf_op jit(solution)/shard_map/sort_points/pallas_call | solution.py:336
  3.6 3.5 %collective-permute-start.1 = (f32[560,128]{1,0:T(8,128)}, f32[560,128]{1,0:T(8,128)S(1)}, u32[]{:S(2)}, u32[]{:S(2)}) collective-permute-start(f32[560,128]{1,0:T(8,128)} %get-tuple-element.13.pay), channel_id=1, source_target_pairs={{1,0},{2,1},{3,2},{4,3},{5,4},{6,5},{7,6},{8,7},{9,8},{10,9},{11,1... | collective-permute-start | bytes 860168 | tf_op jit(solution)/shard_map/ppermute | solution.py:355
  7.0 0.0 collective-permute-start
  7.0 0.0 copy-done
  7.1 0.0 copy-start.7
  7.1 0.0 copy-start.9
  7.1 0.0 copy-start.10
  7.1 0.0 copy-start.2
  7.1 0.0 copy-start.4
  7.1 0.6 %grid_table.1.table = f32[4096,128]{1,0:T(8,128)S(1)} custom-call(f32[128,4096]{1,0:T(8,128)S(1)} %bitcast.20), custom_call_target="tpu_custom_call" | custom-call | bytes 8388608 | tf_op jit(solution)/shard_map/grid_table/pallas_call | solution.py:327
  7.7 0.2 copy-done.7
  7.9 0.1 copy.14
  8.1 0.0 copy-done.9
  8.1 0.1 slice.28
  8.2 0.0 copy-done.10
  8.2 0.1 pad_select_fusion
  8.3 0.1 copy.15
  8.4 0.1 tile.10.coupling
  8.5 0.0 copy-done.2
  8.5 0.0 copy-done.4
  8.6 2.7 %own_points_early.1.q0 = f32[16,128]{1,0:T(8,128)S(1)} custom-call(s32[3072]{0:T(1024)S(1)} %bitcast.22, f32[4096,128]{1,0:T(8,128)S(1)} %grid_table.1.table, f32[560,128]{1,0:T(8,128)S(1)} %copy-done.2), custom_call_target="tpu_custom_call" | custom-call | flops 1000000000 | bytes 8388608 | tf_op jit(solution)/shard_map/own_points_early/pallas_call | solution.py:359
  11.3 0.0 copy-start.1
  11.3 0.0 copy-start.5
  11.3 0.2 collective-permute-done.1.pay_hi
  11.5 3.9 %collective-permute-done.pay_lo = f32[560,128]{1,0:T(8,128)S(1)} collective-permute-done((f32[560,128]{1,0:T(8,128)}, f32[560,128]{1,0:T(8,128)S(1)}, u32[]{:S(2)}, u32[]{:S(2)}) %collective-permute-start) | collective-permute-done | bytes 286752 | tf_op jit(solution)/shard_map/ppermute | solution.py:354
  15.4 3.7 %side_points.1 = (f32[16,128]{1,0:T(8,128)S(1)}, f32[16,128]{1,0:T(8,128)S(1)}) custom-call(s32[3072]{0:T(1024)S(1)} %fusion.5.list_lo, s32[3072]{0:T(1024)S(1)} %fusion.2.list_hi, f32[4096,128]{1,0:T(8,128)S(1)} %grid_table.1.table, f32[560,128]{1,0:T(8,128)S(1)} %collective-permute-done.pay_lo, f32[560,128]{1,0:T(8,128)S(1)} %collective-permute-done.1.pay_hi), custom_call_target="tpu_custom_call" | custom-call | tf_op jit(solution)/shard_map/side_points/pallas_call | solution.py:370
  19.1 0.2 collective-permute-start.2
  19.3 0.0 copy-start.11
  19.3 0.0 copy-start.8
  19.3 0.0 copy-start.3
  19.3 0.0 copy-start.6
  19.3 0.4 collective-permute-start.3
  19.7 0.0 copy-done.1
  19.7 0.0 copy-done.5
  19.7 2.8 %own_points_late.1 = (f32[16,24,128]{2,1,0:T(8,128)}, f32[16,128]{1,0:T(8,128)S(1)}) custom-call(s32[3072]{0:T(1024)S(1)} %bitcast.23, f32[16]{0:T(128)S(1)} %copy-done.5, f32[128,4096]{1,0:T(8,128)S(1)} %bitcast.21, f32[4096,128]{1,0:T(8,128)S(1)} %grid_table.1.table, f32[560,128]{1,0:T(8,128)S(1)} %copy-done.2, f32[16,128]{1,0:T(8,128)S(1)} %get-tuple-element.14.after), custom_call_target="tpu_custom_call" | custom-call | flops 1000000000 | bytes 8388608 | tf_op jit(solution)/shard_map/own_points_late/pallas_call | solution.py:388
  22.5 0.0 collective-permute-done.2.q2
  22.5 2.1 %collective-permute-done.3.q3 = f32[16,128]{1,0:T(8,128)S(1)} collective-permute-done((f32[16,128]{1,0:T(8,128)S(1)}, f32[16,128]{1,0:T(8,128)S(1)}, u32[]{:S(2)}, u32[]{:S(2)}) %collective-permute-start.3) | collective-permute-done | bytes 8224 | tf_op jit(solution)/shard_map/ppermute | solution.py:386
  24.6 0.1 broadcast_in_dim.29.occ
  24.7 1.0 %partial_matrices.1 = f32[16,24,128]{2,1,0:T(8,128)} custom-call(f32[16,128]{1,0:T(8,128)S(1)} %own_points_early.1.q0, f32[16,128]{1,0:T(8,128)S(1)} %get-tuple-element.15.q1, f32[16,128]{1,0:T(8,128)S(1)} %collective-permute-done.2.q2, f32[16,128]{1,0:T(8,128)S(1)} %collective-permute-done.3.q3, ...), custom_call_target="tpu_custom_call", output_to_operand_aliasing={{}: (5, {})} | custom-call | tf_op jit(solution)/shard_map/partial_matrices/pallas_call | solution.py:399
  25.7 10.8 %all-to-all-start = ((f32[16,24,128]{2,1,0:T(8,128)}), f32[16,24,128]{2,1,0:T(8,128)S(1)}, u32[]{:S(2)}, u32[]{:S(2)}) async-start(f32[16,24,128]{2,1,0:T(8,128)} %partial_matrices.1), calls=%async_computation | async-start | bytes 393216 | tf_op jit(solution)/shard_map/all_to_all | solution.py:416
  36.4 0.0 copy-done.11
  36.4 0.1 iota_compare_fusion
  36.5 0.0 copy-done.8
  36.5 9.9 %all-to-all-done.recv = f32[16,24,128]{2,1,0:T(8,128)S(1)} async-done(((f32[16,24,128]{2,1,0:T(8,128)}), f32[16,24,128]{2,1,0:T(8,128)S(1)}, u32[]{:S(2)}, u32[]{:S(2)}) %all-to-all-start) | async-done | bytes 196640 | tf_op jit(solution)/shard_map/all_to_all | solution.py:416
  46.5 0.0 copy-done.3
  46.5 1.0 %charges.1 = (f32[8,256]{1,0:T(8,128)S(1)}, f32[8,256]{1,0:T(8,128)S(1)}, f32[8,256]{1,0:T(8,128)S(1)}, f32[8,128]{1,0:T(8,128)S(1)}) custom-call(s32[1]{0:T(128)} %bitcast.start, f32[16,24,128]{2,1,0:T(8,128)S(1)} %all-to-all-done.recv, f32[9,8,128]{2,1,0:T(8,128)S(1)} %tile.10.coupling, f32[9,8,512]{2,1,0:T(8,128)S(1)} %select_bitcast_fusion.shapes, ...), custom_call_target="tpu_custom_call" | custom-call | tf_op jit(solution)/shard_map/charges/pallas_call | solution.py:433
  47.4 0.1 reshape.50
  47.5 0.0 collective-permute-start.4
  47.5 0.5 collective-permute-start.5
  48.0 0.0 copy-done.6
  48.0 1.7 %convolution_bitcast_fusion = f32[8,13,13]{2,0,1:T(8,128)} fusion(f32[8,8,16,1]{2,1,0,3:T(8,128)S(1)} %reshape.50, f32[8,16,13,13]{3,1,0,2:T(8,128)S(1)} %copy-done.6), kind=kOutput, calls=%fused_computation | convolution fusion | flops 2076672 | bytes 96032 | tf_op jit(solution)/shard_map/paq,pqij->aij/dot_general | solution.py:444
  49.7 0.0 collective-permute-done.4
  49.7 3.1 %collective-permute-done.5 = f32[8,256]{1,0:T(8,128)S(1)} collective-permute-done((f32[8,256]{1,0:T(8,128)S(1)}, f32[8,256]{1,0:T(8,128)S(1)}, u32[]{:S(2)}, u32[]{:S(2)}) %collective-permute-start.5) | collective-permute-done | bytes 8224 | tf_op jit(solution)/shard_map/ppermute | solution.py:442
  52.8 0.6 %add_add_fusion = f32[8,256]{1,0:T(8,128)} fusion(f32[8,256]{1,0:T(8,128)S(1)} %collective-permute-done.5, f32[8,256]{1,0:T(8,128)S(1)} %get-tuple-element.18, f32[8,256]{1,0:T(8,128)S(1)} %collective-permute-done.4), kind=kLoop, calls=%fused_computation.13 | loop fusion | flops 4096 | bytes 32768 | tf_op jit(solution)/shard_map/add | solution.py:443
  (5 shorter events, 0.1 us)
Async XLA Ops:
  0.6 6.4 %copy-start = (f32[16,8,4096]{2,1,0:T(8,128)S(1)}, f32[16,8,4096]{2,1,0:T(8,128)}, u32[]{:S(2)}) copy-start(f32[16,8,4096]{2,1,0:T(8,128)} %param.10) | copy-start | bytes 6291460
  3.6 7.9 %collective-permute-start.1 = (f32[560,128]{1,0:T(8,128)}, f32[560,128]{1,0:T(8,128)S(1)}, u32[]{:S(2)}, u32[]{:S(2)}) collective-permute-start(f32[560,128]{1,0:T(8,128)} %get-tuple-element.13.pay), channel_id=1, source_target_pairs={{1,0},{2,1},{3,2},{4,3},{5,4},{6,5},{7,6},{8,7},{9,8},{10,9},{11,1... | collective-permute-start | bytes 860168 | tf_op jit(solution)/shard_map/ppermute | solution.py:355
  7.0 8.4 %collective-permute-start = (f32[560,128]{1,0:T(8,128)}, f32[560,128]{1,0:T(8,128)S(1)}, u32[]{:S(2)}, u32[]{:S(2)}) collective-permute-start(f32[560,128]{1,0:T(8,128)} %get-tuple-element.13.pay), channel_id=1, source_target_pairs={{0,1},{1,2},{2,3},{3,4},{4,5},{5,6},{6,7},{7,8},{8,9},{9,10},{10,1... | collective-permute-start | bytes 860168 | tf_op jit(solution)/shard_map/ppermute | solution.py:354
  7.1 0.9 %copy-start.7 = (f32[9,13,13]{2,1,0:T(8,128)S(1)}, f32[9,13,13]{2,1,0:T(8,128)}, u32[]{:S(2)}) copy-start(f32[9,13,13]{2,1,0:T(8,128)} %param.14) | copy-start | bytes 18256
  7.1 1.0 %copy-start.9 = (pred[13,13]{0,1:T(8,128)(4,1)S(1)}, pred[13,13]{0,1:T(8,128)(4,1)}, u32[]{:S(2)}) copy-start(pred[13,13]{0,1:T(8,128)(4,1)} %constant.19.clone) | copy-start | bytes 511
  7.1 1.1 %copy-start.10 = (pred[8,16]{0,1:T(8,128)(4,1)S(1)}, pred[8,16]{0,1:T(8,128)(4,1)}, u32[]{:S(2)}) copy-start(pred[8,16]{0,1:T(8,128)(4,1)} %constant.20.clone) | copy-start | bytes 388
  7.1 1.5 %copy-start.2 = (f32[560,128]{1,0:T(8,128)S(1)}, f32[560,128]{1,0:T(8,128)}, u32[]{:S(2)}) copy-start(f32[560,128]{1,0:T(8,128)} %get-tuple-element.13.pay) | copy-start | bytes 860164
  7.1 1.5 %copy-start.4 = (s32[24,128]{1,0:T(8,128)S(1)}, s32[24,128]{1,0:T(8,128)}, u32[]{:S(2)}) copy-start(s32[24,128]{1,0:T(8,128)} %get-tuple-element.12) | copy-start | bytes 36868
  11.3 8.4 %copy-start.1 = (f32[16,8,4096]{2,1,0:T(8,128)S(1)}, f32[16,8,4096]{2,1,0:T(8,128)}, u32[]{:S(2)}) copy-start(f32[16,8,4096]{2,1,0:T(8,128)} %param.10) | copy-start | bytes 6291460
  11.3 8.4 %copy-start.5 = (f32[16]{0:T(128)S(1)}, f32[16]{0:T(128)}, u32[]{:S(2)}) copy-start(f32[16]{0:T(128)} %occ.1) | copy-start | bytes 196
  19.1 3.4 %collective-permute-start.2 = (f32[16,128]{1,0:T(8,128)S(1)}, f32[16,128]{1,0:T(8,128)S(1)}, u32[]{:S(2)}, u32[]{:S(2)}) collective-permute-start(f32[16,128]{1,0:T(8,128)S(1)} %get-tuple-element.14.after), channel_id=1, source_target_pairs={{1,0},{2,1},{3,2},{4,3},{5,4},{6,5},{7,6},{8,7},{9,8},{10,9},{11,1... | collective-permute-start | bytes 24584 | tf_op jit(solution)/shard_map/ppermute | solution.py:385
  19.3 17.1 %copy-start.11 = (s32[8]{0:T(128)S(1)}, s32[8]{0:T(128)}, u32[]{:S(2)}) copy-start(s32[8]{0:T(128)} %sizes_in.1) | copy-start | bytes 100
  19.3 17.2 %copy-start.8 = (f32[8,9,512]{2,0,1:T(8,128)S(1)}, f32[8,9,512]{2,0,1:T(8,128)}, u32[]{:S(2)}) copy-start(f32[8,9,512]{2,0,1:T(8,128)} %param.13) | copy-start | bytes 442372
  19.3 27.1 %copy-start.3 = (s32[8,512]{1,0:T(8,128)S(1)}, s32[8,512]{1,0:T(8,128)}, u32[]{:S(2)}) copy-start(s32[8,512]{1,0:T(8,128)} %offsets.1) | copy-start | bytes 49156
  19.3 28.7 %copy-start.6 = (f32[8,16,13,13]{3,1,0,2:T(8,128)S(1)}, f32[8,16,13,13]{3,1,0,2:T(8,128)}, u32[]{:S(2)}) copy-start(f32[8,16,13,13]{3,1,0,2:T(8,128)} %constant.21.clone) | copy-start | bytes 259588
  19.3 5.3 %collective-permute-start.3 = (f32[16,128]{1,0:T(8,128)S(1)}, f32[16,128]{1,0:T(8,128)S(1)}, u32[]{:S(2)}, u32[]{:S(2)}) collective-permute-start(f32[16,128]{1,0:T(8,128)S(1)} %get-tuple-element.16), channel_id=1, source_target_pairs={{0,1},{1,2},{2,3},{3,4},{4,5},{5,6},{6,7},{7,8},{8,9},{9,10},{10,1... | collective-permute-start | bytes 24584 | tf_op jit(solution)/shard_map/ppermute | solution.py:386
  25.7 20.8 %all-to-all-start = ((f32[16,24,128]{2,1,0:T(8,128)}), f32[16,24,128]{2,1,0:T(8,128)S(1)}, u32[]{:S(2)}, u32[]{:S(2)}) async-start(f32[16,24,128]{2,1,0:T(8,128)} %partial_matrices.1), calls=%async_computation | async-start | bytes 393216 | tf_op jit(solution)/shard_map/all_to_all | solution.py:416
  47.5 2.2 %collective-permute-start.4 = (f32[8,256]{1,0:T(8,128)S(1)}, f32[8,256]{1,0:T(8,128)S(1)}, u32[]{:S(2)}, u32[]{:S(2)}) collective-permute-start(f32[8,256]{1,0:T(8,128)S(1)} %get-tuple-element.19), channel_id=1, source_target_pairs={{1,0},{2,1},{3,2},{4,3},{5,4},{6,5},{7,6},{8,7},{9,8},{10,9},{11,1... | collective-permute-start | bytes 24584 | tf_op jit(solution)/shard_map/ppermute | solution.py:441
  47.5 5.3 %collective-permute-start.5 = (f32[8,256]{1,0:T(8,128)S(1)}, f32[8,256]{1,0:T(8,128)S(1)}, u32[]{:S(2)}, u32[]{:S(2)}) collective-permute-start(f32[8,256]{1,0:T(8,128)S(1)} %get-tuple-element.20), channel_id=1, source_target_pairs={{0,1},{1,2},{2,3},{3,4},{4,5},{5,6},{6,7},{7,8},{8,9},{9,10},{10,1... | collective-permute-start | bytes 24584 | tf_op jit(solution)/shard_map/ppermute | solution.py:442

commit v12 on v11

--- a/solution.py
+++ b/solution.py
@@ -1,3 +1,5 @@
+import functools
+
 import jax
 import jax.numpy as jnp
 import numpy as np
@@ -217,38 +219,32 @@
     q[...] = own_points(range(EARLY, ATOM_DEV), lists, table, pay, rows)
 
 
-def side_kernel(list_lo, list_hi, table, pay_lo, pay_hi, q_lo, q_hi, rows):
+def side_kernel(prev, points, table, pay, after, q, rows):
+    del after
     rows[...] = jnp.zeros_like(rows)
     step = 8
     most = jnp.int32(0)
     for a in range(ATOM_DEV):
-        most = jnp.maximum(most, jnp.maximum(counts(list_lo, a)[1], counts(list_hi, a)[0]))
-
-    def from_below():
-        for a in range(ATOM_DEV):
-            first = (SPHERE - counts(list_lo, a)[1]) // (2 * step)
-            gather_rows(list_lo, a, first, WORDS // step, step, table, rows)
-
-    def from_above():
-        for a in range(ATOM_DEV):
-            last = (counts(list_hi, a)[0] + (2 * step - 1)) // (2 * step)
-            gather_rows(list_hi, a, 0, last, step, table, rows)
-
-    low, high = range(HALO), range(CZ - HALO, CZ)
+        most = jnp.maximum(most, counts(points, a)[1 if prev else 0])
+
+    for a in range(ATOM_DEV):
+        first, last = 0, WORDS // step
+        if prev:
+            first = (SPHERE - counts(points, a)[1]) // (2 * step)
+        else:
+            last = (counts(points, a)[0] + (2 * step - 1)) // (2 * step)
+        gather_rows(points, a, first, last, step, table, rows)
+
+    shift = -HALO - CZ if prev else CZ - HALO
+    planes = range(HALO) if prev else range(CZ - HALO, CZ)
 
     @pl.when(most <= WORDS)
     def _():
-        from_below()
-        from_above()
-        q_lo[...] = project(pay_lo, rows, -HALO - CZ, low, (1, 3))
-        q_hi[...] = project(pay_hi, rows, CZ - HALO, high, (0, 2))
+        q[...] = project(pay, rows, shift, planes, (1, 3) if prev else (0, 2))
 
     @pl.when(most > WORDS)
     def _():
-        from_below()
-        q_lo[...] = project(pay_lo, rows, -HALO - CZ, low, range(TILES))
-        from_above()
-        q_hi[...] = project(pay_hi, rows, CZ - HALO, high, range(TILES))
+        q[...] = project(pay, rows, shift, planes, range(TILES))
 
 
 def matrix_kernel(q0, q1, q2, q3, occ, packed, out, block, sem):
@@ -367,21 +363,22 @@
         name="own_points_early",
     )(own_list, table, pay)
 
-    q_lo, q_hi = pl.pallas_call(
-        side_kernel,
-        out_shape=(shape(BANDS, LANES), shape(BANDS, LANES)),
-        in_specs=[SM, SM, VM, VM, VM],
-        out_specs=(VM, VM),
-        scratch_shapes=[pltpu.VMEM((ATOM_DEV * SPHERE, LANES), F32)],
-        compiler_params=params(),
-        name="side_points",
-    )(
-        words_of(pay_lo),
-        words_of(pay_hi),
-        table,
-        pay_lo,
-        pay_hi,
-    )
+    def side(prev, block, after):
+        return pl.pallas_call(
+            functools.partial(side_kernel, prev),
+            out_shape=shape(BANDS, LANES),
+            in_specs=[SM, VM, VM, ANY],
+            out_specs=VM,
+            scratch_shapes=scratch,
+            compiler_params=params(),
+            cost_estimate=pl.CostEstimate(
+                flops=10**9, bytes_accessed=6 * 2**20, transcendentals=0
+            ),
+            name="previous_points" if prev else "next_points",
+        )(words_of(block), table, block, after)
+
+    q_hi = side(False, pay_hi, q_early)
+    q_lo = side(True, pay_lo, q_hi)
     back_hi = lax.ppermute(q_lo, "slab", to_prev)
     back_lo = lax.ppermute(q_hi, "slab", to_next)
 

time: 53.5 us -> 55.7 us (1.041); the launches traced: 53.4 us -> 54.7 us
  waiting for transfers between devices: 19.3 us -> 13.5 us
  starting transfers between devices: 15.4 us -> 18.8 us
  local copies, waits for them, and re-layouts: 0.89 us -> 3.6 us
  Pallas kernels: 14.6 us -> 15.5 us
    ppermute x1, waiting for transfers between devices: 3.9 us -> 0.03 us  [local(): pay_lo = lax.ppermute(pay, 'slab', to_next)]
    ppermute x1, starting transfers between devices: 0.24 us -> 3.73 us  [local(): back_hi = lax.ppermute(q_lo, 'slab', to_prev)]
    unnamed x25 -> x29, local copies, waits for them, and re-layouts: 0.43 us -> 3.14 us
    ppermute x1, waiting for transfers between devices: 2.12 us -> 0.01 us  [local(): back_lo = lax.ppermute(q_hi, 'slab', to_next)]
    pallas_call x1 -> x2, Pallas kernels: 3.65 us -> 4.86 us  [side(): pl.pallas_call(functools.partial(side_kernel, prev), out_shape=shape(BAND...]
    ppermute x1, starting transfers between devices: 0.03 us -> 0.84 us  [local(): from_above = lax.ppermute(down, 'slab', to_prev)]
  transfers between devices with their start and end apart: 7 -> 7, of which waited for: 5 -> 2; matrix products, arithmetic and copies ran while one was open for 4% -> 4% of each run, Pallas kernels for 11% -> 19%
where the time goes in v12:
time: 55.7 us; the launch traced here: 54.7 us
  starting transfers between devices  18.8 us (34%)
  Pallas kernels  15.5 us (28%)
  waiting for transfers between devices  13.5 us (24%)
  local copies, waits for them, and re-layouts  3.6 us (6%)
  matrix products  1.69 us (3%)
  other arithmetic  0.83 us (1%)
  between operations  0.82 us (1%)
    all_to_all x1, starting transfers between devices, local(): recv = lax.all_to_all(packed, 'band', 0, 0)  10.8 us
    all_to_all x1, waiting for transfers between devices, local(): recv = lax.all_to_all(packed, 'band', 0, 0)  9.94 us
    pallas_call x2, Pallas kernels, side(): pl.pallas_call(functools.partial(side_kernel, prev), out_shape=shape(BAND...  4.86 us
    ppermute x1, starting transfers between devices, local(): back_hi = lax.ppermute(q_lo, 'slab', to_prev)  3.73 us
    ppermute x1, waiting for transfers between devices, local(): from_below = lax.ppermute(up, 'slab', to_next)  3.49 us
    ppermute x1, starting transfers between devices, local(): pay_hi = lax.ppermute(pay, 'slab', to_prev)  3.46 us
    unnamed x29, local copies, waits for them, and re-layouts  3.14 us
    pallas_call x1, Pallas kernels, local(): pl.pallas_call(sort_kernel, out_shape=(shape(SORTED + 2 * LIST, LANES), j...  2.94 us
  transfers between devices with their start and end apart: 7, of which 2 were waited for; matrix products, arithmetic and copies ran while one was open for 4% of the time, Pallas kernels for 19%

profile of v12, /device:TPU:32, one launch (start us, length us, event | category | flops | bytes accessed | tf_op | source)
XLA Modules:
  0.0 54.7 jit_solution(15814858990957205225)
XLA Ops:
  0.6 0.0 copy-start
  0.6 2.9 %sort_points.1 = (f32[560,128]{1,0:T(8,128)}, s32[24,128]{1,0:T(8,128)}) custom-call(s32[8]{0:T(128)} %sizes_in.1, s32[8,512]{1,0:T(8,128)} %offsets.1, f32[13,8,512]{2,1,0:T(8,128)} %bitcast.25), custom_call_target="tpu_custom_call" | custom-call | flops 1000000000 | bytes 8388608 | tf_op jit(solution)/shard_map/sort_points/pallas_call | solution.py:332
  3.6 3.5 %collective-permute-start.1 = (f32[560,128]{1,0:T(8,128)}, f32[560,128]{1,0:T(8,128)S(1)}, u32[]{:S(2)}, u32[]{:S(2)}) collective-permute-start(f32[560,128]{1,0:T(8,128)} %get-tuple-element.11.pay), channel_id=1, source_target_pairs={{1,0},{2,1},{3,2},{4,3},{5,4},{6,5},{7,6},{8,7},{9,8},{10,9},{11,1... | collective-permute-start | bytes 860168 | tf_op jit(solution)/shard_map/ppermute | solution.py:351
  7.0 0.0 collective-permute-start
  7.0 0.0 copy-done
  7.1 0.0 copy-start.9
  7.1 0.0 copy-start.11
  7.1 0.0 copy-start.12
  7.1 0.0 copy-start.4
  7.1 0.0 copy-start.6
  7.1 0.6 %grid_table.1.table = f32[4096,128]{1,0:T(8,128)S(1)} custom-call(f32[128,4096]{1,0:T(8,128)S(1)} %bitcast.20), custom_call_target="tpu_custom_call" | custom-call | bytes 8388608 | tf_op jit(solution)/shard_map/grid_table/pallas_call | solution.py:323
  7.7 0.0 copy-start.1
  7.7 1.3 %copy-done.1 = f32[4096,128]{1,0:T(8,128)} copy-done((f32[4096,128]{1,0:T(8,128)}, f32[4096,128]{1,0:T(8,128)S(1)}, u32[]{:S(2)}) %copy-start.1) | copy-done | bytes 2097176
  9.0 0.0 copy-done.9
  9.0 0.1 copy.14
  9.2 0.0 copy-done.11
  9.2 0.1 slice.28
  9.3 0.0 copy-done.12
  9.3 0.1 pad_select_fusion
  9.4 0.1 copy.15
  9.5 0.1 tile.10.coupling
  9.6 0.0 copy-done.4
  9.6 0.0 copy-done.6
  9.7 0.0 copy-start.2
  9.7 1.6 %copy-done.2 = f32[4096,128]{1,0:T(8,128)S(1)} copy-done((f32[4096,128]{1,0:T(8,128)S(1)}, f32[4096,128]{1,0:T(8,128)}, u32[]{:S(2)}) %copy-start.2) | copy-done | bytes 2097176
  11.3 0.0 copy-start.3
  11.3 2.6 %own_points_early.1.after.q0 = f32[16,128]{1,0:T(8,128)S(1)} custom-call(s32[3072]{0:T(1024)S(1)} %bitcast.22, f32[4096,128]{1,0:T(8,128)S(1)} %copy-done.2, f32[560,128]{1,0:T(8,128)S(1)} %copy-done.4), custom_call_target="tpu_custom_call" | custom-call | flops 1000000000 | bytes 8388608 | tf_op jit(solution)/shard_map/own_points_early/pallas_call | solution.py:355
  13.9 0.0 collective-permute-done.1.pay
  13.9 0.0 copy-done.3
  13.9 2.6 %next_points.1.after = f32[16,128]{1,0:T(8,128)S(1)} custom-call(s32[3072]{0:T(1024)S(1)} %fusion.2.points, f32[4096,128]{1,0:T(8,128)S(1)} %copy-done.3, f32[560,128]{1,0:T(8,128)S(1)} %collective-permute-done.1.pay, f32[16,128]{1,0:T(8,128)S(1)} %own_points_early.1.after.q0), custom_call_target="tpu_custom_call" | custom-call | flops 1000000000 | bytes 6291456 | tf_op jit(solution)/shard_map/next_points/pallas_call | solution.py:367
  16.6 0.0 copy-start.7
  16.6 0.0 collective-permute-start.3
  16.6 0.0 collective-permute-done.pay
  16.6 2.2 %previous_points.1.after = f32[16,128]{1,0:T(8,128)S(1)} custom-call(s32[3072]{0:T(1024)S(1)} %fusion.5.points, f32[4096,128]{1,0:T(8,128)S(1)} %copy-done.3, f32[560,128]{1,0:T(8,128)S(1)} %collective-permute-done.pay, f32[16,128]{1,0:T(8,128)S(1)} %next_points.1.after), custom_call_target="tpu_custom_call" | custom-call | flops 1000000000 | bytes 6291456 | tf_op jit(solution)/shard_map/previous_points/pallas_call | solution.py:367
  18.9 0.0 copy-start.13
  18.9 0.0 copy-start.10
  18.9 0.0 copy-start.5
  18.9 0.0 copy-start.8
  18.9 3.7 %collective-permute-start.2 = (f32[16,128]{1,0:T(8,128)S(1)}, f32[16,128]{1,0:T(8,128)S(1)}, u32[]{:S(2)}, u32[]{:S(2)}) collective-permute-start(f32[16,128]{1,0:T(8,128)S(1)} %previous_points.1.after), channel_id=1, source_target_pairs={{1,0},{2,1},{3,2},{4,3},{5,4},{6,5},{7,6},{8,7},{9,8},{10,9},{11,1... | collective-permute-start | bytes 24584 | tf_op jit(solution)/shard_map/ppermute | solution.py:382
  22.6 0.0 copy-done.7
  22.6 2.5 %own_points_late.1 = (f32[16,24,128]{2,1,0:T(8,128)}, f32[16,128]{1,0:T(8,128)S(1)}) custom-call(s32[3072]{0:T(1024)S(1)} %bitcast.23, f32[16]{0:T(128)S(1)} %copy-done.7, f32[128,4096]{1,0:T(8,128)S(1)} %bitcast.21, f32[4096,128]{1,0:T(8,128)S(1)} %copy-done.3, f32[560,128]{1,0:T(8,128)S(1)} %copy-done.4, f32[16,128]{1,0:T(8,128)S(1)} %previous_points.1.after), custom_call_target="tpu_custom_call" | custom-call | flops 1000000000 | bytes 8388608 | tf_op jit(solution)/shard_map/own_points_late/pallas_call | solution.py:385
  25.2 0.0 collective-permute-done.2.q2
  25.2 0.0 collective-permute-done.3.q3
  25.2 0.1 broadcast_in_dim.29.occ
  25.2 1.0 %partial_matrices.1 = f32[16,24,128]{2,1,0:T(8,128)} custom-call(f32[16,128]{1,0:T(8,128)S(1)} %own_points_early.1.after.q0, f32[16,128]{1,0:T(8,128)S(1)} %get-tuple-element.12.q1, f32[16,128]{1,0:T(8,128)S(1)} %collective-permute-done.2.q2, f32[16,128]{1,0:T(8,128)S(1)} %collective-permute-done.3.q3, ...), custom_call_target="tpu_custom_call", output_to_operand_aliasing={{}: (5, {})} | custom-call | tf_op jit(solution)/shard_map/partial_matrices/pallas_call | solution.py:396
  26.2 10.8 %all-to-all-start = ((f32[16,24,128]{2,1,0:T(8,128)}), f32[16,24,128]{2,1,0:T(8,128)S(1)}, u32[]{:S(2)}, u32[]{:S(2)}) async-start(f32[16,24,128]{2,1,0:T(8,128)} %partial_matrices.1), calls=%async_computation | async-start | bytes 393216 | tf_op jit(solution)/shard_map/all_to_all | solution.py:413
  37.0 0.0 copy-done.13
  37.0 0.1 iota_compare_fusion
  37.1 0.0 copy-done.10
  37.1 9.9 %all-to-all-done.recv = f32[16,24,128]{2,1,0:T(8,128)S(1)} async-done(((f32[16,24,128]{2,1,0:T(8,128)}), f32[16,24,128]{2,1,0:T(8,128)S(1)}, u32[]{:S(2)}, u32[]{:S(2)}) %all-to-all-start) | async-done | bytes 196640 | tf_op jit(solution)/shard_map/all_to_all | solution.py:413
  47.0 0.0 copy-done.5
  47.0 1.0 %charges.1 = (f32[8,256]{1,0:T(8,128)S(1)}, f32[8,256]{1,0:T(8,128)S(1)}, f32[8,256]{1,0:T(8,128)S(1)}, f32[8,128]{1,0:T(8,128)S(1)}) custom-call(s32[1]{0:T(128)} %bitcast.start, f32[16,24,128]{2,1,0:T(8,128)S(1)} %all-to-all-done.recv, f32[9,8,128]{2,1,0:T(8,128)S(1)} %tile.10.coupling, f32[9,8,512]{2,1,0:T(8,128)S(1)} %select_bitcast_fusion.shapes, ...), custom_call_target="tpu_custom_call" | custom-call | tf_op jit(solution)/shard_map/charges/pallas_call | solution.py:430
  48.0 0.1 reshape.50
  48.1 0.8 %collective-permute-start.4 = (f32[8,256]{1,0:T(8,128)S(1)}, f32[8,256]{1,0:T(8,128)S(1)}, u32[]{:S(2)}, u32[]{:S(2)}) collective-permute-start(f32[8,256]{1,0:T(8,128)S(1)} %get-tuple-element.15), channel_id=1, source_target_pairs={{1,0},{2,1},{3,2},{4,3},{5,4},{6,5},{7,6},{8,7},{9,8},{10,9},{11,1... | collective-permute-start | bytes 24584 | tf_op jit(solution)/shard_map/ppermute | solution.py:438
  48.9 0.0 collective-permute-start.5
  48.9 0.0 copy-done.8
  48.9 1.7 %convolution_bitcast_fusion = f32[8,13,13]{2,0,1:T(8,128)} fusion(f32[8,8,16,1]{2,1,0,3:T(8,128)S(1)} %reshape.50, f32[8,16,13,13]{3,1,0,2:T(8,128)S(1)} %copy-done.8), kind=kOutput, calls=%fused_computation | convolution fusion | flops 2076672 | bytes 96032 | tf_op jit(solution)/shard_map/paq,pqij->aij/dot_general | solution.py:441
  50.6 0.0 collective-permute-done.4
  50.6 3.5 %collective-permute-done.5 = f32[8,256]{1,0:T(8,128)S(1)} collective-permute-done((f32[8,256]{1,0:T(8,128)S(1)}, f32[8,256]{1,0:T(8,128)S(1)}, u32[]{:S(2)}, u32[]{:S(2)}) %collective-permute-start.5) | collective-permute-done | bytes 8224 | tf_op jit(solution)/shard_map/ppermute | solution.py:439
  54.1 0.6 %add_add_fusion = f32[8,256]{1,0:T(8,128)} fusion(f32[8,256]{1,0:T(8,128)S(1)} %collective-permute-done.5, f32[8,256]{1,0:T(8,128)S(1)} %get-tuple-element.14, f32[8,256]{1,0:T(8,128)S(1)} %collective-permute-done.4), kind=kLoop, calls=%fused_computation.13 | loop fusion | flops 4096 | bytes 32768 | tf_op jit(solution)/shard_map/add | solution.py:440
  (5 shorter events, 0.1 us)
Async XLA Ops:
  0.6 6.4 %copy-start = (f32[16,8,4096]{2,1,0:T(8,128)S(1)}, f32[16,8,4096]{2,1,0:T(8,128)}, u32[]{:S(2)}) copy-start(f32[16,8,4096]{2,1,0:T(8,128)} %param.10) | copy-start | bytes 6291460
  3.6 10.3 %collective-permute-start.1 = (f32[560,128]{1,0:T(8,128)}, f32[560,128]{1,0:T(8,128)S(1)}, u32[]{:S(2)}, u32[]{:S(2)}) collective-permute-start(f32[560,128]{1,0:T(8,128)} %get-tuple-element.11.pay), channel_id=1, source_target_pairs={{1,0},{2,1},{3,2},{4,3},{5,4},{6,5},{7,6},{8,7},{9,8},{10,9},{11,1... | collective-permute-start | bytes 860168 | tf_op jit(solution)/shard_map/ppermute | solution.py:351
  7.0 9.5 %collective-permute-start = (f32[560,128]{1,0:T(8,128)}, f32[560,128]{1,0:T(8,128)S(1)}, u32[]{:S(2)}, u32[]{:S(2)}) collective-permute-start(f32[560,128]{1,0:T(8,128)} %get-tuple-element.11.pay), channel_id=1, source_target_pairs={{0,1},{1,2},{2,3},{3,4},{4,5},{5,6},{6,7},{7,8},{8,9},{9,10},{10,1... | collective-permute-start | bytes 860168 | tf_op jit(solution)/shard_map/ppermute | solution.py:350
  7.1 2.0 %copy-start.9 = (f32[9,13,13]{2,1,0:T(8,128)S(1)}, f32[9,13,13]{2,1,0:T(8,128)}, u32[]{:S(2)}) copy-start(f32[9,13,13]{2,1,0:T(8,128)} %param.14) | copy-start | bytes 18256
  7.1 2.1 %copy-start.11 = (pred[13,13]{0,1:T(8,128)(4,1)S(1)}, pred[13,13]{0,1:T(8,128)(4,1)}, u32[]{:S(2)}) copy-start(pred[13,13]{0,1:T(8,128)(4,1)} %constant.19.clone) | copy-start | bytes 511
  7.1 2.2 %copy-start.12 = (pred[8,16]{0,1:T(8,128)(4,1)S(1)}, pred[8,16]{0,1:T(8,128)(4,1)}, u32[]{:S(2)}) copy-start(pred[8,16]{0,1:T(8,128)(4,1)} %constant.20.clone) | copy-start | bytes 388
  7.1 2.6 %copy-start.4 = (f32[560,128]{1,0:T(8,128)S(1)}, f32[560,128]{1,0:T(8,128)}, u32[]{:S(2)}) copy-start(f32[560,128]{1,0:T(8,128)} %get-tuple-element.11.pay) | copy-start | bytes 860164
  7.1 2.6 %copy-start.6 = (s32[24,128]{1,0:T(8,128)S(1)}, s32[24,128]{1,0:T(8,128)}, u32[]{:S(2)}) copy-start(s32[24,128]{1,0:T(8,128)} %get-tuple-element.10) | copy-start | bytes 36868
  7.7 1.3 %copy-start.1 = (f32[4096,128]{1,0:T(8,128)}, f32[4096,128]{1,0:T(8,128)S(1)}, u32[]{:S(2)}) copy-start(f32[4096,128]{1,0:T(8,128)S(1)} %grid_table.1.table) | copy-start | bytes 6291460
  9.7 1.6 %copy-start.2 = (f32[4096,128]{1,0:T(8,128)S(1)}, f32[4096,128]{1,0:T(8,128)}, u32[]{:S(2)}) copy-start(f32[4096,128]{1,0:T(8,128)} %copy-done.1) | copy-start | bytes 6291460
  11.3 2.7 %copy-start.3 = (f32[4096,128]{1,0:T(8,128)S(1)}, f32[4096,128]{1,0:T(8,128)}, u32[]{:S(2)}) copy-start(f32[4096,128]{1,0:T(8,128)} %copy-done.1) | copy-start | bytes 6291460
  16.6 6.1 %copy-start.7 = (f32[16]{0:T(128)S(1)}, f32[16]{0:T(128)}, u32[]{:S(2)}) copy-start(f32[16]{0:T(128)} %occ.1) | copy-start | bytes 196
  16.6 8.6 %collective-permute-start.3 = (f32[16,128]{1,0:T(8,128)S(1)}, f32[16,128]{1,0:T(8,128)S(1)}, u32[]{:S(2)}, u32[]{:S(2)}) collective-permute-start(f32[16,128]{1,0:T(8,128)S(1)} %next_points.1.after), channel_id=1, source_target_pairs={{0,1},{1,2},{2,3},{3,4},{4,5},{5,6},{6,7},{7,8},{8,9},{9,10},{10,1... | collective-permute-start | bytes 24584 | tf_op jit(solution)/shard_map/ppermute | solution.py:383
  18.9 18.1 %copy-start.13 = (s32[8]{0:T(128)S(1)}, s32[8]{0:T(128)}, u32[]{:S(2)}) copy-start(s32[8]{0:T(128)} %sizes_in.1) | copy-start | bytes 100
  18.9 18.2 %copy-start.10 = (f32[8,9,512]{2,0,1:T(8,128)S(1)}, f32[8,9,512]{2,0,1:T(8,128)}, u32[]{:S(2)}) copy-start(f32[8,9,512]{2,0,1:T(8,128)} %param.13) | copy-start | bytes 442372
  18.9 28.2 %copy-start.5 = (s32[8,512]{1,0:T(8,128)S(1)}, s32[8,512]{1,0:T(8,128)}, u32[]{:S(2)}) copy-start(s32[8,512]{1,0:T(8,128)} %offsets.1) | copy-start | bytes 49156
  18.9 30.1 %copy-start.8 = (f32[8,16,13,13]{3,1,0,2:T(8,128)S(1)}, f32[8,16,13,13]{3,1,0,2:T(8,128)}, u32[]{:S(2)}) copy-start(f32[8,16,13,13]{3,1,0,2:T(8,128)} %constant.21.clone) | copy-start | bytes 259588
  18.9 6.3 %collective-permute-start.2 = (f32[16,128]{1,0:T(8,128)S(1)}, f32[16,128]{1,0:T(8,128)S(1)}, u32[]{:S(2)}, u32[]{:S(2)}) collective-permute-start(f32[16,128]{1,0:T(8,128)S(1)} %previous_points.1.after), channel_id=1, source_target_pairs={{1,0},{2,1},{3,2},{4,3},{5,4},{6,5},{7,6},{8,7},{9,8},{10,9},{11,1... | collective-permute-start | bytes 24584 | tf_op jit(solution)/shard_map/ppermute | solution.py:382
  26.2 20.8 %all-to-all-start = ((f32[16,24,128]{2,1,0:T(8,128)}), f32[16,24,128]{2,1,0:T(8,128)S(1)}, u32[]{:S(2)}, u32[]{:S(2)}) async-start(f32[16,24,128]{2,1,0:T(8,128)} %partial_matrices.1), calls=%async_computation | async-start | bytes 393216 | tf_op jit(solution)/shard_map/all_to_all | solution.py:413
  48.1 2.5 %collective-permute-start.4 = (f32[8,256]{1,0:T(8,128)S(1)}, f32[8,256]{1,0:T(8,128)S(1)}, u32[]{:S(2)}, u32[]{:S(2)}) collective-permute-start(f32[8,256]{1,0:T(8,128)S(1)} %get-tuple-element.15), channel_id=1, source_target_pairs={{1,0},{2,1},{3,2},{4,3},{5,4},{6,5},{7,6},{8,7},{9,8},{10,9},{11,1... | collective-permute-start | bytes 24584 | tf_op jit(solution)/shard_map/ppermute | solution.py:438
  48.9 5.2 %collective-permute-start.5 = (f32[8,256]{1,0:T(8,128)S(1)}, f32[8,256]{1,0:T(8,128)S(1)}, u32[]{:S(2)}, u32[]{:S(2)}) collective-permute-start(f32[8,256]{1,0:T(8,128)S(1)} %get-tuple-element.16), channel_id=1, source_target_pairs={{0,1},{1,2},{2,3},{3,4},{4,5},{5,6},{6,7},{7,8},{8,9},{9,10},{10,1... | collective-permute-start | bytes 24584 | tf_op jit(solution)/shard_map/ppermute | solution.py:439

commit v13 on v12

--- a/solution.py
+++ b/solution.py
@@ -31,7 +31,7 @@
 ANY = pl.BlockSpec(memory_space=pl.ANY)
 
 
-def params(limit=48 * 2**20):
+def params(limit=50 * 2**20):
     return pltpu.CompilerParams(vmem_limit_bytes=limit)
 
 

time: 55.7 us -> 54.8 us (0.984); the launches traced: 54.7 us -> 54.5 us
  local copies, waits for them, and re-layouts: 3.6 us -> 0.68 us
  Pallas kernels: 15.5 us -> 17.3 us
    unnamed x29 -> x25, local copies, waits for them, and re-layouts: 3.14 us -> 0.22 us
    pallas_call x1, Pallas kernels: 0.59 us -> 2.25 us  [local(): pl.pallas_call(table_kernel, out_shape=shape(PLANE, LANES), in_specs=[VM]...]
    pallas_call x1, Pallas kernels: 2.53 us -> 3.49 us  [local(): pl.pallas_call(late_kernel, out_shape=(shape(16, 24, LANES), shape(BANDS,...]
    pallas_call x2, Pallas kernels: 4.86 us -> 4.24 us  [side(): pl.pallas_call(functools.partial(side_kernel, prev), out_shape=shape(BAND...]
  transfers between devices with their start and end apart: 7 -> 7, of which waited for: 2 -> 3; matrix products, arithmetic and copies ran while one was open for 4% -> 4% of each run, Pallas kernels for 19% -> 23%
where the time goes in v13:
time: 54.8 us; the launch traced here: 54.5 us
  starting transfers between devices  19.2 us (35%)
  Pallas kernels  17.3 us (32%)
  waiting for transfers between devices  13.9 us (25%)
  matrix products  1.69 us (3%)
  other arithmetic  0.83 us (2%)
  between operations  0.81 us (1%)
  local copies, waits for them, and re-layouts  0.68 us (1%)
    all_to_all x1, starting transfers between devices, local(): recv = lax.all_to_all(packed, 'band', 0, 0)  10.8 us
    all_to_all x1, waiting for transfers between devices, local(): recv = lax.all_to_all(packed, 'band', 0, 0)  9.94 us
    pallas_call x2, Pallas kernels, side(): pl.pallas_call(functools.partial(side_kernel, prev), out_shape=shape(BAND...  4.24 us
    ppermute x1, starting transfers between devices, local(): back_hi = lax.ppermute(q_lo, 'slab', to_prev)  4.07 us
    pallas_call x1, Pallas kernels, local(): pl.pallas_call(late_kernel, out_shape=(shape(16, 24, LANES), shape(BANDS,...  3.49 us
    ppermute x1, waiting for transfers between devices, local(): from_below = lax.ppermute(up, 'slab', to_next)  3.49 us
    ppermute x1, starting transfers between devices, local(): pay_hi = lax.ppermute(pay, 'slab', to_prev)  3.46 us
    pallas_call x1, Pallas kernels, local(): pl.pallas_call(sort_kernel, out_shape=(shape(SORTED + 2 * LIST, LANES), j...  2.78 us
  transfers between devices with their start and end apart: 7, of which 3 were waited for; matrix products, arithmetic and copies ran while one was open for 4% of the time, Pallas kernels for 23%

profile of v13, /device:TPU:32, one launch (start us, length us, event | category | flops | bytes accessed | tf_op | source)
XLA Modules:
  0.0 54.5 jit_solution(9467326937530344076)
XLA Ops:
  0.6 2.8 %sort_points.1 = (f32[560,128]{1,0:T(8,128)}, s32[24,128]{1,0:T(8,128)}) custom-call(s32[8]{0:T(128)} %sizes_in.1, s32[8,512]{1,0:T(8,128)} %offsets.1, f32[13,8,512]{2,1,0:T(8,128)} %bitcast.25), custom_call_target="tpu_custom_call" | custom-call | flops 1000000000 | bytes 8388608 | tf_op jit(solution)/shard_map/sort_points/pallas_call | solution.py:332
  3.4 3.5 %collective-permute-start.1 = (f32[560,128]{1,0:T(8,128)}, f32[560,128]{1,0:T(8,128)S(1)}, u32[]{:S(2)}, u32[]{:S(2)}) collective-permute-start(f32[560,128]{1,0:T(8,128)} %get-tuple-element.11.pay), channel_id=1, source_target_pairs={{1,0},{2,1},{3,2},{4,3},{5,4},{6,5},{7,6},{8,7},{9,8},{10,9},{11,1... | collective-permute-start | bytes 860168 | tf_op jit(solution)/shard_map/ppermute | solution.py:351
  6.9 0.0 collective-permute-start
  6.9 0.0 copy-start.7
  6.9 0.0 copy-start.9
  6.9 0.0 copy-start.10
  6.9 0.0 copy-start.2
  6.9 0.0 copy-start.4
  6.9 2.2 %grid_table.1.table = f32[4096,128]{1,0:T(8,128)S(1)} custom-call(f32[128,4096]{1,0:T(8,128)} %bitcast.20), custom_call_target="tpu_custom_call" | custom-call | bytes 8388608 | tf_op jit(solution)/shard_map/grid_table/pallas_call | solution.py:323
  9.2 0.0 copy-done.7
  9.2 0.0 copy-start.1
  9.2 0.1 copy.14
  9.3 0.0 copy-done.9
  9.4 0.1 slice.28
  9.4 0.0 copy-done.10
  9.4 0.1 pad_select_fusion
  9.5 0.1 copy.15
  9.6 0.1 tile.10.coupling
  9.8 0.0 copy-done.2
  9.8 0.0 copy-done.4
  9.8 2.6 %own_points_early.1.after.q0 = f32[16,128]{1,0:T(8,128)S(1)} custom-call(s32[3072]{0:T(1024)S(1)} %bitcast.22, f32[4096,128]{1,0:T(8,128)S(1)} %grid_table.1.table, f32[560,128]{1,0:T(8,128)S(1)} %copy-done.2), custom_call_target="tpu_custom_call" | custom-call | flops 1000000000 | bytes 8388608 | tf_op jit(solution)/shard_map/own_points_early/pallas_call | solution.py:355
  12.4 0.0 collective-permute-done.1.pay
  12.4 2.3 %next_points.1.after = f32[16,128]{1,0:T(8,128)S(1)} custom-call(s32[3072]{0:T(1024)S(1)} %fusion.2.points, f32[4096,128]{1,0:T(8,128)S(1)} %grid_table.1.table, f32[560,128]{1,0:T(8,128)S(1)} %collective-permute-done.1.pay, f32[16,128]{1,0:T(8,128)S(1)} %own_points_early.1.after.q0), custom_call_target="tpu_custom_call" | custom-call | flops 1000000000 | bytes 6291456 | tf_op jit(solution)/shard_map/next_points/pallas_call | solution.py:367
  14.7 0.0 copy-start
  14.7 0.0 copy-start.5
  14.7 0.0 collective-permute-start.3
  14.8 0.5 collective-permute-done.pay
  15.3 0.0 copy-done.1
  15.3 1.9 %previous_points.1.after = f32[16,128]{1,0:T(8,128)S(1)} custom-call(s32[3072]{0:T(1024)S(1)} %fusion.5.points, f32[4096,128]{1,0:T(8,128)S(1)} %grid_table.1.table, f32[560,128]{1,0:T(8,128)S(1)} %collective-permute-done.pay, f32[16,128]{1,0:T(8,128)S(1)} %next_points.1.after), custom_call_target="tpu_custom_call" | custom-call | flops 1000000000 | bytes 6291456 | tf_op jit(solution)/shard_map/previous_points/pallas_call | solution.py:367
  17.2 0.0 copy-start.11
  17.2 0.0 copy-start.8
  17.2 0.0 copy-start.3
  17.2 0.0 copy-start.6
  17.3 4.1 %collective-permute-start.2 = (f32[16,128]{1,0:T(8,128)S(1)}, f32[16,128]{1,0:T(8,128)S(1)}, u32[]{:S(2)}, u32[]{:S(2)}) collective-permute-start(f32[16,128]{1,0:T(8,128)S(1)} %previous_points.1.after), channel_id=1, source_target_pairs={{1,0},{2,1},{3,2},{4,3},{5,4},{6,5},{7,6},{8,7},{9,8},{10,9},{11,1... | collective-permute-start | bytes 24584 | tf_op jit(solution)/shard_map/ppermute | solution.py:382
  21.3 0.0 copy-done
  21.3 0.0 copy-done.5
  21.3 3.5 %own_points_late.1 = (f32[16,24,128]{2,1,0:T(8,128)}, f32[16,128]{1,0:T(8,128)S(1)}) custom-call(s32[3072]{0:T(1024)S(1)} %bitcast.23, f32[16]{0:T(128)S(1)} %copy-done.5, f32[128,4096]{1,0:T(8,128)S(1)} %bitcast.21, f32[4096,128]{1,0:T(8,128)} %copy-done.1, f32[560,128]{1,0:T(8,128)S(1)} %copy-done.2, f32[16,128]{1,0:T(8,128)S(1)} %previous_points.1.after), custom_call_target="tpu_custom_call" | custom-call | flops 1000000000 | bytes 8388608 | tf_op jit(solution)/shard_map/own_points_late/pallas_call | solution.py:385
  24.8 0.0 collective-permute-done.2.q2
  24.8 0.0 collective-permute-done.3.q3
  24.8 0.1 broadcast_in_dim.29.occ
  24.9 1.0 %partial_matrices.1 = f32[16,24,128]{2,1,0:T(8,128)} custom-call(f32[16,128]{1,0:T(8,128)S(1)} %own_points_early.1.after.q0, f32[16,128]{1,0:T(8,128)S(1)} %get-tuple-element.12.q1, f32[16,128]{1,0:T(8,128)S(1)} %collective-permute-done.2.q2, f32[16,128]{1,0:T(8,128)S(1)} %collective-permute-done.3.q3, ...), custom_call_target="tpu_custom_call", output_to_operand_aliasing={{}: (5, {})} | custom-call | tf_op jit(solution)/shard_map/partial_matrices/pallas_call | solution.py:396
  25.9 10.8 %all-to-all-start = ((f32[16,24,128]{2,1,0:T(8,128)}), f32[16,24,128]{2,1,0:T(8,128)S(1)}, u32[]{:S(2)}, u32[]{:S(2)}) async-start(f32[16,24,128]{2,1,0:T(8,128)} %partial_matrices.1), calls=%async_computation | async-start | bytes 393216 | tf_op jit(solution)/shard_map/all_to_all | solution.py:413
  36.7 0.0 copy-done.11
  36.7 0.1 iota_compare_fusion
  36.8 0.0 copy-done.8
  36.8 9.9 %all-to-all-done.recv = f32[16,24,128]{2,1,0:T(8,128)S(1)} async-done(((f32[16,24,128]{2,1,0:T(8,128)}), f32[16,24,128]{2,1,0:T(8,128)S(1)}, u32[]{:S(2)}, u32[]{:S(2)}) %all-to-all-start) | async-done | bytes 196640 | tf_op jit(solution)/shard_map/all_to_all | solution.py:413
  46.7 0.0 copy-done.3
  46.7 1.0 %charges.1 = (f32[8,256]{1,0:T(8,128)S(1)}, f32[8,256]{1,0:T(8,128)S(1)}, f32[8,256]{1,0:T(8,128)S(1)}, f32[8,128]{1,0:T(8,128)S(1)}) custom-call(s32[1]{0:T(128)} %bitcast.start, f32[16,24,128]{2,1,0:T(8,128)S(1)} %all-to-all-done.recv, f32[9,8,128]{2,1,0:T(8,128)S(1)} %tile.10.coupling, f32[9,8,512]{2,1,0:T(8,128)S(1)} %select_bitcast_fusion.shapes, ...), custom_call_target="tpu_custom_call" | custom-call | tf_op jit(solution)/shard_map/charges/pallas_call | solution.py:430
  47.7 0.1 reshape.50
  47.8 0.9 %collective-permute-start.4 = (f32[8,256]{1,0:T(8,128)S(1)}, f32[8,256]{1,0:T(8,128)S(1)}, u32[]{:S(2)}, u32[]{:S(2)}) collective-permute-start(f32[8,256]{1,0:T(8,128)S(1)} %get-tuple-element.15), channel_id=1, source_target_pairs={{1,0},{2,1},{3,2},{4,3},{5,4},{6,5},{7,6},{8,7},{9,8},{10,9},{11,1... | collective-permute-start | bytes 24584 | tf_op jit(solution)/shard_map/ppermute | solution.py:438
  48.7 0.0 collective-permute-start.5
  48.7 0.0 copy-done.6
  48.7 1.7 %convolution_bitcast_fusion = f32[8,13,13]{2,0,1:T(8,128)} fusion(f32[8,8,16,1]{2,1,0,3:T(8,128)S(1)} %reshape.50, f32[8,16,13,13]{3,1,0,2:T(8,128)S(1)} %copy-done.6), kind=kOutput, calls=%fused_computation | convolution fusion | flops 2076672 | bytes 96032 | tf_op jit(solution)/shard_map/paq,pqij->aij/dot_general | solution.py:441
  50.4 0.0 collective-permute-done.4
  50.4 3.5 %collective-permute-done.5 = f32[8,256]{1,0:T(8,128)S(1)} collective-permute-done((f32[8,256]{1,0:T(8,128)S(1)}, f32[8,256]{1,0:T(8,128)S(1)}, u32[]{:S(2)}, u32[]{:S(2)}) %collective-permute-start.5) | collective-permute-done | bytes 8224 | tf_op jit(solution)/shard_map/ppermute | solution.py:439
  53.9 0.6 %add_add_fusion = f32[8,256]{1,0:T(8,128)} fusion(f32[8,256]{1,0:T(8,128)S(1)} %collective-permute-done.5, f32[8,256]{1,0:T(8,128)S(1)} %get-tuple-element.14, f32[8,256]{1,0:T(8,128)S(1)} %collective-permute-done.4), kind=kLoop, calls=%fused_computation.13 | loop fusion | flops 4096 | bytes 32768 | tf_op jit(solution)/shard_map/add | solution.py:440
  (5 shorter events, 0.1 us)
Async XLA Ops:
  3.4 9.0 %collective-permute-start.1 = (f32[560,128]{1,0:T(8,128)}, f32[560,128]{1,0:T(8,128)S(1)}, u32[]{:S(2)}, u32[]{:S(2)}) collective-permute-start(f32[560,128]{1,0:T(8,128)} %get-tuple-element.11.pay), channel_id=1, source_target_pairs={{1,0},{2,1},{3,2},{4,3},{5,4},{6,5},{7,6},{8,7},{9,8},{10,9},{11,1... | collective-permute-start | bytes 860168 | tf_op jit(solution)/shard_map/ppermute | solution.py:351
  6.9 8.4 %collective-permute-start = (f32[560,128]{1,0:T(8,128)}, f32[560,128]{1,0:T(8,128)S(1)}, u32[]{:S(2)}, u32[]{:S(2)}) collective-permute-start(f32[560,128]{1,0:T(8,128)} %get-tuple-element.11.pay), channel_id=1, source_target_pairs={{0,1},{1,2},{2,3},{3,4},{4,5},{5,6},{6,7},{7,8},{8,9},{9,10},{10,1... | collective-permute-start | bytes 860168 | tf_op jit(solution)/shard_map/ppermute | solution.py:350
  6.9 2.3 %copy-start.7 = (f32[9,13,13]{2,1,0:T(8,128)S(1)}, f32[9,13,13]{2,1,0:T(8,128)}, u32[]{:S(2)}) copy-start(f32[9,13,13]{2,1,0:T(8,128)} %param.14) | copy-start | bytes 18256
  6.9 2.5 %copy-start.9 = (pred[13,13]{0,1:T(8,128)(4,1)S(1)}, pred[13,13]{0,1:T(8,128)(4,1)}, u32[]{:S(2)}) copy-start(pred[13,13]{0,1:T(8,128)(4,1)} %constant.19.clone) | copy-start | bytes 511
  6.9 2.5 %copy-start.10 = (pred[8,16]{0,1:T(8,128)(4,1)S(1)}, pred[8,16]{0,1:T(8,128)(4,1)}, u32[]{:S(2)}) copy-start(pred[8,16]{0,1:T(8,128)(4,1)} %constant.20.clone) | copy-start | bytes 388
  6.9 2.9 %copy-start.2 = (f32[560,128]{1,0:T(8,128)S(1)}, f32[560,128]{1,0:T(8,128)}, u32[]{:S(2)}) copy-start(f32[560,128]{1,0:T(8,128)} %get-tuple-element.11.pay) | copy-start | bytes 860164
  6.9 2.9 %copy-start.4 = (s32[24,128]{1,0:T(8,128)S(1)}, s32[24,128]{1,0:T(8,128)}, u32[]{:S(2)}) copy-start(s32[24,128]{1,0:T(8,128)} %get-tuple-element.10) | copy-start | bytes 36868
  9.2 6.1 %copy-start.1 = (f32[4096,128]{1,0:T(8,128)}, f32[4096,128]{1,0:T(8,128)S(1)}, u32[]{:S(2)}) copy-start(f32[4096,128]{1,0:T(8,128)S(1)} %grid_table.1.table) | copy-start | bytes 6291460
  14.7 6.6 %copy-start = (f32[16,8,4096]{2,1,0:T(8,128)S(1)}, f32[16,8,4096]{2,1,0:T(8,128)}, u32[]{:S(2)}) copy-start(f32[16,8,4096]{2,1,0:T(8,128)} %param.10) | copy-start | bytes 6291460
  14.7 6.6 %copy-start.5 = (f32[16]{0:T(128)S(1)}, f32[16]{0:T(128)}, u32[]{:S(2)}) copy-start(f32[16]{0:T(128)} %occ.1) | copy-start | bytes 196
  14.7 10.1 %collective-permute-start.3 = (f32[16,128]{1,0:T(8,128)S(1)}, f32[16,128]{1,0:T(8,128)S(1)}, u32[]{:S(2)}, u32[]{:S(2)}) collective-permute-start(f32[16,128]{1,0:T(8,128)S(1)} %next_points.1.after), channel_id=1, source_target_pairs={{0,1},{1,2},{2,3},{3,4},{4,5},{5,6},{6,7},{7,8},{8,9},{9,10},{10,1... | collective-permute-start | bytes 24584 | tf_op jit(solution)/shard_map/ppermute | solution.py:383
  17.2 19.5 %copy-start.11 = (s32[8]{0:T(128)S(1)}, s32[8]{0:T(128)}, u32[]{:S(2)}) copy-start(s32[8]{0:T(128)} %sizes_in.1) | copy-start | bytes 100
  17.2 19.5 %copy-start.8 = (f32[8,9,512]{2,0,1:T(8,128)S(1)}, f32[8,9,512]{2,0,1:T(8,128)}, u32[]{:S(2)}) copy-start(f32[8,9,512]{2,0,1:T(8,128)} %param.13) | copy-start | bytes 442372
  17.2 29.5 %copy-start.3 = (s32[8,512]{1,0:T(8,128)S(1)}, s32[8,512]{1,0:T(8,128)}, u32[]{:S(2)}) copy-start(s32[8,512]{1,0:T(8,128)} %offsets.1) | copy-start | bytes 49156
  17.2 31.5 %copy-start.6 = (f32[8,16,13,13]{3,1,0,2:T(8,128)S(1)}, f32[8,16,13,13]{3,1,0,2:T(8,128)}, u32[]{:S(2)}) copy-start(f32[8,16,13,13]{3,1,0,2:T(8,128)} %constant.21.clone) | copy-start | bytes 259588
  17.3 7.6 %collective-permute-start.2 = (f32[16,128]{1,0:T(8,128)S(1)}, f32[16,128]{1,0:T(8,128)S(1)}, u32[]{:S(2)}, u32[]{:S(2)}) collective-permute-start(f32[16,128]{1,0:T(8,128)S(1)} %previous_points.1.after), channel_id=1, source_target_pairs={{1,0},{2,1},{3,2},{4,3},{5,4},{6,5},{7,6},{8,7},{9,8},{10,9},{11,1... | collective-permute-start | bytes 24584 | tf_op jit(solution)/shard_map/ppermute | solution.py:382
  25.9 20.8 %all-to-all-start = ((f32[16,24,128]{2,1,0:T(8,128)}), f32[16,24,128]{2,1,0:T(8,128)S(1)}, u32[]{:S(2)}, u32[]{:S(2)}) async-start(f32[16,24,128]{2,1,0:T(8,128)} %partial_matrices.1), calls=%async_computation | async-start | bytes 393216 | tf_op jit(solution)/shard_map/all_to_all | solution.py:413
  47.8 2.6 %collective-permute-start.4 = (f32[8,256]{1,0:T(8,128)S(1)}, f32[8,256]{1,0:T(8,128)S(1)}, u32[]{:S(2)}, u32[]{:S(2)}) collective-permute-start(f32[8,256]{1,0:T(8,128)S(1)} %get-tuple-element.15), channel_id=1, source_target_pairs={{1,0},{2,1},{3,2},{4,3},{5,4},{6,5},{7,6},{8,7},{9,8},{10,9},{11,1... | collective-permute-start | bytes 24584 | tf_op jit(solution)/shard_map/ppermute | solution.py:438
  48.7 5.2 %collective-permute-start.5 = (f32[8,256]{1,0:T(8,128)S(1)}, f32[8,256]{1,0:T(8,128)S(1)}, u32[]{:S(2)}, u32[]{:S(2)}) collective-permute-start(f32[8,256]{1,0:T(8,128)S(1)} %get-tuple-element.16), channel_id=1, source_target_pairs={{0,1},{1,2},{2,3},{3,4},{4,5},{5,6},{6,7},{7,8},{8,9},{9,10},{10,1... | collective-permute-start | bytes 24584 | tf_op jit(solution)/shard_map/ppermute | solution.py:439
